TPU v7x, 256 devices: a whole 4x4x8 slice. The times are simulated.
256 devices in a mesh: tm: 32 (over z, y), chan: 8 (over x, core).
Axes of the slice: x: 4, y: 4, z: 8, core: 2. Of those that a mesh axis runs over, the one named last changes fastest.
Arguments:
- records: bfloat16 [512, 100, 16384], P('tm', None, 'chan'), may hold values from -6 to 6
- alive: int32 [16384], P('chan'), may hold values 0 or 1
- partner: int32 [128, 9], P('tm'), may hold values from 0 to 127, as said below
Outputs:
- stack: bfloat16 [128, 9, 16, 2, 128, 128], P('tm', None, 'chan')
Inputs may be any that keep to these rules, and one draw needn't show every extreme that they name: partner[a, k] = min(a + o, 127), where o runs over the offsets 0 to 8, each once in a row; partner[a, 0] = a.
All inputs are finite; a program needn't handle non-finite values. No bound on the sum of `alive` on one device may be relied on, other than what follows from the above.
Results may differ from a plain program's by a relative error of at most 0.0052.
Values may be sent and summed in bfloat16 or wider, within the bound.
No kernel may reach another device: no remote copies, remote signals or barrier semaphores. Data moves between devices by JAX's collectives and lax.ppermute only.
A program may use at most 128 MiB of HBM per device.

v0:
```python
import math

import jax
import jax.numpy as jnp
from jax import lax
from jax.sharding import PartitionSpec as P

NBIN = 16
BLOCK = 128
BAND = 8
BLK_DEV = 4


def passed_along(block, axis, distance):
    devices = range(lax.axis_size(axis))
    route = [(i - distance, i) for i in devices if i - distance in devices]
    return lax.ppermute(block, axis, route)


def dft_table(length, count):
    samples = jnp.arange(length, dtype=jnp.float32)
    freqs = jnp.arange(count, dtype=jnp.float32) + 4.0
    angle = 2.0 * jnp.pi * freqs[:, None] * samples[None, :] / length
    factor = jnp.sqrt(jnp.float32(2.0) / length)
    return jnp.stack([jnp.cos(angle) * factor, -jnp.sin(angle) * factor], axis=1)


def per_device(records, alive, partner):
    table = dft_table(records.shape[1], NBIN)
    signal = records.astype(jnp.float32)
    power = jnp.mean(signal * signal, axis=1, keepdims=True)
    normed = signal / jnp.sqrt(power + 1e-05) * alive.astype(jnp.float32)[None, None, :]
    spectra = jnp.einsum("fpt,wtc->wfpc", table, normed, precision=lax.Precision.HIGHEST).astype(
        jnp.bfloat16
    )
    local = lax.all_to_all(
        lax.all_to_all(spectra, "chan", split_axis=1, concat_axis=3, tiled=True),
        "tm",
        split_axis=3,
        concat_axis=0,
        tiled=True,
    )
    reach = (BLK_DEV - 1 + BAND) // BLK_DEV
    pieces = [local]
    for distance in range(1, reach + 1):
        pieces.append(passed_along(local, "tm", -distance))
    window = jnp.concatenate(pieces, axis=3)
    count = local.shape[0]
    grouped = window.reshape(count, local.shape[1], 2, (reach + 1) * BLK_DEV, BLOCK)
    anchor = lax.axis_index("tm") * BLK_DEV
    inverse = 1.0 / math.sqrt(count)
    results = []
    for column in range(BLK_DEV):
        own = local[:, :, :, column * BLOCK : (column + 1) * BLOCK]
        relative = partner[column] - anchor
        others = jnp.take(grouped, relative, axis=3)
        product = jnp.einsum("wfpi,wfqkj->kfpqij", own, others, preferred_element_type=jnp.float32)
        real_part = product[:, :, 0, 0] + product[:, :, 1, 1]
        imag_part = product[:, :, 0, 1] - product[:, :, 1, 0]
        results.append((jnp.stack([real_part, imag_part], axis=2) * inverse).astype(jnp.bfloat16))
    return jnp.stack(results, axis=0)


def solution(mesh):
    return jax.shard_map(
        per_device,
        mesh=mesh,
        in_specs=(P("tm", None, "chan"), P("chan"), P("tm", None)),
        out_specs=P("tm", None, "chan", None, None, None),
        check_vma=False,
    )
```

profile of v0, /device:TPU:32, one launch (start us, length us, event | category | flops | bytes accessed | tf_op | source)
XLA Modules:
  0.0 419.4 jit_solution(11039066880458251926)
XLA Ops:
  0.0 0.1 cosine_multiply_fusion
  0.1 0.0 copy-start.5
  0.1 4.2 fusion.2
  4.4 4.9 %fusion.4 = f32[16,100,2048,1]{2,0,1,3:T(8,128)S(1)} fusion(bf16[16,100,2048]{2,0,1:T(8,128)(2,1)} %param.5, f32[2048]{0:T(1024)S(1)} %convert_element_type.53, f32[16,2048]{1,0:T(8,128)S(1)} %add_sqrt_fusion), kind=kLoop, calls=%fused_computation.10 | loop fusion | flops 9830400 | bytes 19800064 | tf_op jit(solution)/shard_map/mul | solution.py:32
  9.3 18.6 %fusion.16 = bf16[16,16,2,2048]{3,1,2,0:T(8,128)(2,1)S(1)} fusion(f32[16,100,2048,1]{2,0,1,3:T(8,128)S(1)} %fusion.4, f32[16,1,100]{2,0,1:T(8,128)S(1)} %get-tuple-element.30, f32[16,1,100]{2,0,1:T(8,128)S(1)} %get-tuple-element.29), kind=kOutput, calls=%fused_computation.25 | convolution fusion | flops 1259342976 | bytes 15217152 | tf_op jit(solution)/shard_map/fpt,wtc->wfpc/dot_general | solution.py:33
  27.9 2.2 copy.44
  30.1 31.6 %all_to_all.36 = bf16[16,16,2,2048]{3,2,0,1:T(2,128)(2,1)S(1)} all-to-all(bf16[16,16,2,2048]{3,2,0,1:T(2,128)(2,1)S(1)} %copy.44), channel_id=1, replica_groups=mesh['tm'=32,'chan'=8] {'chan'}, dimensions={1} | all-to-all | bytes 4194304 | tf_op jit(solution)/shard_map/all_to_all | solution.py:37
  61.7 1.2 copy.125
  62.9 18.0 %copy.77 = bf16[16,2,2,8,2048]{0,2,1,4,3:T(2,128)(2,1)} copy(bf16[16,2,2,8,2048]{4,3,0,2,1:T(8,128)(2,1)S(1)} %bitcast.114) | data formatting | bytes 4194304 | tf_op jit(solution)/shard_map/all_to_all | solution.py:37
  80.8 19.7 %reshape.481 = bf16[32,2,16384]{2,1,0:T(2,128)(2,1)S(1)} reshape(bf16[16384,2,2,16]{3,2,1,0:T(2,128)(2,1)} %bitcast.107) | data formatting | bytes 4194304
  100.6 60.7 %all_to_all.37 = bf16[32,2,16384]{2,1,0:T(2,128)(2,1)} all-to-all(bf16[32,2,16384]{2,1,0:T(2,128)(2,1)S(1)} %reshape.481), channel_id=1, replica_groups=mesh['tm'=32,'chan'=8] {'tm'}, dimensions={0} | all-to-all | bytes 4194304 | tf_op jit(solution)/shard_map/all_to_all | solution.py:36
  161.3 16.5 %reshape.482 = bf16[16384,2,2,16]{3,2,1,0:T(2,128)(2,1)} reshape(bf16[32,2,16384]{2,1,0:T(2,128)(2,1)} %all_to_all.37) | data formatting | bytes 4194304
  177.7 33.4 %copy.79 = bf16[16,2,2,32,512]{4,0,3,2,1:T(8,128)(2,1)S(1)} copy(bf16[16,2,2,32,512]{0,2,1,4,3:T(2,128)(2,1)} %bitcast.108) | data formatting | bytes 4194304 | tf_op jit(solution)/shard_map/all_to_all | solution.py:36
  211.1 5.3 %collective-permute-start = (bf16[512,2,2,512]{3,0,2,1:T(8,128)(2,1)S(1)}, bf16[512,2,2,512]{3,0,2,1:T(8,128)(2,1)}, u32[]{:S(2)}, u32[]{:S(2)}) collective-permute-start(bf16[512,2,2,512]{3,0,2,1:T(8,128)(2,1)S(1)} %bitcast.109), channel_id=1, source_target_pairs={{8,0},{16,8},{24,16},{32,24},{40,32},{48,40},{56,48},{64,56},{72,6... | collective-permute-start | bytes 6291464 | tf_op jit(solution)/shard_map/ppermute | solution.py:17
  216.4 2.8 collective-permute-start.1
  219.3 2.0 concatenate.38
  221.3 1.4 slice_bitcast_fusion.4
  222.8 0.5 copy-done
  223.3 1.7 copy_dynamic-update-slice_fusion
  225.0 82.4 %collective-permute-done = bf16[512,2,2,512]{3,0,2,1:T(8,128)(2,1)} collective-permute-done((bf16[512,2,2,512]{3,0,2,1:T(8,128)(2,1)S(1)}, bf16[512,2,2,512]{3,0,2,1:T(8,128)(2,1)}, u32[]{:S(2)}, u32[]{:S(2)}) %collective-permute-start) | collective-permute-done | bytes 2097184 | tf_op jit(solution)/shard_map/ppermute | solution.py:17
  307.4 3.4 bitcast_dynamic-update-slice_fusion.1
  310.8 38.5 %collective-permute-done.1 = bf16[512,2,2,512]{3,0,2,1:T(8,128)(2,1)} collective-permute-done((bf16[512,2,2,512]{3,0,2,1:T(8,128)(2,1)S(1)}, bf16[512,2,2,512]{3,0,2,1:T(8,128)(2,1)}, u32[]{:S(2)}, u32[]{:S(2)}) %collective-permute-start.1) | collective-permute-done | bytes 2097184 | tf_op jit(solution)/shard_map/ppermute | solution.py:17
  349.4 3.4 bitcast_dynamic-update-slice_fusion
  352.8 6.5 %gather_fusion = bf16[9,512,2,2,128]{4,1,3,2,0:T(8,128)(2,1)} fusion(bf16[512,2,2,12,128]{4,0,3,2,1:T(8,128)(2,1)} %bitcast_dynamic-update-slice_fusion, s32[1024]{0:T(1024)S(1)} %pad_clamp_fusion.3), kind=kCustom, calls=%fused_computation.clone | custom fusion | bytes 9437220 | tf_op jit(solution)/shard_map/jit(_take)/gather | solution.py:56
  359.3 6.5 %gather_fusion.1 = bf16[9,512,2,2,128]{4,1,3,2,0:T(8,128)(2,1)} fusion(bf16[512,2,2,12,128]{4,0,3,2,1:T(8,128)(2,1)} %bitcast_dynamic-update-slice_fusion, s32[1024]{0:T(1024)S(1)} %pad_clamp_fusion.2), kind=kCustom, calls=%fused_computation.1.clone | custom fusion | bytes 9437220 | tf_op jit(solution)/shard_map/jit(_take)/gather | solution.py:56
  365.8 6.9 %select_bitcast_fusion.2 = (bf16[512,2,2,9,128,1]{4,0,2,1,3,5:T(8,128)(2,1)}, bf16[512,2,2,9,128,1]{4,0,2,1,3,5:T(8,128)(2,1)S(1)}) fusion(bf16[9,512,2,2,128]{4,1,3,2,0:T(8,128)(2,1)} %gather_fusion.1, pred[9]{0:T(512)(128)(4,1)S(1)} %get-tuple-element.23, bf16[9,512,2,2,128]{4,1,3,2,0:T(8,128)(2,1)} %gather_fusion, pred[9]{0:T(512)(128)(4,1)S(1)} %get-tuple-element.6), kind=kLoop, calls=%fused_computation.22 | loop fusion | flops 4718592 | bytes 18874386 | tf_op jit(solution)/shard_map/jit(_take)/select_n | solution.py:56
  372.7 2.0 fusion.23
  374.7 0.0 copy-start.2
  374.7 0.1 fusion.41
  374.8 0.1 fusion.43
  375.0 2.1 copy-done.2
  377.0 2.0 fusion.26
  379.0 1.3 fusion.40
  380.4 6.5 %gather_fusion.2 = bf16[9,512,2,2,128]{4,1,3,2,0:T(8,128)(2,1)} fusion(bf16[512,2,2,12,128]{4,0,3,2,1:T(8,128)(2,1)} %bitcast_dynamic-update-slice_fusion, s32[1024]{0:T(1024)S(1)} %pad_clamp_fusion.1), kind=kCustom, calls=%fused_computation.2.clone | custom fusion | bytes 9437220 | tf_op jit(solution)/shard_map/jit(_take)/gather | solution.py:56
  386.9 6.5 %gather_fusion.3 = bf16[9,512,2,2,128]{4,1,3,2,0:T(8,128)(2,1)} fusion(bf16[512,2,2,12,128]{4,0,3,2,1:T(8,128)(2,1)} %bitcast_dynamic-update-slice_fusion, s32[1024]{0:T(1024)S(1)} %pad_clamp_fusion), kind=kCustom, calls=%fused_computation.3.clone | custom fusion | bytes 9437220 | tf_op jit(solution)/shard_map/jit(_take)/gather | solution.py:56
  393.4 6.9 %select_bitcast_fusion = (bf16[512,2,2,9,128,1]{4,0,2,1,3,5:T(8,128)(2,1)S(1)}, bf16[512,2,2,9,128,1]{4,0,2,1,3,5:T(8,128)(2,1)}) fusion(bf16[9,512,2,2,128]{4,1,3,2,0:T(8,128)(2,1)} %gather_fusion.3, pred[9]{0:T(512)(128)(4,1)S(1)} %get-tuple-element.27, bf16[9,512,2,2,128]{4,1,3,2,0:T(8,128)(2,1)} %gather_fusion.2, pred[9]{0:T(512)(128)(4,1)S(1)} %get-tuple-element.25), kind=kLoop, calls=%fused_computation.20 | loop fusion | flops 4718592 | bytes 18874386 | tf_op jit(solution)/shard_map/jit(_take)/select_n | solution.py:56
  400.3 4.3 %fusion.29 = f32[9,2,2,2,128,128]{4,5,0,1,3,2:T(8,128)S(1)} fusion(bf16[512,2,2,9,128,1]{4,0,2,1,3,5:T(8,128)(2,1)} %get-tuple-element.32, bf16[512,2,2,128,1,1]{3,0,2,1,4,5:T(8,128)(2,1)S(1)} %copy-done.4), kind=kOutput, calls=%fused_computation.36 | convolution fusion | flops 1207959552 | bytes 9961472 | tf_op jit(solution)/shard_map/wfpi,wfqkj->kfpqij/dot_general | solution.py:57
  404.6 0.4 fusion.38
  405.0 0.6 copy-done.3
  405.6 2.0 fusion.32
  407.7 0.4 fusion.36
  408.0 0.3 fusion.19
  408.4 0.9 copy-done.1
  409.3 0.4 fusion.20
  409.7 0.3 fusion.21
  410.0 0.3 fusion.22
  410.3 2.5 pad_maximum_fusion
  412.8 6.6 %copy.62 = bf16[4,9,2,2,128,128]{5,4,3,2,1,0:T(8,128)(2,1)} copy(bf16[4,9,2,2,128,128]{4,5,1,2,3,0:T(8,128)(2,1)} %pad_maximum_fusion) | data formatting | bytes 9437184 | tf_op jit(solution)/shard_map/stack | solution.py:61
  (16 shorter events, 0.1 us)
Async XLA Ops:
  0.1 4.3 %copy-start.5 = (s32[2048]{0:T(1024)S(1)}, s32[2048]{0:T(1024)}, u32[]{:S(2)}) copy-start(s32[2048]{0:T(1024)} %param.6) | copy-start | bytes 24580
  177.7 41.5 %copy-start.6 = (s32[4,9]{1,0:T(4,128)S(1)}, s32[4,9]{1,0:T(4,128)}, u32[]{:S(2)}) copy-start(s32[4,9]{1,0:T(4,128)} %param.7) | copy-start | bytes 436
  211.1 96.3 %collective-permute-start = (bf16[512,2,2,512]{3,0,2,1:T(8,128)(2,1)S(1)}, bf16[512,2,2,512]{3,0,2,1:T(8,128)(2,1)}, u32[]{:S(2)}, u32[]{:S(2)}) collective-permute-start(bf16[512,2,2,512]{3,0,2,1:T(8,128)(2,1)S(1)} %bitcast.109), channel_id=1, source_target_pairs={{8,0},{16,8},{24,16},{32,24},{40,32},{48,40},{56,48},{64,56},{72,6... | collective-permute-start | bytes 6291464 | tf_op jit(solution)/shard_map/ppermute | solution.py:17
  216.4 132.9 %collective-permute-start.1 = (bf16[512,2,2,512]{3,0,2,1:T(8,128)(2,1)S(1)}, bf16[512,2,2,512]{3,0,2,1:T(8,128)(2,1)}, u32[]{:S(2)}, u32[]{:S(2)}) collective-permute-start(bf16[512,2,2,512]{3,0,2,1:T(8,128)(2,1)S(1)} %bitcast.110), channel_id=1, source_target_pairs={{16,0},{24,8},{32,16},{40,24},{48,32},{56,40},{64,48},{72,56},{80,... | collective-permute-start | bytes 6291464 | tf_op jit(solution)/shard_map/ppermute | solution.py:17
  221.3 2.0 copy-start
  374.7 2.3 copy-start.2
  393.4 6.9 %copy-start.4 = (bf16[512,2,2,128,1,1]{3,0,2,1,4,5:T(8,128)(2,1)S(1)}, bf16[512,2,2,128,1,1]{3,0,2,1,4,5:T(8,128)(2,1)}, u32[]{:S(2)}) copy-start(bf16[512,2,2,128,1,1]{3,0,2,1,4,5:T(8,128)(2,1)} %get-tuple-element.22) | copy-start | bytes 1572868
  404.6 1.0 copy-start.3
  408.0 1.3 copy-start.1
where the time goes:
time: 424 us; the launch traced here: 419 us
  local copies, waits for them, and re-layouts  140 us (33%)
  waiting for transfers between devices  121 us (29%)
  blocking collectives  92.3 us (22%)
  other arithmetic  29.2 us (7%)
  matrix products  29 us (7%)
  starting transfers between devices  8.09 us (2%)
    ppermute x2, waiting for transfers between devices, passed_along(): return lax.ppermute(block, axis, route)  121 us
    all_to_all x1, blocking collectives, per_device(): lax.all_to_all(lax.all_to_all(spectra, 'chan', split_axis=1, concat_axis=...  60.7 us
    unnamed x18, local copies, waits for them, and re-layouts  45.5 us
    all_to_all x1, local copies, waits for them, and re-layouts, per_device(): lax.all_to_all(lax.all_to_all(spectra, 'chan', split_axis=1, concat_axis=...  33.4 us
    all_to_all x1, blocking collectives, per_device(): lax.all_to_all(spectra, 'chan', split_axis=1, concat_axis=3, tiled=True)  31.6 us
    gather x4, local copies, waits for them, and re-layouts, per_device(): others = jnp.take(grouped, relative, axis=3)  26 us
    all_to_all x2, local copies, waits for them, and re-layouts, per_device(): lax.all_to_all(spectra, 'chan', split_axis=1, concat_axis=3, tiled=True)  19.1 us
    dot_general x1, matrix products, per_device(): jnp.einsum('fpt,wtc->wfpc', table, normed, precision=lax.Precision.HIGHEST)  18.6 us
  transfers between devices with their start and end apart: 2, of which 2 were waited for; matrix products, arithmetic and copies ran while one was open for 2% of the time, Pallas kernels for 0%

commit v1 on v0

v1 whole, which is shorter than its diff:
```python
import math

import jax
import jax.numpy as jnp
import numpy as np
from jax import lax
from jax.experimental import pallas as pl
from jax.experimental.pallas import tpu as pltpu
from jax.sharding import PartitionSpec as P

WINLEN = 100
NBIN = 16
BLOCK = 128
WIN_DEV = 16
WINDOWS = 512
PAIRS = 9
NZ, NY, NC = 8, 4, 8
NF = 2
GROUP = 4
REACH = 12
COLS = 256
BOTH = ("tm", "chan")


def dft_rows():
    t = np.arange(WINLEN)
    bins = np.arange(NBIN) + 4
    angle = 2.0 * np.pi * bins[:, None] * t[None, :] / WINLEN
    table = np.stack([np.cos(angle), -np.sin(angle)], axis=1) * math.sqrt(2.0 / WINLEN)
    high = table.astype(jnp.bfloat16)
    low = (table - high.astype(np.float64)).astype(jnp.bfloat16)
    parts = np.stack([high, low]).astype(np.float32).reshape(2, NC, NF, 2, WINLEN)
    parts = parts.transpose(1, 0, 2, 3, 4)
    rows = parts[:, :, :, :, None, :, None] * np.eye(WIN_DEV, dtype=np.float32)[:, None, :]
    return rows.reshape(NC, 2 * NF * 2 * WIN_DEV, WINLEN * WIN_DEV).astype(jnp.bfloat16)


def spectra_kernel(order, records, alive, *refs):
    rows, outs = refs[:NC], refs[NC:]
    x = records[...]
    signal = x.astype(jnp.float32)
    power = jnp.sum(signal * signal, axis=0) * (1.0 / WINLEN)
    scale = alive[...].astype(jnp.float32) / jnp.sqrt(power + 1e-05)
    x = x.reshape(WINLEN * WIN_DEV, COLS)
    lhs = jnp.concatenate([r[0] for r in rows], axis=0)
    y = jnp.dot(lhs, x, preferred_element_type=jnp.float32)
    half = NF * 2 * WIN_DEV
    for k in range(NC):
        at = 2 * half * k
        value = y[at : at + half] + y[at + half : at + 2 * half]
        for f in range(NF):
            for p in range(2):
                row = (f * 2 + p) * WIN_DEV
                scaled = (value[row : row + WIN_DEV] * scale).astype(jnp.bfloat16)
                for b in range(COLS // BLOCK):
                    outs[f * NC + k][b, p] = scaled[:, b * BLOCK : (b + 1) * BLOCK]


def spectra_slots(records, alive, order):
    channels = records.shape[2]
    blocks = channels // BLOCK
    rows = jnp.asarray(dft_rows())
    per = COLS // BLOCK
    grid_spec = pltpu.PrefetchScalarGridSpec(
        num_scalar_prefetch=1,
        grid=(channels // COLS,),
        in_specs=[
            pl.BlockSpec((WINLEN, WIN_DEV, COLS), lambda n, o: (0, 0, n)),
            pl.BlockSpec((1, COLS), lambda n, o: (0, n)),
        ]
        + [pl.BlockSpec((1,) + rows.shape[1:], lambda n, o, k=k: (o[k], 0, 0)) for k in range(NC)],
        out_specs=[pl.BlockSpec((per, 2, WIN_DEV, BLOCK), lambda n, o: (n, 0, 0, 0))] * (NF * NC),
    )
    return pl.pallas_call(
        spectra_kernel,
        grid_spec=grid_spec,
        out_shape=[jax.ShapeDtypeStruct((blocks, 2, WIN_DEV, BLOCK), jnp.bfloat16)] * (NF * NC),
        compiler_params=pltpu.CompilerParams(vmem_limit_bytes=40 << 20),
        name="spectra",
    )(order, records, alive, *([rows] * NC))


def pack_kernel(place, *refs):
    slots, halo, outs = refs[:NC], refs[NC], refs[NC + 1 :]
    y = place[0]
    for k in range(NY):
        target = lax.rem(y + k, NY)
        for i in range(3):
            group = target + i

            @pl.when(group < NY)
            def _():
                for s in range(NC):
                    outs[k][s, i] = slots[s][group]

            @pl.when(group >= NY)
            def _():
                for s in range(NC):
                    outs[k][s, i] = halo[s, group - NY]


def pack(place, slots, halo):
    vmem = pl.BlockSpec(memory_space=pltpu.VMEM)
    shape = jax.ShapeDtypeStruct((NC, 3, GROUP, 2, WIN_DEV, BLOCK), jnp.bfloat16)
    return pl.pallas_call(
        pack_kernel,
        in_specs=[pl.BlockSpec(memory_space=pltpu.SMEM)] + [vmem] * (NC + 1),
        out_specs=[vmem] * NY,
        out_shape=[shape] * NY,
        compiler_params=pltpu.CompilerParams(vmem_limit_bytes=16 << 20),
        name="pack",
    )(place, *slots, halo)


def block_of(refs, index):
    pieces = []
    for ref in refs:
        value = ref[:, index]
        halves = [value[:, p].reshape(NC * WIN_DEV, BLOCK) for p in range(2)]
        pieces.append(jnp.concatenate(halves, axis=1))
    return jnp.concatenate(pieces, axis=0)


def stack_kernel(relative, *refs):
    spectra, out, own_t = refs[:NY], refs[-2], refs[-1]
    a = pl.program_id(0)
    own_t[...] = block_of(spectra, a).T
    for k in range(PAIRS):
        other = block_of(spectra, relative[a, k])
        product = jnp.dot(own_t[...], other, preferred_element_type=jnp.float32)
        real = product[:BLOCK, :BLOCK] + product[BLOCK:, BLOCK:]
        imag = product[:BLOCK, BLOCK:] - product[BLOCK:, :BLOCK]
        inverse = 1.0 / math.sqrt(WINDOWS)
        out[0, k, 0, 0] = (real * inverse).astype(jnp.bfloat16)
        out[0, k, 0, 1] = (imag * inverse).astype(jnp.bfloat16)


def stacks(relative, spectra, f, earlier=None):
    shape = (GROUP, PAIRS, NF, 2, BLOCK, BLOCK)
    whole = pl.BlockSpec((NC, REACH, 2, WIN_DEV, BLOCK), lambda a, r: (0, 0, 0, 0, 0))
    args = [s.reshape(NC, REACH, 2, WIN_DEV, BLOCK) for s in spectra]
    specs = [whole] * NY
    aliases = {}
    if earlier is not None:
        args.append(earlier)
        specs.append(pl.BlockSpec(memory_space=pl.ANY))
        aliases = {1 + NY: 0}
    grid_spec = pltpu.PrefetchScalarGridSpec(
        num_scalar_prefetch=1,
        grid=(GROUP,),
        in_specs=specs,
        out_specs=pl.BlockSpec((1, PAIRS, 1, 2, BLOCK, BLOCK), lambda a, r: (a, 0, f, 0, 0, 0)),
        scratch_shapes=[pltpu.VMEM((2 * BLOCK, WINDOWS), jnp.bfloat16)],
    )
    return pl.pallas_call(
        stack_kernel,
        grid_spec=grid_spec,
        out_shape=jax.ShapeDtypeStruct(shape, jnp.bfloat16),
        input_output_aliases=aliases,
        compiler_params=pltpu.CompilerParams(vmem_limit_bytes=24 << 20),
        name="stacks",
    )(relative, *args)


def slot_route(k):
    route = []
    for z in range(NZ):
        for y in range(NY):
            for c in range(NC):
                route.append(((z * NY + y) * NC + c, (c * NY + y) * NC + (c + z + k) % NC))
    return route


def per_device(records, alive, partner):
    tm, chan = lax.axis_index("tm"), lax.axis_index("chan")
    z, y = tm // NY, tm % NY
    order = (chan + z + jnp.arange(NC, dtype=jnp.int32)) % NC
    sent = spectra_slots(jnp.transpose(records, (1, 0, 2)), alive.reshape(1, -1), order)
    place = y.reshape(1).astype(jnp.int32)
    relative = partner - tm * GROUP
    down = [(i, i - NY) for i in range(NY, NZ * NY)]
    result = None
    for f in range(NF):
        slots = [lax.ppermute(sent[f * NC + k], BOTH, slot_route(k)) for k in range(NC)]
        slots = [s.reshape(NY, GROUP, 2, WIN_DEV, BLOCK) for s in slots]
        halo = lax.ppermute(jnp.stack([slots[(k - 1) % NC][:2] for k in range(NC)]), "tm", down)
        packed = pack(place, slots, halo)
        spectra = [packed[0]]
        for k in range(1, NY):
            route = [(i, i // NY * NY + (i + k) % NY) for i in range(NZ * NY)]
            spectra.append(lax.ppermute(packed[k], "tm", route))
        result = stacks(relative, spectra, f, result)
    return result


def solution(mesh):
    return jax.shard_map(
        per_device,
        mesh=mesh,
        in_specs=(P("tm", None, "chan"), P("chan"), P("tm", None)),
        out_specs=P("tm", None, "chan", None, None, None),
        check_vma=False,
    )
```

time: 424 us -> 254 us (0.60)
  local copies, waits for them, and re-layouts: 140 us -> 6.73 us
  starting transfers between devices: 8.09 us -> 132 us
  blocking collectives: 92.3 us -> 0 us
  waiting for transfers between devices: 121 us -> 89.3 us
  other arithmetic: 29.2 us -> 0.01 us
  matrix products: 29 us -> 0 us
  Pallas kernels: 0 us -> 24.9 us
    ppermute x2 -> x24, starting transfers between devices: 8.09 us -> 132 us  [the longest x16 110 us: per_device(): lax.ppermute(sent[f * NC + k], BOTH, slot_route(k))]
    all_to_all x2 -> x0, blocking collectives: 92.3 us -> none  [the longest x1 60.7 us: per_device(): lax.all_to_all(lax.all_to_all(spectra, 'chan', split_axis=1, concat_axis=...]
    all_to_all x3 -> x0, local copies, waits for them, and re-layouts: 52.5 us -> none  [the longest x1 33.4 us: per_device(): lax.all_to_all(lax.all_to_all(spectra, 'chan', split_axis=1, concat_axis=...]
    unnamed x18 -> x26, local copies, waits for them, and re-layouts: 45.5 us -> 6.6 us
    ppermute x2 -> x24, waiting for transfers between devices: 121 us -> 89.3 us  [the longest x6 47.5 us: per_device(): spectra.append(lax.ppermute(packed[k], 'tm', route))]
    dot_general x5 -> x0, matrix products: 29 us -> none  [the longest x1 18.6 us: per_device(): jnp.einsum('fpt,wtc->wfpc', table, normed, precision=lax.Precision.HIGHEST)]
    gather x4 -> x0, local copies, waits for them, and re-layouts: 26 us -> none  [per_device(): others = jnp.take(grouped, relative, axis=3)]
    pallas_call x0 -> x5, Pallas kernels: none -> 24.9 us  [the longest x2 11.1 us: stacks(): pl.pallas_call(stack_kernel, grid_spec=grid_spec, out_shape=jax.ShapeDtyp...]
  transfers between devices with their start and end apart: 2 -> 24, of which waited for: 2 -> 10; matrix products, arithmetic and copies ran while one was open for 2% -> 0% of each run, Pallas kernels for 0% -> 3%
where the time goes in v1:
time: 254 us; the launch traced here: 253 us
  starting transfers between devices  132 us (52%)
  waiting for transfers between devices  89.3 us (35%)
  Pallas kernels  24.9 us (10%)
  local copies, waits for them, and re-layouts  6.73 us (3%)
    ppermute x16, starting transfers between devices, per_device(): lax.ppermute(sent[f * NC + k], BOTH, slot_route(k))  110 us
    ppermute x6, waiting for transfers between devices, per_device(): spectra.append(lax.ppermute(packed[k], 'tm', route))  47.5 us
    ppermute x16, waiting for transfers between devices, per_device(): lax.ppermute(sent[f * NC + k], BOTH, slot_route(k))  28.6 us
    ppermute x2, waiting for transfers between devices, per_device(): lax.ppermute(jnp.stack([slots[(k - 1) % NC][:2] for k in range(NC)]), 'tm...  13.1 us
    ppermute x6, starting transfers between devices, per_device(): spectra.append(lax.ppermute(packed[k], 'tm', route))  11.7 us
    pallas_call x2, Pallas kernels, stacks(): pl.pallas_call(stack_kernel, grid_spec=grid_spec, out_shape=jax.ShapeDtyp...  11.1 us
    pallas_call x1, Pallas kernels, spectra_slots(): pl.pallas_call(spectra_kernel, grid_spec=grid_spec, out_shape=[jax.ShapeD...  10.6 us
    ppermute x2, starting transfers between devices, per_device(): lax.ppermute(jnp.stack([slots[(k - 1) % NC][:2] for k in range(NC)]), 'tm...  10.2 us
  transfers between devices with their start and end apart: 24, of which 10 were waited for; matrix products, arithmetic and copies ran while one was open for 0% of the time, Pallas kernels for 3%

profile of v1, /device:TPU:32, one launch (start us, length us, event | category | flops | bytes accessed | tf_op | source)
XLA Modules:
  0.0 253.4 jit_solution(17063584613116690375)
XLA Ops:
  0.0 0.0 copy-start
  0.0 2.0 copy-done
  2.0 2.9 %copy-done.1 = bf16[16,100,2048]{2,0,1:T(8,128)(2,1)S(1)} copy-done((bf16[16,100,2048]{2,0,1:T(8,128)(2,1)S(1)}, bf16[16,100,2048]{2,0,1:T(8,128)(2,1)}, u32[]{:S(2)}) %copy-start.1) | copy-done | bytes 6553624
  4.8 0.7 copy-done.4
  5.5 10.6 %spectra.1 = (bf16[16,2,16,128]{3,2,1,0:T(8,128)(2,1)S(1)}, bf16[16,2,16,128]{3,2,1,0:T(8,128)(2,1)S(1)}, bf16[16,2,16,128]{3,2,1,0:T(8,128)(2,1)S(1)}, bf16[16,...) custom-call(s32[8]{0:T(128)S(1)} %and_select_fusion.order, ...), custom_call_target="tpu_custom_call" | custom-call | tf_op jit(solution)/shard_map/spectra/pallas_call | solution.py:74
  16.1 0.0 copy-start.5
  16.2 3.8 %collective-permute-start.19 = (bf16[16,2,16,128]{3,2,1,0:T(8,128)(2,1)S(1)}, bf16[16,2,16,128]{3,2,1,0:T(8,128)(2,1)S(1)}, u32[]{:S(2)}, u32[]{:S(2)}) collective-permute-start(bf16[16,2,16,128]{3,2,1,0:T(8,128)(2,1)S(1)} %get-tuple-element.48), channel_id=1, source_target_pairs={{0,7},{1,32},{2,65},{3,98},{4,131},{5,164},{6,197},{7,230},{8,15},... | collective-permute-start | bytes 393224 | tf_op jit(solution)/shard_map/ppermute | solution.py:184
  19.9 1.9 collective-permute-start.12
  21.9 1.9 collective-permute-start
  23.8 9.8 %collective-permute-start.1 = (bf16[16,2,16,128]{3,2,1,0:T(8,128)(2,1)S(1)}, bf16[16,2,16,128]{3,2,1,0:T(8,128)(2,1)S(1)}, u32[]{:S(2)}, u32[]{:S(2)}) collective-permute-start(bf16[16,2,16,128]{3,2,1,0:T(8,128)(2,1)S(1)} %get-tuple-element.30), channel_id=1, source_target_pairs={{0,1},{1,34},{2,67},{3,100},{4,133},{5,166},{6,199},{7,224},{8,9},... | collective-permute-start | bytes 393224 | tf_op jit(solution)/shard_map/ppermute | solution.py:184
  33.5 5.3 %collective-permute-start.2 = (bf16[16,2,16,128]{3,2,1,0:T(8,128)(2,1)S(1)}, bf16[16,2,16,128]{3,2,1,0:T(8,128)(2,1)S(1)}, u32[]{:S(2)}, u32[]{:S(2)}) collective-permute-start(bf16[16,2,16,128]{3,2,1,0:T(8,128)(2,1)S(1)} %get-tuple-element.31), channel_id=1, source_target_pairs={{0,2},{1,35},{2,68},{3,101},{4,134},{5,167},{6,192},{7,225},{8,10}... | collective-permute-start | bytes 393224 | tf_op jit(solution)/shard_map/ppermute | solution.py:184
  38.9 3.8 %collective-permute-start.13 = (bf16[16,2,16,128]{3,2,1,0:T(8,128)(2,1)S(1)}, bf16[16,2,16,128]{3,2,1,0:T(8,128)(2,1)S(1)}, u32[]{:S(2)}, u32[]{:S(2)}) collective-permute-start(bf16[16,2,16,128]{3,2,1,0:T(8,128)(2,1)S(1)} %get-tuple-element.42), channel_id=1, source_target_pairs={{0,1},{1,34},{2,67},{3,100},{4,133},{5,166},{6,199},{7,224},{8,9},... | collective-permute-start | bytes 393224 | tf_op jit(solution)/shard_map/ppermute | solution.py:184
  42.7 18.3 %collective-permute-done.12 = bf16[16,2,16,128]{3,2,1,0:T(8,128)(2,1)S(1)} collective-permute-done((bf16[16,2,16,128]{3,2,1,0:T(8,128)(2,1)S(1)}, bf16[16,2,16,128]{3,2,1,0:T(8,128)(2,1)S(1)}, u32[]{:S(2)}, u32[]{:S(2)}) %collective-permute-start.12) | collective-permute-done | bytes 131104 | tf_op jit(solution)/shard_map/ppermute | solution.py:184
  61.1 6.8 %collective-permute-start.14 = (bf16[16,2,16,128]{3,2,1,0:T(8,128)(2,1)S(1)}, bf16[16,2,16,128]{3,2,1,0:T(8,128)(2,1)S(1)}, u32[]{:S(2)}, u32[]{:S(2)}) collective-permute-start(bf16[16,2,16,128]{3,2,1,0:T(8,128)(2,1)S(1)} %get-tuple-element.43), channel_id=1, source_target_pairs={{0,2},{1,35},{2,68},{3,101},{4,134},{5,167},{6,192},{7,225},{8,10}... | collective-permute-start | bytes 393224 | tf_op jit(solution)/shard_map/ppermute | solution.py:184
  68.0 0.0 collective-permute-done.13
  68.0 6.8 %collective-permute-start.15 = (bf16[16,2,16,128]{3,2,1,0:T(8,128)(2,1)S(1)}, bf16[16,2,16,128]{3,2,1,0:T(8,128)(2,1)S(1)}, u32[]{:S(2)}, u32[]{:S(2)}) collective-permute-start(bf16[16,2,16,128]{3,2,1,0:T(8,128)(2,1)S(1)} %get-tuple-element.44), channel_id=1, source_target_pairs={{0,3},{1,36},{2,69},{3,102},{4,135},{5,160},{6,193},{7,226},{8,11}... | collective-permute-start | bytes 393224 | tf_op jit(solution)/shard_map/ppermute | solution.py:184
  74.9 0.0 collective-permute-done.14
  74.9 4.8 %collective-permute-start.16 = (bf16[16,2,16,128]{3,2,1,0:T(8,128)(2,1)S(1)}, bf16[16,2,16,128]{3,2,1,0:T(8,128)(2,1)S(1)}, u32[]{:S(2)}, u32[]{:S(2)}) collective-permute-start(bf16[16,2,16,128]{3,2,1,0:T(8,128)(2,1)S(1)} %get-tuple-element.45), channel_id=1, source_target_pairs={{0,4},{1,37},{2,70},{3,103},{4,128},{5,161},{6,194},{7,227},{8,12}... | collective-permute-start | bytes 393224 | tf_op jit(solution)/shard_map/ppermute | solution.py:184
  79.7 0.0 collective-permute-done.15
  79.7 22.2 %collective-permute-start.17 = (bf16[16,2,16,128]{3,2,1,0:T(8,128)(2,1)S(1)}, bf16[16,2,16,128]{3,2,1,0:T(8,128)(2,1)S(1)}, u32[]{:S(2)}, u32[]{:S(2)}) collective-permute-start(bf16[16,2,16,128]{3,2,1,0:T(8,128)(2,1)S(1)} %get-tuple-element.46), channel_id=1, source_target_pairs={{0,5},{1,38},{2,71},{3,96},{4,129},{5,162},{6,195},{7,228},{8,13},... | collective-permute-start | bytes 393224 | tf_op jit(solution)/shard_map/ppermute | solution.py:184
  102.0 12.5 %collective-permute-start.18 = (bf16[16,2,16,128]{3,2,1,0:T(8,128)(2,1)S(1)}, bf16[16,2,16,128]{3,2,1,0:T(8,128)(2,1)S(1)}, u32[]{:S(2)}, u32[]{:S(2)}) collective-permute-start(bf16[16,2,16,128]{3,2,1,0:T(8,128)(2,1)S(1)} %get-tuple-element.47), channel_id=1, source_target_pairs={{0,6},{1,39},{2,64},{3,97},{4,130},{5,163},{6,196},{7,229},{8,14},... | collective-permute-start | bytes 393224 | tf_op jit(solution)/shard_map/ppermute | solution.py:184
  114.6 3.5 %collective-permute-start.7 = (bf16[16,2,16,128]{3,2,1,0:T(8,128)(2,1)S(1)}, bf16[16,2,16,128]{3,2,1,0:T(8,128)(2,1)S(1)}, u32[]{:S(2)}, u32[]{:S(2)}) collective-permute-start(bf16[16,2,16,128]{3,2,1,0:T(8,128)(2,1)S(1)} %get-tuple-element.36), channel_id=1, source_target_pairs={{0,7},{1,32},{2,65},{3,98},{4,131},{5,164},{6,197},{7,230},{8,15},... | collective-permute-start | bytes 393224 | tf_op jit(solution)/shard_map/ppermute | solution.py:184
  118.1 7.5 %collective-permute-start.3 = (bf16[16,2,16,128]{3,2,1,0:T(8,128)(2,1)S(1)}, bf16[16,2,16,128]{3,2,1,0:T(8,128)(2,1)S(1)}, u32[]{:S(2)}, u32[]{:S(2)}) collective-permute-start(bf16[16,2,16,128]{3,2,1,0:T(8,128)(2,1)S(1)} %get-tuple-element.32), channel_id=1, source_target_pairs={{0,3},{1,36},{2,69},{3,102},{4,135},{5,160},{6,193},{7,226},{8,11}... | collective-permute-start | bytes 393224 | tf_op jit(solution)/shard_map/ppermute | solution.py:184
  125.7 3.8 %collective-permute-start.20 = (bf16[8,2,4,2,16,128]{5,4,3,2,1,0:T(8,128)(2,1)S(1)}, bf16[8,2,4,2,16,128]{5,4,3,2,1,0:T(8,128)(2,1)S(1)}, u32[]{:S(2)}, u32[]{:S(2)}) collective-permute-start(bf16[8,2,4,2,16,128]{5,4,3,2,1,0:T(8,128)(2,1)S(1)} %constant_dynamic-update-slice_fusion.8), channel_id=1, source_target_pairs={{32,0},{40,8},{48,16},{56,24},{64,32},{72,40},{80,48},{88,56},{96,... | collective-permute-start | bytes 1572872 | tf_op jit(solution)/shard_map/ppermute | solution.py:186
  129.6 6.5 %collective-permute-start.4 = (bf16[16,2,16,128]{3,2,1,0:T(8,128)(2,1)S(1)}, bf16[16,2,16,128]{3,2,1,0:T(8,128)(2,1)S(1)}, u32[]{:S(2)}, u32[]{:S(2)}) collective-permute-start(bf16[16,2,16,128]{3,2,1,0:T(8,128)(2,1)S(1)} %get-tuple-element.33), channel_id=1, source_target_pairs={{0,4},{1,37},{2,70},{3,103},{4,128},{5,161},{6,194},{7,227},{8,12}... | collective-permute-start | bytes 393224 | tf_op jit(solution)/shard_map/ppermute | solution.py:184
  136.1 10.9 %collective-permute-start.5 = (bf16[16,2,16,128]{3,2,1,0:T(8,128)(2,1)S(1)}, bf16[16,2,16,128]{3,2,1,0:T(8,128)(2,1)S(1)}, u32[]{:S(2)}, u32[]{:S(2)}) collective-permute-start(bf16[16,2,16,128]{3,2,1,0:T(8,128)(2,1)S(1)} %get-tuple-element.34), channel_id=1, source_target_pairs={{0,5},{1,38},{2,71},{3,96},{4,129},{5,162},{6,195},{7,228},{8,13},... | collective-permute-start | bytes 393224 | tf_op jit(solution)/shard_map/ppermute | solution.py:184
  147.1 1.9 collective-permute-start.6
  149.1 8.1 %collective-permute-done.4 = bf16[16,2,16,128]{3,2,1,0:T(8,128)(2,1)S(1)} collective-permute-done((bf16[16,2,16,128]{3,2,1,0:T(8,128)(2,1)S(1)}, bf16[16,2,16,128]{3,2,1,0:T(8,128)(2,1)S(1)}, u32[]{:S(2)}, u32[]{:S(2)}) %collective-permute-start.4) | collective-permute-done | bytes 131104 | tf_op jit(solution)/shard_map/ppermute | solution.py:184
  157.2 7.4 %collective-permute-done.20.refs_8_ = bf16[8,2,4,2,16,128]{5,4,3,2,1,0:T(8,128)(2,1)S(1)} collective-permute-done((bf16[8,2,4,2,16,128]{5,4,3,2,1,0:T(8,128)(2,1)S(1)}, bf16[8,2,4,2,16,128]{5,4,3,2,1,0:T(8,128)(2,1)S(1)}, u32[]{:S(2)}, u32[]{:S(2)}) %collective-permute-start.20) | collective-permute-done | bytes 524320 | tf_op jit(solution)/shard_map/ppermute | solution.py:186
  164.7 1.4 pack.3
  166.1 1.6 collective-permute-start.21
  167.7 2.1 collective-permute-done.5
  169.9 6.4 %collective-permute-start.8 = (bf16[8,2,4,2,16,128]{5,4,3,2,1,0:T(8,128)(2,1)S(1)}, bf16[8,2,4,2,16,128]{5,4,3,2,1,0:T(8,128)(2,1)S(1)}, u32[]{:S(2)}, u32[]{:S(2)}) collective-permute-start(bf16[8,2,4,2,16,128]{5,4,3,2,1,0:T(8,128)(2,1)S(1)} %constant_dynamic-update-slice_fusion), channel_id=1, source_target_pairs={{32,0},{40,8},{48,16},{56,24},{64,32},{72,40},{80,48},{88,56},{96,... | collective-permute-start | bytes 1572872 | tf_op jit(solution)/shard_map/ppermute | solution.py:186
  176.3 3.3 %collective-permute-start.22 = (bf16[8,3,4,2,16,128]{5,4,3,2,1,0:T(8,128)(2,1)}, bf16[8,3,4,2,16,128]{5,4,3,2,1,0:T(8,128)(2,1)S(1)}, u32[]{:S(2)}, u32[]{:S(2)}) collective-permute-start(bf16[8,3,4,2,16,128]{5,4,3,2,1,0:T(8,128)(2,1)} %get-tuple-element.51), channel_id=1, source_target_pairs={{0,16},{8,24},{16,0},{24,8},{32,48},{40,56},{48,32},{56,40},{64,80... | collective-permute-start | bytes 2359304 | tf_op jit(solution)/shard_map/ppermute | solution.py:191
  179.6 1.1 collective-permute-start.23
  180.6 5.7 %collective-permute-done.8.refs_8_ = bf16[8,2,4,2,16,128]{5,4,3,2,1,0:T(8,128)(2,1)S(1)} collective-permute-done((bf16[8,2,4,2,16,128]{5,4,3,2,1,0:T(8,128)(2,1)S(1)}, bf16[8,2,4,2,16,128]{5,4,3,2,1,0:T(8,128)(2,1)S(1)}, u32[]{:S(2)}, u32[]{:S(2)}) %collective-permute-start.8) | collective-permute-done | bytes 524320 | tf_op jit(solution)/shard_map/ppermute | solution.py:186
  186.3 1.7 pack.2
  188.1 0.9 copy-done.2
  188.9 1.6 collective-permute-start.9
  190.5 2.9 %collective-permute-start.10 = (bf16[8,3,4,2,16,128]{5,4,3,2,1,0:T(8,128)(2,1)}, bf16[8,3,4,2,16,128]{5,4,3,2,1,0:T(8,128)(2,1)}, u32[]{:S(2)}, u32[]{:S(2)}) collective-permute-start(bf16[8,3,4,2,16,128]{5,4,3,2,1,0:T(8,128)(2,1)} %get-tuple-element.39), channel_id=1, source_target_pairs={{0,16},{8,24},{16,0},{24,8},{32,48},{40,56},{48,32},{56,40},{64,80... | collective-permute-start | bytes 2359304 | tf_op jit(solution)/shard_map/ppermute | solution.py:191
  193.4 1.4 collective-permute-start.11
  194.8 11.1 %collective-permute-done.22 = bf16[8,3,4,2,16,128]{5,4,3,2,1,0:T(8,128)(2,1)S(1)} collective-permute-done((bf16[8,3,4,2,16,128]{5,4,3,2,1,0:T(8,128)(2,1)}, bf16[8,3,4,2,16,128]{5,4,3,2,1,0:T(8,128)(2,1)S(1)}, u32[]{:S(2)}, u32[]{:S(2)}) %collective-permute-start.22) | collective-permute-done | bytes 786464 | tf_op jit(solution)/shard_map/ppermute | solution.py:191
  205.9 9.9 %collective-permute-done.23 = bf16[8,3,4,2,16,128]{5,4,3,2,1,0:T(8,128)(2,1)S(1)} collective-permute-done((bf16[8,3,4,2,16,128]{5,4,3,2,1,0:T(8,128)(2,1)}, bf16[8,3,4,2,16,128]{5,4,3,2,1,0:T(8,128)(2,1)S(1)}, u32[]{:S(2)}, u32[]{:S(2)}) %collective-permute-start.23) | collective-permute-done | bytes 786464 | tf_op jit(solution)/shard_map/ppermute | solution.py:191
  215.8 4.8 %stacks.2.refs_4_ = bf16[4,9,2,2,128,128]{5,4,3,2,1,0:T(8,128)(2,1)} custom-call(s32[4,9]{1,0:T(4,128)S(1)} %broadcast_subtract_fusion.relative, bf16[8,12,2,16,128]{4,3,2,1,0:T(8,128)(2,1)S(1)} %bitcast.44, bf16[8,12,2,16,128]{4,3,2,1,0:T(8,128)(2,1)S(1)} %bitcast.45, bf16[8,12,2,16,128]{4,3,2,1,0:T(8,128)(2,1)S(1)} %bitcast.46, ...), custom_call_target="tpu_custom_call" | custom-call | tf_op jit(solution)/shard_map/stacks/pallas_call | solution.py:155
  220.5 2.2 collective-permute-done.9
  222.7 15.6 %collective-permute-done.10 = bf16[8,3,4,2,16,128]{5,4,3,2,1,0:T(8,128)(2,1)} collective-permute-done((bf16[8,3,4,2,16,128]{5,4,3,2,1,0:T(8,128)(2,1)}, bf16[8,3,4,2,16,128]{5,4,3,2,1,0:T(8,128)(2,1)}, u32[]{:S(2)}, u32[]{:S(2)}) %collective-permute-start.10) | collective-permute-done | bytes 786464 | tf_op jit(solution)/shard_map/ppermute | solution.py:191
  238.3 8.7 %collective-permute-done.11 = bf16[8,3,4,2,16,128]{5,4,3,2,1,0:T(8,128)(2,1)} collective-permute-done((bf16[8,3,4,2,16,128]{5,4,3,2,1,0:T(8,128)(2,1)}, bf16[8,3,4,2,16,128]{5,4,3,2,1,0:T(8,128)(2,1)}, u32[]{:S(2)}, u32[]{:S(2)}) %collective-permute-start.11) | collective-permute-done | bytes 786464 | tf_op jit(solution)/shard_map/ppermute | solution.py:191
  247.0 6.4 %stacks.3 = bf16[4,9,2,2,128,128]{5,4,3,2,1,0:T(8,128)(2,1)} custom-call(s32[4,9]{1,0:T(4,128)S(1)} %broadcast_subtract_fusion.relative, bf16[8,12,2,16,128]{4,3,2,1,0:T(8,128)(2,1)S(1)} %bitcast.48, bf16[8,12,2,16,128]{4,3,2,1,0:T(8,128)(2,1)} %bitcast.20.refs_1_, bf16[8,12,2,16,128]{4,3,2,1,0:T(8,128)(2,1)} %bitcast.21.refs_2_, ...), custom_call_target="tpu_custom_call", output_to_operand_aliasing={{}: (5, {})} | custom-call | tf_op jit(solution)/shard_map/stacks/pallas_call | solution.py:155
  (51 shorter events, 0.4 us)
Async XLA Ops:
  0.0 2.0 copy-start
  2.0 2.9 %copy-start.1 = (bf16[16,100,2048]{2,0,1:T(8,128)(2,1)S(1)}, bf16[16,100,2048]{2,0,1:T(8,128)(2,1)}, u32[]{:S(2)}) copy-start(bf16[16,100,2048]{2,0,1:T(8,128)(2,1)} %param.4) | copy-start | bytes 19660804
  4.8 0.7 copy-start.4
  16.1 178.6 %copy-start.5 = (s32[4,9]{1,0:T(4,128)S(1)}, s32[4,9]{1,0:T(4,128)}, u32[]{:S(2)}) copy-start(s32[4,9]{1,0:T(4,128)} %param.6) | copy-start | bytes 436
  16.2 22.7 %collective-permute-start.19 = (bf16[16,2,16,128]{3,2,1,0:T(8,128)(2,1)S(1)}, bf16[16,2,16,128]{3,2,1,0:T(8,128)(2,1)S(1)}, u32[]{:S(2)}, u32[]{:S(2)}) collective-permute-start(bf16[16,2,16,128]{3,2,1,0:T(8,128)(2,1)S(1)} %get-tuple-element.48), channel_id=1, source_target_pairs={{0,7},{1,32},{2,65},{3,98},{4,131},{5,164},{6,197},{7,230},{8,15},... | collective-permute-start | bytes 393224 | tf_op jit(solution)/shard_map/ppermute | solution.py:184
  19.9 41.2 %collective-permute-start.12 = (bf16[16,2,16,128]{3,2,1,0:T(8,128)(2,1)S(1)}, bf16[16,2,16,128]{3,2,1,0:T(8,128)(2,1)S(1)}, u32[]{:S(2)}, u32[]{:S(2)}) collective-permute-start(bf16[16,2,16,128]{3,2,1,0:T(8,128)(2,1)S(1)} %get-tuple-element.41), channel_id=1, source_target_pairs={{0,0},{1,33},{2,66},{3,99},{4,132},{5,165},{6,198},{7,231},{8,8},{... | collective-permute-start | bytes 393224 | tf_op jit(solution)/shard_map/ppermute | solution.py:184
  21.9 107.7 %collective-permute-start = (bf16[16,2,16,128]{3,2,1,0:T(8,128)(2,1)S(1)}, bf16[16,2,16,128]{3,2,1,0:T(8,128)(2,1)S(1)}, u32[]{:S(2)}, u32[]{:S(2)}) collective-permute-start(bf16[16,2,16,128]{3,2,1,0:T(8,128)(2,1)S(1)} %get-tuple-element.29), channel_id=1, source_target_pairs={{0,0},{1,33},{2,66},{3,99},{4,132},{5,165},{6,198},{7,231},{8,8},{... | collective-permute-start | bytes 393224 | tf_op jit(solution)/shard_map/ppermute | solution.py:184
  23.8 112.4 %collective-permute-start.1 = (bf16[16,2,16,128]{3,2,1,0:T(8,128)(2,1)S(1)}, bf16[16,2,16,128]{3,2,1,0:T(8,128)(2,1)S(1)}, u32[]{:S(2)}, u32[]{:S(2)}) collective-permute-start(bf16[16,2,16,128]{3,2,1,0:T(8,128)(2,1)S(1)} %get-tuple-element.30), channel_id=1, source_target_pairs={{0,1},{1,34},{2,67},{3,100},{4,133},{5,166},{6,199},{7,224},{8,9},... | collective-permute-start | bytes 393224 | tf_op jit(solution)/shard_map/ppermute | solution.py:184
  33.5 113.5 %collective-permute-start.2 = (bf16[16,2,16,128]{3,2,1,0:T(8,128)(2,1)S(1)}, bf16[16,2,16,128]{3,2,1,0:T(8,128)(2,1)S(1)}, u32[]{:S(2)}, u32[]{:S(2)}) collective-permute-start(bf16[16,2,16,128]{3,2,1,0:T(8,128)(2,1)S(1)} %get-tuple-element.31), channel_id=1, source_target_pairs={{0,2},{1,35},{2,68},{3,101},{4,134},{5,167},{6,192},{7,225},{8,10}... | collective-permute-start | bytes 393224 | tf_op jit(solution)/shard_map/ppermute | solution.py:184
  38.9 29.1 %collective-permute-start.13 = (bf16[16,2,16,128]{3,2,1,0:T(8,128)(2,1)S(1)}, bf16[16,2,16,128]{3,2,1,0:T(8,128)(2,1)S(1)}, u32[]{:S(2)}, u32[]{:S(2)}) collective-permute-start(bf16[16,2,16,128]{3,2,1,0:T(8,128)(2,1)S(1)} %get-tuple-element.42), channel_id=1, source_target_pairs={{0,1},{1,34},{2,67},{3,100},{4,133},{5,166},{6,199},{7,224},{8,9},... | collective-permute-start | bytes 393224 | tf_op jit(solution)/shard_map/ppermute | solution.py:184
  61.1 13.8 %collective-permute-start.14 = (bf16[16,2,16,128]{3,2,1,0:T(8,128)(2,1)S(1)}, bf16[16,2,16,128]{3,2,1,0:T(8,128)(2,1)S(1)}, u32[]{:S(2)}, u32[]{:S(2)}) collective-permute-start(bf16[16,2,16,128]{3,2,1,0:T(8,128)(2,1)S(1)} %get-tuple-element.43), channel_id=1, source_target_pairs={{0,2},{1,35},{2,68},{3,101},{4,134},{5,167},{6,192},{7,225},{8,10}... | collective-permute-start | bytes 393224 | tf_op jit(solution)/shard_map/ppermute | solution.py:184
  68.0 11.7 %collective-permute-start.15 = (bf16[16,2,16,128]{3,2,1,0:T(8,128)(2,1)S(1)}, bf16[16,2,16,128]{3,2,1,0:T(8,128)(2,1)S(1)}, u32[]{:S(2)}, u32[]{:S(2)}) collective-permute-start(bf16[16,2,16,128]{3,2,1,0:T(8,128)(2,1)S(1)} %get-tuple-element.44), channel_id=1, source_target_pairs={{0,3},{1,36},{2,69},{3,102},{4,135},{5,160},{6,193},{7,226},{8,11}... | collective-permute-start | bytes 393224 | tf_op jit(solution)/shard_map/ppermute | solution.py:184
  74.9 27.1 %collective-permute-start.16 = (bf16[16,2,16,128]{3,2,1,0:T(8,128)(2,1)S(1)}, bf16[16,2,16,128]{3,2,1,0:T(8,128)(2,1)S(1)}, u32[]{:S(2)}, u32[]{:S(2)}) collective-permute-start(bf16[16,2,16,128]{3,2,1,0:T(8,128)(2,1)S(1)} %get-tuple-element.45), channel_id=1, source_target_pairs={{0,4},{1,37},{2,70},{3,103},{4,128},{5,161},{6,194},{7,227},{8,12}... | collective-permute-start | bytes 393224 | tf_op jit(solution)/shard_map/ppermute | solution.py:184
  79.7 34.9 %collective-permute-start.17 = (bf16[16,2,16,128]{3,2,1,0:T(8,128)(2,1)S(1)}, bf16[16,2,16,128]{3,2,1,0:T(8,128)(2,1)S(1)}, u32[]{:S(2)}, u32[]{:S(2)}) collective-permute-start(bf16[16,2,16,128]{3,2,1,0:T(8,128)(2,1)S(1)} %get-tuple-element.46), channel_id=1, source_target_pairs={{0,5},{1,38},{2,71},{3,96},{4,129},{5,162},{6,195},{7,228},{8,13},... | collective-permute-start | bytes 393224 | tf_op jit(solution)/shard_map/ppermute | solution.py:184
  102.0 16.2 %collective-permute-start.18 = (bf16[16,2,16,128]{3,2,1,0:T(8,128)(2,1)S(1)}, bf16[16,2,16,128]{3,2,1,0:T(8,128)(2,1)S(1)}, u32[]{:S(2)}, u32[]{:S(2)}) collective-permute-start(bf16[16,2,16,128]{3,2,1,0:T(8,128)(2,1)S(1)} %get-tuple-element.47), channel_id=1, source_target_pairs={{0,6},{1,39},{2,64},{3,97},{4,130},{5,163},{6,196},{7,229},{8,14},... | collective-permute-start | bytes 393224 | tf_op jit(solution)/shard_map/ppermute | solution.py:184
  114.6 11.1 %collective-permute-start.7 = (bf16[16,2,16,128]{3,2,1,0:T(8,128)(2,1)S(1)}, bf16[16,2,16,128]{3,2,1,0:T(8,128)(2,1)S(1)}, u32[]{:S(2)}, u32[]{:S(2)}) collective-permute-start(bf16[16,2,16,128]{3,2,1,0:T(8,128)(2,1)S(1)} %get-tuple-element.36), channel_id=1, source_target_pairs={{0,7},{1,32},{2,65},{3,98},{4,131},{5,164},{6,197},{7,230},{8,15},... | collective-permute-start | bytes 393224 | tf_op jit(solution)/shard_map/ppermute | solution.py:184
  118.1 30.9 %collective-permute-start.3 = (bf16[16,2,16,128]{3,2,1,0:T(8,128)(2,1)S(1)}, bf16[16,2,16,128]{3,2,1,0:T(8,128)(2,1)S(1)}, u32[]{:S(2)}, u32[]{:S(2)}) collective-permute-start(bf16[16,2,16,128]{3,2,1,0:T(8,128)(2,1)S(1)} %get-tuple-element.32), channel_id=1, source_target_pairs={{0,3},{1,36},{2,69},{3,102},{4,135},{5,160},{6,193},{7,226},{8,11}... | collective-permute-start | bytes 393224 | tf_op jit(solution)/shard_map/ppermute | solution.py:184
  125.7 39.0 %collective-permute-start.20 = (bf16[8,2,4,2,16,128]{5,4,3,2,1,0:T(8,128)(2,1)S(1)}, bf16[8,2,4,2,16,128]{5,4,3,2,1,0:T(8,128)(2,1)S(1)}, u32[]{:S(2)}, u32[]{:S(2)}) collective-permute-start(bf16[8,2,4,2,16,128]{5,4,3,2,1,0:T(8,128)(2,1)S(1)} %constant_dynamic-update-slice_fusion.8), channel_id=1, source_target_pairs={{32,0},{40,8},{48,16},{56,24},{64,32},{72,40},{80,48},{88,56},{96,... | collective-permute-start | bytes 1572872 | tf_op jit(solution)/shard_map/ppermute | solution.py:186
  129.6 27.6 %collective-permute-start.4 = (bf16[16,2,16,128]{3,2,1,0:T(8,128)(2,1)S(1)}, bf16[16,2,16,128]{3,2,1,0:T(8,128)(2,1)S(1)}, u32[]{:S(2)}, u32[]{:S(2)}) collective-permute-start(bf16[16,2,16,128]{3,2,1,0:T(8,128)(2,1)S(1)} %get-tuple-element.33), channel_id=1, source_target_pairs={{0,4},{1,37},{2,70},{3,103},{4,128},{5,161},{6,194},{7,227},{8,12}... | collective-permute-start | bytes 393224 | tf_op jit(solution)/shard_map/ppermute | solution.py:184
  136.1 33.7 %collective-permute-start.5 = (bf16[16,2,16,128]{3,2,1,0:T(8,128)(2,1)S(1)}, bf16[16,2,16,128]{3,2,1,0:T(8,128)(2,1)S(1)}, u32[]{:S(2)}, u32[]{:S(2)}) collective-permute-start(bf16[16,2,16,128]{3,2,1,0:T(8,128)(2,1)S(1)} %get-tuple-element.34), channel_id=1, source_target_pairs={{0,5},{1,38},{2,71},{3,96},{4,129},{5,162},{6,195},{7,228},{8,13},... | collective-permute-start | bytes 393224 | tf_op jit(solution)/shard_map/ppermute | solution.py:184
  147.1 22.7 %collective-permute-start.6 = (bf16[16,2,16,128]{3,2,1,0:T(8,128)(2,1)S(1)}, bf16[16,2,16,128]{3,2,1,0:T(8,128)(2,1)S(1)}, u32[]{:S(2)}, u32[]{:S(2)}) collective-permute-start(bf16[16,2,16,128]{3,2,1,0:T(8,128)(2,1)S(1)} %get-tuple-element.35), channel_id=1, source_target_pairs={{0,6},{1,39},{2,64},{3,97},{4,130},{5,163},{6,196},{7,229},{8,14},... | collective-permute-start | bytes 393224 | tf_op jit(solution)/shard_map/ppermute | solution.py:184
  166.1 27.3 %collective-permute-start.21 = (bf16[8,3,4,2,16,128]{5,4,3,2,1,0:T(8,128)(2,1)S(1)}, bf16[8,3,4,2,16,128]{5,4,3,2,1,0:T(8,128)(2,1)S(1)}, u32[]{:S(2)}, u32[]{:S(2)}) collective-permute-start(bf16[8,3,4,2,16,128]{5,4,3,2,1,0:T(8,128)(2,1)S(1)} %get-tuple-element.50), channel_id=1, source_target_pairs={{0,8},{8,16},{16,24},{24,0},{32,40},{40,48},{48,56},{56,32},{64,72... | collective-permute-start | bytes 2359304 | tf_op jit(solution)/shard_map/ppermute | solution.py:191
  169.9 16.4 %collective-permute-start.8 = (bf16[8,2,4,2,16,128]{5,4,3,2,1,0:T(8,128)(2,1)S(1)}, bf16[8,2,4,2,16,128]{5,4,3,2,1,0:T(8,128)(2,1)S(1)}, u32[]{:S(2)}, u32[]{:S(2)}) collective-permute-start(bf16[8,2,4,2,16,128]{5,4,3,2,1,0:T(8,128)(2,1)S(1)} %constant_dynamic-update-slice_fusion), channel_id=1, source_target_pairs={{32,0},{40,8},{48,16},{56,24},{64,32},{72,40},{80,48},{88,56},{96,... | collective-permute-start | bytes 1572872 | tf_op jit(solution)/shard_map/ppermute | solution.py:186
  176.3 29.6 %collective-permute-start.22 = (bf16[8,3,4,2,16,128]{5,4,3,2,1,0:T(8,128)(2,1)}, bf16[8,3,4,2,16,128]{5,4,3,2,1,0:T(8,128)(2,1)S(1)}, u32[]{:S(2)}, u32[]{:S(2)}) collective-permute-start(bf16[8,3,4,2,16,128]{5,4,3,2,1,0:T(8,128)(2,1)} %get-tuple-element.51), channel_id=1, source_target_pairs={{0,16},{8,24},{16,0},{24,8},{32,48},{40,56},{48,32},{56,40},{64,80... | collective-permute-start | bytes 2359304 | tf_op jit(solution)/shard_map/ppermute | solution.py:191
  179.6 36.2 %collective-permute-start.23 = (bf16[8,3,4,2,16,128]{5,4,3,2,1,0:T(8,128)(2,1)}, bf16[8,3,4,2,16,128]{5,4,3,2,1,0:T(8,128)(2,1)S(1)}, u32[]{:S(2)}, u32[]{:S(2)}) collective-permute-start(bf16[8,3,4,2,16,128]{5,4,3,2,1,0:T(8,128)(2,1)} %get-tuple-element.52), channel_id=1, source_target_pairs={{0,24},{8,0},{16,8},{24,16},{32,56},{40,32},{48,40},{56,48},{64,88... | collective-permute-start | bytes 2359304 | tf_op jit(solution)/shard_map/ppermute | solution.py:191
  188.1 0.9 copy-start.2
  188.9 33.8 %collective-permute-start.9 = (bf16[8,3,4,2,16,128]{5,4,3,2,1,0:T(8,128)(2,1)}, bf16[8,3,4,2,16,128]{5,4,3,2,1,0:T(8,128)(2,1)}, u32[]{:S(2)}, u32[]{:S(2)}) collective-permute-start(bf16[8,3,4,2,16,128]{5,4,3,2,1,0:T(8,128)(2,1)} %get-tuple-element.38), channel_id=1, source_target_pairs={{0,8},{8,16},{16,24},{24,0},{32,40},{40,48},{48,56},{56,32},{64,72... | collective-permute-start | bytes 2359304 | tf_op jit(solution)/shard_map/ppermute | solution.py:191
  190.5 47.8 %collective-permute-start.10 = (bf16[8,3,4,2,16,128]{5,4,3,2,1,0:T(8,128)(2,1)}, bf16[8,3,4,2,16,128]{5,4,3,2,1,0:T(8,128)(2,1)}, u32[]{:S(2)}, u32[]{:S(2)}) collective-permute-start(bf16[8,3,4,2,16,128]{5,4,3,2,1,0:T(8,128)(2,1)} %get-tuple-element.39), channel_id=1, source_target_pairs={{0,16},{8,24},{16,0},{24,8},{32,48},{40,56},{48,32},{56,40},{64,80... | collective-permute-start | bytes 2359304 | tf_op jit(solution)/shard_map/ppermute | solution.py:191
  193.4 53.6 %collective-permute-start.11 = (bf16[8,3,4,2,16,128]{5,4,3,2,1,0:T(8,128)(2,1)}, bf16[8,3,4,2,16,128]{5,4,3,2,1,0:T(8,128)(2,1)}, u32[]{:S(2)}, u32[]{:S(2)}) collective-permute-start(bf16[8,3,4,2,16,128]{5,4,3,2,1,0:T(8,128)(2,1)} %get-tuple-element.40), channel_id=1, source_target_pairs={{0,24},{8,0},{16,8},{24,16},{32,56},{40,32},{48,40},{56,48},{64,88... | collective-permute-start | bytes 2359304 | tf_op jit(solution)/shard_map/ppermute | solution.py:191
  194.8 52.3 %copy-start.3 = (bf16[8,3,4,2,16,128]{5,4,3,2,1,0:T(8,128)(2,1)S(1)}, bf16[8,3,4,2,16,128]{5,4,3,2,1,0:T(8,128)(2,1)}, u32[]{:S(2)}) copy-start(bf16[8,3,4,2,16,128]{5,4,3,2,1,0:T(8,128)(2,1)} %copy-done.2) | copy-start | bytes 2359300

commit v2 on v1

v2 whole, which is shorter than its diff:
```python
import functools
import math

import jax
import jax.numpy as jnp
import numpy as np
from jax import lax
from jax.experimental import pallas as pl
from jax.experimental.pallas import tpu as pltpu
from jax.sharding import PartitionSpec as P

WINLEN = 100
NBIN = 16
BLOCK = 128
WIN_DEV = 16
WINDOWS = 512
PAIRS = 9
NZ, NY, NC = 8, 4, 8
NF = 2
GROUP = 4
REACH = 12
COLS = 512


def dft_rows():
    t = np.arange(WINLEN)
    bins = np.arange(NBIN) + 4
    angle = 2.0 * np.pi * bins[:, None] * t[None, :] / WINLEN
    table = np.stack([np.cos(angle), -np.sin(angle)], axis=1) * math.sqrt(2.0 / WINLEN)
    high = table.astype(jnp.bfloat16)
    low = (table - high.astype(np.float64)).astype(jnp.bfloat16)
    parts = np.stack([high, low]).astype(np.float32).reshape(2, NC, NF, 2, WINLEN)
    parts = parts.transpose(2, 1, 0, 3, 4)
    rows = parts[:, :, :, :, None, :, None] * np.eye(WIN_DEV, dtype=np.float32)[:, None, :]
    return rows.reshape(NF, NC, 4 * WIN_DEV, WINLEN * WIN_DEV).astype(jnp.bfloat16)


def spectra_kernel(order, records, alive, *refs):
    rows, outs = refs[:NC], refs[NC:]
    x = records[...]
    signal = x.astype(jnp.float32)
    power = jnp.sum(signal * signal, axis=0) * (1.0 / WINLEN)
    scale = alive[...].astype(jnp.float32) / jnp.sqrt(power + 1e-05)
    x = x.reshape(WINLEN * WIN_DEV, COLS)
    lhs = jnp.concatenate([r[0, 0] for r in rows], axis=0)
    y = jnp.dot(lhs, x, preferred_element_type=jnp.float32)
    for k in range(NC):
        at = 4 * WIN_DEV * k
        value = y[at : at + 2 * WIN_DEV] + y[at + 2 * WIN_DEV : at + 4 * WIN_DEV]
        for p in range(2):
            scaled = (value[p * WIN_DEV : (p + 1) * WIN_DEV] * scale).astype(jnp.bfloat16)
            for b in range(COLS // BLOCK):
                part = scaled[:, b * BLOCK : (b + 1) * BLOCK]
                if len(outs) == NC:
                    outs[k][b, p] = part
                else:
                    outs[0][k, b, p] = part


def spectra_of(f, records, alive, rows, order, apart):
    channels = records.shape[2]
    blocks = channels // BLOCK
    per = COLS // BLOCK
    if apart:
        shape = [jax.ShapeDtypeStruct((blocks, 2, WIN_DEV, BLOCK), jnp.bfloat16)] * NC
        out_specs = [pl.BlockSpec((per, 2, WIN_DEV, BLOCK), lambda n, o: (n, 0, 0, 0))] * NC
    else:
        shape = jax.ShapeDtypeStruct((NC, blocks, 2, WIN_DEV, BLOCK), jnp.bfloat16)
        out_specs = pl.BlockSpec((NC, per, 2, WIN_DEV, BLOCK), lambda n, o: (0, n, 0, 0, 0))
    grid_spec = pltpu.PrefetchScalarGridSpec(
        num_scalar_prefetch=1,
        grid=(channels // COLS,),
        in_specs=[
            pl.BlockSpec((WINLEN, WIN_DEV, COLS), lambda n, o: (0, 0, n)),
            pl.BlockSpec((1, COLS), lambda n, o: (0, n)),
        ]
        + [pl.BlockSpec((1, 1) + rows.shape[2:], lambda n, o, k=k: (f, o[k], 0, 0)) for k in range(NC)],
        out_specs=out_specs,
    )
    return pl.pallas_call(
        spectra_kernel,
        grid_spec=grid_spec,
        out_shape=shape,
        compiler_params=pltpu.CompilerParams(vmem_limit_bytes=60 << 20),
        name="spectra",
    )(order, records, alive, *([rows] * NC))


def arrange_kernel(order, *refs):
    for k in range(NC):
        refs[NC][order[k]] = refs[k][...]


def arrange(order, slots):
    vmem = pl.BlockSpec(memory_space=pltpu.VMEM)
    return pl.pallas_call(
        arrange_kernel,
        in_specs=[pl.BlockSpec(memory_space=pltpu.SMEM)] + [vmem] * NC,
        out_specs=vmem,
        out_shape=jax.ShapeDtypeStruct((NC,) + slots[0].shape, jnp.bfloat16),
        compiler_params=pltpu.CompilerParams(vmem_limit_bytes=16 << 20),
        name="arrange",
    )(order, *slots)


def pack_kernel(first, count, place, *refs):
    planes, halo, outs = refs[0], refs[1], refs[-NY:]
    y = place[0]
    for k in range(NY):
        target = lax.rem(y + k, NY)
        for i in range(count):
            group = target + first + i
            if first == 0:
                outs[k][:, i] = planes[:, group]
            else:

                @pl.when(group < NY)
                def _():
                    outs[k][:, i] = planes[:, group]

                @pl.when(group >= NY)
                def _():
                    outs[k][:, i] = halo[:, group - NY]


def pack(place, first, count, *sources):
    vmem = pl.BlockSpec(memory_space=pltpu.VMEM)
    shape = jax.ShapeDtypeStruct((NZ, count, GROUP, 2, WIN_DEV, BLOCK), jnp.bfloat16)
    return pl.pallas_call(
        functools.partial(pack_kernel, first, count),
        in_specs=[pl.BlockSpec(memory_space=pltpu.SMEM)] + [vmem] * len(sources),
        out_specs=[vmem] * NY,
        out_shape=[shape] * NY,
        compiler_params=pltpu.CompilerParams(vmem_limit_bytes=16 << 20),
        name="pack",
    )(place, *sources)


def stack_kernel(relative, *refs):
    near, far, out, window, own_t = refs[:NY], refs[NY : 2 * NY], refs[-3], refs[-2], refs[-1]
    a = pl.program_id(0)
    rows = NZ * WIN_DEV

    @pl.when(a == 0)
    def _():
        for y in range(NY):
            for b in range(REACH):
                for p in range(2):
                    ref, at = (near[y], b) if b < GROUP else (far[y], b - GROUP)
                    tile = ref[:, at // GROUP, at % GROUP, p].reshape(rows, BLOCK)
                    window[b, y * rows : (y + 1) * rows, p * BLOCK : (p + 1) * BLOCK] = tile

    own_t[...] = window[a].T
    for k in range(PAIRS):
        other = window[relative[a, k]]
        product = jnp.dot(own_t[...], other, preferred_element_type=jnp.float32)
        real = product[:BLOCK, :BLOCK] + product[BLOCK:, BLOCK:]
        imag = product[:BLOCK, BLOCK:] - product[BLOCK:, :BLOCK]
        inverse = 1.0 / math.sqrt(WINDOWS)
        out[0, k, 0, 0] = (real * inverse).astype(jnp.bfloat16)
        out[0, k, 0, 1] = (imag * inverse).astype(jnp.bfloat16)


def stacks(relative, near, far, f, earlier=None):
    shape = (GROUP, PAIRS, NF, 2, BLOCK, BLOCK)
    args = [*near, *far]
    specs = [pl.BlockSpec(s.shape, lambda a, r: (0,) * 6) for s in args]
    aliases = {}
    if earlier is not None:
        aliases = {1 + len(args): 0}
        args.append(earlier)
        specs.append(pl.BlockSpec(memory_space=pl.ANY))
    grid_spec = pltpu.PrefetchScalarGridSpec(
        num_scalar_prefetch=1,
        grid=(GROUP,),
        in_specs=specs,
        out_specs=pl.BlockSpec((1, PAIRS, 1, 2, BLOCK, BLOCK), lambda a, r: (a, 0, f, 0, 0, 0)),
        scratch_shapes=[
            pltpu.VMEM((REACH, WINDOWS, 2 * BLOCK), jnp.bfloat16),
            pltpu.VMEM((2 * BLOCK, WINDOWS), jnp.bfloat16),
        ],
    )
    return pl.pallas_call(
        stack_kernel,
        grid_spec=grid_spec,
        out_shape=jax.ShapeDtypeStruct(shape, jnp.bfloat16),
        input_output_aliases=aliases,
        compiler_params=pltpu.CompilerParams(vmem_limit_bytes=24 << 20),
        name="stacks",
    )(relative, *args)


def per_device(records, alive, partner):
    tm = lax.axis_index("tm")
    place = (tm % NY).reshape(1).astype(jnp.int32)
    relative = partner - tm * GROUP
    rows = jnp.asarray(dft_rows())
    records, alive = jnp.transpose(records, (1, 0, 2)), alive.reshape(1, -1)
    columns = [[z * NY + y for z in range(NZ)] for y in range(NY)]
    down = [(i, i - NY) for i in range(NY, NZ * NY)]
    rounds = [[(i, i // NY * NY + (i + k) % NY) for i in range(NZ * NY)] for k in range(NY)]

    def along_y(packed):
        return [packed[0]] + [lax.ppermute(packed[k], "tm", rounds[k]) for k in range(1, NY)]

    def across_z(sent):
        planes = lax.all_to_all(
            sent, "tm", split_axis=0, concat_axis=0, tiled=True, axis_index_groups=columns
        )
        return planes.reshape(NZ, NY, GROUP, 2, WIN_DEV, BLOCK)

    def halo_of(planes):
        return lax.ppermute(planes[:, :2], "tm", down)

    barrier = lax.optimization_barrier
    plain = jnp.arange(NC, dtype=jnp.int32)
    mixed = jnp.bitwise_xor(plain, lax.axis_index("chan").astype(jnp.int32))
    own0 = spectra_of(0, records, alive, rows, plain, False)
    own1 = spectra_of(1, records, alive, rows, mixed, True)
    sent0 = lax.all_to_all(own0, "chan", split_axis=0, concat_axis=0, tiled=True)
    sent0, own1 = barrier((sent0, own1))
    planes0 = across_z(sent0)
    slots1 = [own1[0]]
    for k in range(1, NC):
        slots1.append(lax.ppermute(own1[k], "chan", [(c, c ^ k) for c in range(NC)]))
    planes0, slots1 = barrier((planes0, slots1))
    near0 = along_y(pack(place, 0, 1, planes0))
    far0 = pack(place, 1, 2, planes0, halo_of(planes0))
    sent1 = arrange(mixed, slots1)
    sent1, near0, far0 = barrier((sent1, near0, far0))
    far0 = along_y(far0)
    planes1 = across_z(sent1)
    planes1, near0, far0 = barrier((planes1, near0, far0))
    halo1 = halo_of(planes1)
    near1 = along_y(pack(place, 0, 1, planes1))
    halo1, near1 = barrier((halo1, near1))
    far1 = along_y(pack(place, 1, 2, planes1, halo1))
    result = stacks(relative, near0, far0, 0)
    return stacks(relative, near1, far1, 1, result)


def solution(mesh):
    return jax.shard_map(
        per_device,
        mesh=mesh,
        in_specs=(P("tm", None, "chan"), P("chan"), P("tm", None)),
        out_specs=P("tm", None, "chan", None, None, None),
        check_vma=False,
    )
```

time: 254 us -> 172 us (0.68)
  starting transfers between devices: 132 us -> 50.1 us
  waiting for transfers between devices: 89.3 us -> 79.5 us
  Pallas kernels: 24.9 us -> 32.3 us
    ppermute x24 -> x21, starting transfers between devices: 132 us -> 33.7 us  [the longest x12 19.7 us: along_y(): lax.ppermute(packed[k], 'tm', rounds[k])]
    ppermute x24 -> x21, waiting for transfers between devices: 89.3 us -> 65.7 us  [the longest x12 50 us: along_y(): lax.ppermute(packed[k], 'tm', rounds[k])]
    all_to_all x0 -> x3, starting transfers between devices: none -> 16.4 us  [the longest x2 12.1 us: across_z(): lax.all_to_all(sent, 'tm', split_axis=0, concat_axis=0, tiled=True, axis_...]
    all_to_all x0 -> x3, waiting for transfers between devices: none -> 13.7 us  [the longest x1 7 us: per_device(): lax.all_to_all(own0, 'chan', split_axis=0, concat_axis=0, tiled=True)]
    pallas_call x3 -> x7, Pallas kernels: 13.8 us -> 20.5 us  [the longest x2 17.2 us: spectra_of(): pl.pallas_call(spectra_kernel, grid_spec=grid_spec, out_shape=shape, comp...]
    unnamed x26 -> x44, local copies, waits for them, and re-layouts: 6.6 us -> 7.41 us
  transfers between devices with their start and end apart: 24 -> 24, of which waited for: 10 -> 15; matrix products, arithmetic and copies ran while one was open for 0% -> 0% of each run, Pallas kernels for 3% -> 9%
where the time goes in v2:
time: 172 us; the launch traced here: 171 us
  waiting for transfers between devices  79.5 us (46%)
  starting transfers between devices  50.1 us (29%)
  Pallas kernels  32.3 us (19%)
  local copies, waits for them, and re-layouts  8.78 us (5%)
    ppermute x12, waiting for transfers between devices, along_y(): lax.ppermute(packed[k], 'tm', rounds[k])  50 us
    ppermute x12, starting transfers between devices, along_y(): lax.ppermute(packed[k], 'tm', rounds[k])  19.7 us
    pallas_call x2, Pallas kernels, spectra_of(): pl.pallas_call(spectra_kernel, grid_spec=grid_spec, out_shape=shape, comp...  17.2 us
    ppermute x7, waiting for transfers between devices, per_device(): lax.ppermute(own1[k], 'chan', [(c, c ^ k) for c in range(NC)])  12.6 us
    all_to_all x2, starting transfers between devices, across_z(): lax.all_to_all(sent, 'tm', split_axis=0, concat_axis=0, tiled=True, axis_...  12.1 us
    pallas_call x2, Pallas kernels, stacks(): pl.pallas_call(stack_kernel, grid_spec=grid_spec, out_shape=jax.ShapeDtyp...  11.8 us
    ppermute x7, starting transfers between devices, per_device(): lax.ppermute(own1[k], 'chan', [(c, c ^ k) for c in range(NC)])  7.74 us
    unnamed x44, local copies, waits for them, and re-layouts  7.41 us
  transfers between devices with their start and end apart: 24, of which 15 were waited for; matrix products, arithmetic and copies ran while one was open for 0% of the time, Pallas kernels for 9%

profile of v2, /device:TPU:32, one launch (start us, length us, event | category | flops | bytes accessed | tf_op | source)
XLA Modules:
  0.0 171.4 jit_solution(13690999382890992357)
XLA Ops:
  0.5 8.6 %spectra.2 = bf16[8,16,2,16,128]{4,3,2,1,0:T(8,128)(2,1)} custom-call(s32[8]{0:T(128)} %iota.6.order, bf16[100,16,2048]{2,1,0:T(8,128)(2,1)} %bitcast.11, s32[1,2048]{1,0:T(1,128)} %bitcast.13, bf16[2,8,64,1600]{3,2,1,0:T(8,128)(2,1)} %constant.24.clone.refs_0_.refs_1_.refs_2_.refs_3_.refs_4_.refs_5_.refs_6_.refs_7_, ...), custom_call_target="tpu_custom_call" | custom-call | tf_op jit(solution)/shard_map/spectra/pallas_call | solution.py:80
  9.1 4.3 %all-to-all-start = ((bf16[8,16,2,16,128]{4,3,2,1,0:T(8,128)(2,1)}), bf16[8,16,2,16,128]{4,3,2,1,0:T(8,128)(2,1)}, u32[]{:S(2)}, u32[]{:S(2)}) async-start(bf16[8,16,2,16,128]{4,3,2,1,0:T(8,128)(2,1)} %spectra.2), calls=%async_computation | async-start | bytes 2097152 | tf_op jit(solution)/shard_map/all_to_all | solution.py:220
  13.9 8.6 %spectra.3 = (bf16[16,2,16,128]{3,2,1,0:T(8,128)(2,1)}, bf16[16,2,16,128]{3,2,1,0:T(8,128)(2,1)}, bf16[16,2,16,128]{3,2,1,0:T(8,128)(2,1)}, bf16[16,2,16,128]{3,...) custom-call(s32[8]{0:T(128)} %iota_xor_fusion.order, ...), custom_call_target="tpu_custom_call" | custom-call | tf_op jit(solution)/shard_map/spectra/pallas_call | solution.py:80
  22.5 7.0 %all-to-all-done = bf16[8,16,2,16,128]{4,3,2,1,0:T(8,128)(2,1)} async-done(((bf16[8,16,2,16,128]{4,3,2,1,0:T(8,128)(2,1)}), bf16[8,16,2,16,128]{4,3,2,1,0:T(8,128)(2,1)}, u32[]{:S(2)}, u32[]{:S(2)}) %all-to-all-start) | async-done | bytes 1048608 | tf_op jit(solution)/shard_map/all_to_all | solution.py:220
  29.5 8.6 %all-to-all-start.1 = ((bf16[8,16,2,16,128]{4,3,2,1,0:T(8,128)(2,1)}), bf16[8,16,2,16,128]{4,3,2,1,0:T(8,128)(2,1)S(1)}, u32[]{:S(2)}, u32[]{:S(2)}) async-start(bf16[8,16,2,16,128]{4,3,2,1,0:T(8,128)(2,1)} %all-to-all-done), calls=%async_computation.1 | async-start | bytes 2097152 | tf_op jit(solution)/shard_map/all_to_all | solution.py:207
  38.6 1.3 collective-permute-start.2
  39.9 0.9 collective-permute-start.3
  40.8 2.2 %collective-permute-start.4 = (bf16[16,2,16,128]{3,2,1,0:T(8,128)(2,1)}, bf16[16,2,16,128]{3,2,1,0:T(8,128)(2,1)S(1)}, u32[]{:S(2)}, u32[]{:S(2)}) collective-permute-start(bf16[16,2,16,128]{3,2,1,0:T(8,128)(2,1)} %get-tuple-element.84), channel_id=1, source_target_pairs={{0,5},{1,4},{2,7},{3,6},{4,1},{5,0},{6,3},{7,2},{8,13},{9,12},{10,... | collective-permute-start | bytes 393224 | tf_op jit(solution)/shard_map/ppermute | solution.py:225
  43.0 1.2 collective-permute-start.5
  44.5 1.6 collective-permute-start.6
  46.6 4.3 %collective-permute-done.3.refs_4_ = bf16[16,2,16,128]{3,2,1,0:T(8,128)(2,1)S(1)} collective-permute-done((bf16[16,2,16,128]{3,2,1,0:T(8,128)(2,1)}, bf16[16,2,16,128]{3,2,1,0:T(8,128)(2,1)S(1)}, u32[]{:S(2)}, u32[]{:S(2)}) %collective-permute-start.3) | collective-permute-done | bytes 131104 | tf_op jit(solution)/shard_map/ppermute | solution.py:225
  50.9 2.1 %collective-permute-done.4.refs_5_ = bf16[16,2,16,128]{3,2,1,0:T(8,128)(2,1)S(1)} collective-permute-done((bf16[16,2,16,128]{3,2,1,0:T(8,128)(2,1)}, bf16[16,2,16,128]{3,2,1,0:T(8,128)(2,1)S(1)}, u32[]{:S(2)}, u32[]{:S(2)}) %collective-permute-start.4) | collective-permute-done | bytes 131104 | tf_op jit(solution)/shard_map/ppermute | solution.py:225
  52.9 3.1 %collective-permute-done.5.refs_6_ = bf16[16,2,16,128]{3,2,1,0:T(8,128)(2,1)S(1)} collective-permute-done((bf16[16,2,16,128]{3,2,1,0:T(8,128)(2,1)}, bf16[16,2,16,128]{3,2,1,0:T(8,128)(2,1)S(1)}, u32[]{:S(2)}, u32[]{:S(2)}) %collective-permute-start.5) | collective-permute-done | bytes 131104 | tf_op jit(solution)/shard_map/ppermute | solution.py:225
  56.1 2.3 %collective-permute-done.6.refs_7_ = bf16[16,2,16,128]{3,2,1,0:T(8,128)(2,1)S(1)} collective-permute-done((bf16[16,2,16,128]{3,2,1,0:T(8,128)(2,1)}, bf16[16,2,16,128]{3,2,1,0:T(8,128)(2,1)S(1)}, u32[]{:S(2)}, u32[]{:S(2)}) %collective-permute-start.6) | collective-permute-done | bytes 131104 | tf_op jit(solution)/shard_map/ppermute | solution.py:225
  58.4 6.7 %all-to-all-done.1 = bf16[8,16,2,16,128]{4,3,2,1,0:T(8,128)(2,1)S(1)} async-done(((bf16[8,16,2,16,128]{4,3,2,1,0:T(8,128)(2,1)}), bf16[8,16,2,16,128]{4,3,2,1,0:T(8,128)(2,1)S(1)}, u32[]{:S(2)}, u32[]{:S(2)}) %all-to-all-start.1) | async-done | bytes 1048608 | tf_op jit(solution)/shard_map/all_to_all | solution.py:207
  65.1 0.8 slice.6
  66.0 3.4 %collective-permute-start.10 = (bf16[8,2,4,2,16,128]{5,4,3,2,1,0:T(8,128)(2,1)}, bf16[8,2,4,2,16,128]{5,4,3,2,1,0:T(8,128)(2,1)S(1)}, u32[]{:S(2)}, u32[]{:S(2)}) collective-permute-start(bf16[8,2,4,2,16,128]{5,4,3,2,1,0:T(8,128)(2,1)} %slice.6), channel_id=1, source_target_pairs={{32,0},{40,8},{48,16},{56,24},{64,32},{72,40},{80,48},{88,56},{96,... | collective-permute-start | bytes 1572872 | tf_op jit(solution)/shard_map/ppermute | solution.py:213
  69.4 1.7 collective-permute-start.7
  71.1 2.9 %collective-permute-start.8 = (bf16[8,1,4,2,16,128]{5,4,3,2,1,0:T(8,128)(2,1)S(1)}, bf16[8,1,4,2,16,128]{5,4,3,2,1,0:T(8,128)(2,1)S(1)}, u32[]{:S(2)}, u32[]{:S(2)}) collective-permute-start(bf16[8,1,4,2,16,128]{5,4,3,2,1,0:T(8,128)(2,1)S(1)} %get-tuple-element.98), channel_id=1, source_target_pairs={{0,16},{8,24},{16,0},{24,8},{32,48},{40,56},{48,32},{56,40},{64,80... | collective-permute-start | bytes 786440 | tf_op jit(solution)/shard_map/ppermute | solution.py:204
  74.0 1.3 collective-permute-start.9
  75.3 0.9 copy-done.16
  76.2 1.6 arrange.1
  77.8 3.2 %collective-permute-done.10.refs_1_ = bf16[8,2,4,2,16,128]{5,4,3,2,1,0:T(8,128)(2,1)S(1)} collective-permute-done((bf16[8,2,4,2,16,128]{5,4,3,2,1,0:T(8,128)(2,1)}, bf16[8,2,4,2,16,128]{5,4,3,2,1,0:T(8,128)(2,1)S(1)}, u32[]{:S(2)}, u32[]{:S(2)}) %collective-permute-start.10) | collective-permute-done | bytes 524320 | tf_op jit(solution)/shard_map/ppermute | solution.py:213
  81.3 4.2 %collective-permute-done.8.refs_2_ = bf16[8,1,4,2,16,128]{5,4,3,2,1,0:T(8,128)(2,1)S(1)} collective-permute-done((bf16[8,1,4,2,16,128]{5,4,3,2,1,0:T(8,128)(2,1)S(1)}, bf16[8,1,4,2,16,128]{5,4,3,2,1,0:T(8,128)(2,1)S(1)}, u32[]{:S(2)}, u32[]{:S(2)}) %collective-permute-start.8) | collective-permute-done | bytes 262176 | tf_op jit(solution)/shard_map/ppermute | solution.py:204
  85.5 3.5 %all-to-all-start.2 = ((bf16[8,16,2,16,128]{4,3,2,1,0:T(8,128)(2,1)}), bf16[8,16,2,16,128]{4,3,2,1,0:T(8,128)(2,1)S(1)}, u32[]{:S(2)}, u32[]{:S(2)}) async-start(bf16[8,16,2,16,128]{4,3,2,1,0:T(8,128)(2,1)} %arrange.1), calls=%async_computation.2 | async-start | bytes 2097152 | tf_op jit(solution)/shard_map/all_to_all | solution.py:207
  89.1 1.3 collective-permute-start.11
  90.4 2.4 %collective-permute-start.12 = (bf16[8,2,4,2,16,128]{5,4,3,2,1,0:T(8,128)(2,1)}, bf16[8,2,4,2,16,128]{5,4,3,2,1,0:T(8,128)(2,1)S(1)}, u32[]{:S(2)}, u32[]{:S(2)}) collective-permute-start(bf16[8,2,4,2,16,128]{5,4,3,2,1,0:T(8,128)(2,1)} %copy-done.19), channel_id=1, source_target_pairs={{0,16},{8,24},{16,0},{24,8},{32,48},{40,56},{48,32},{56,40},{64,80... | collective-permute-start | bytes 1572872 | tf_op jit(solution)/shard_map/ppermute | solution.py:204
  92.8 1.6 collective-permute-start.13
  94.4 9.3 %collective-permute-done.11.refs_5_ = bf16[8,2,4,2,16,128]{5,4,3,2,1,0:T(8,128)(2,1)S(1)} collective-permute-done((bf16[8,2,4,2,16,128]{5,4,3,2,1,0:T(8,128)(2,1)}, bf16[8,2,4,2,16,128]{5,4,3,2,1,0:T(8,128)(2,1)S(1)}, u32[]{:S(2)}, u32[]{:S(2)}) %collective-permute-start.11) | collective-permute-done | bytes 524320 | tf_op jit(solution)/shard_map/ppermute | solution.py:204
  103.6 12.4 %collective-permute-done.12.refs_6_ = bf16[8,2,4,2,16,128]{5,4,3,2,1,0:T(8,128)(2,1)S(1)} collective-permute-done((bf16[8,2,4,2,16,128]{5,4,3,2,1,0:T(8,128)(2,1)}, bf16[8,2,4,2,16,128]{5,4,3,2,1,0:T(8,128)(2,1)S(1)}, u32[]{:S(2)}, u32[]{:S(2)}) %collective-permute-start.12) | collective-permute-done | bytes 524320 | tf_op jit(solution)/shard_map/ppermute | solution.py:204
  116.1 2.9 %collective-permute-start.14 = (bf16[8,2,4,2,16,128]{5,4,3,2,1,0:T(8,128)(2,1)S(1)}, bf16[8,2,4,2,16,128]{5,4,3,2,1,0:T(8,128)(2,1)S(1)}, u32[]{:S(2)}, u32[]{:S(2)}) collective-permute-start(bf16[8,2,4,2,16,128]{5,4,3,2,1,0:T(8,128)(2,1)S(1)} %slice.7), channel_id=1, source_target_pairs={{32,0},{40,8},{48,16},{56,24},{64,32},{72,40},{80,48},{88,56},{96,... | collective-permute-start | bytes 1572872 | tf_op jit(solution)/shard_map/ppermute | solution.py:213
  119.8 1.3 collective-permute-start.15
  121.1 3.1 %collective-permute-start.16 = (bf16[8,1,4,2,16,128]{5,4,3,2,1,0:T(8,128)(2,1)S(1)}, bf16[8,1,4,2,16,128]{5,4,3,2,1,0:T(8,128)(2,1)S(1)}, u32[]{:S(2)}, u32[]{:S(2)}) collective-permute-start(bf16[8,1,4,2,16,128]{5,4,3,2,1,0:T(8,128)(2,1)S(1)} %get-tuple-element.116), channel_id=1, source_target_pairs={{0,16},{8,24},{16,0},{24,8},{32,48},{40,56},{48,32},{56,40},{64,80... | collective-permute-start | bytes 786440 | tf_op jit(solution)/shard_map/ppermute | solution.py:204
  124.2 0.9 collective-permute-start.17
  125.1 9.4 %collective-permute-done.15.refs_1_ = bf16[8,1,4,2,16,128]{5,4,3,2,1,0:T(8,128)(2,1)S(1)} collective-permute-done((bf16[8,1,4,2,16,128]{5,4,3,2,1,0:T(8,128)(2,1)S(1)}, bf16[8,1,4,2,16,128]{5,4,3,2,1,0:T(8,128)(2,1)S(1)}, u32[]{:S(2)}, u32[]{:S(2)}) %collective-permute-start.15) | collective-permute-done | bytes 262176 | tf_op jit(solution)/shard_map/ppermute | solution.py:204
  134.6 0.7 copy-done.10
  135.3 0.7 copy-done.12
  136.0 0.7 copy-done.14
  136.7 1.4 pack.7
  138.1 0.8 copy-done
  138.9 3.0 %collective-permute-start.19 = (bf16[8,2,4,2,16,128]{5,4,3,2,1,0:T(8,128)(2,1)}, bf16[8,2,4,2,16,128]{5,4,3,2,1,0:T(8,128)(2,1)}, u32[]{:S(2)}, u32[]{:S(2)}) collective-permute-start(bf16[8,2,4,2,16,128]{5,4,3,2,1,0:T(8,128)(2,1)} %get-tuple-element.125), channel_id=1, source_target_pairs={{0,16},{8,24},{16,0},{24,8},{32,48},{40,56},{48,32},{56,40},{64,80... | collective-permute-start | bytes 1572872 | tf_op jit(solution)/shard_map/ppermute | solution.py:204
  142.1 0.9 copy-done.3
  143.1 0.9 copy-done.5
  144.0 0.9 copy-done.7
  145.0 5.3 %stacks.2.refs_8_ = bf16[4,9,2,2,128,128]{5,4,3,2,1,0:T(8,128)(2,1)} custom-call(s32[4,9]{1,0:T(4,128)S(1)} %broadcast_subtract_fusion.relative, bf16[8,1,4,2,16,128]{5,4,3,2,1,0:T(8,128)(2,1)S(1)} %get-tuple-element.127.refs_0_, bf16[8,1,4,2,16,128]{5,4,3,2,1,0:T(8,128)(2,1)S(1)} %copy-done.3, bf16[8,1,4,2,16,128]{5,4,3,2,1,0:T(8,128)(2,1)S(1)} %copy-done.5, ...), custom_call_target="tpu_custom_call" | custom-call | tf_op jit(solution)/shard_map/stacks/pallas_call | solution.py:183
  150.3 2.2 %collective-permute-done.18.refs_5_ = bf16[8,2,4,2,16,128]{5,4,3,2,1,0:T(8,128)(2,1)S(1)} collective-permute-done((bf16[8,2,4,2,16,128]{5,4,3,2,1,0:T(8,128)(2,1)}, bf16[8,2,4,2,16,128]{5,4,3,2,1,0:T(8,128)(2,1)S(1)}, u32[]{:S(2)}, u32[]{:S(2)}) %collective-permute-start.18) | collective-permute-done | bytes 524320 | tf_op jit(solution)/shard_map/ppermute | solution.py:204
  152.5 12.4 %collective-permute-done.19.refs_6_ = bf16[8,2,4,2,16,128]{5,4,3,2,1,0:T(8,128)(2,1)} collective-permute-done((bf16[8,2,4,2,16,128]{5,4,3,2,1,0:T(8,128)(2,1)}, bf16[8,2,4,2,16,128]{5,4,3,2,1,0:T(8,128)(2,1)}, u32[]{:S(2)}, u32[]{:S(2)}) %collective-permute-start.19) | collective-permute-done | bytes 524320 | tf_op jit(solution)/shard_map/ppermute | solution.py:204
  164.9 6.5 %stacks.3 = bf16[4,9,2,2,128,128]{5,4,3,2,1,0:T(8,128)(2,1)} custom-call(s32[4,9]{1,0:T(4,128)S(1)} %broadcast_subtract_fusion.relative, bf16[8,1,4,2,16,128]{5,4,3,2,1,0:T(8,128)(2,1)S(1)} %copy-done.9, bf16[8,1,4,2,16,128]{5,4,3,2,1,0:T(8,128)(2,1)S(1)} %copy-done.11, ...), custom_call_target="tpu_custom_call", output_to_operand_aliasing={{}: (9, {})} | custom-call | tf_op jit(solution)/shard_map/stacks/pallas_call | solution.py:183
  (58 shorter events, 3.8 us)
Async XLA Ops:
  9.1 20.4 %all-to-all-start = ((bf16[8,16,2,16,128]{4,3,2,1,0:T(8,128)(2,1)}), bf16[8,16,2,16,128]{4,3,2,1,0:T(8,128)(2,1)}, u32[]{:S(2)}, u32[]{:S(2)}) async-start(bf16[8,16,2,16,128]{4,3,2,1,0:T(8,128)(2,1)} %spectra.2), calls=%async_computation | async-start | bytes 2097152 | tf_op jit(solution)/shard_map/all_to_all | solution.py:220
  13.9 61.4 %copy-start.17 = (s32[8]{0:T(128)S(1)}, s32[8]{0:T(128)}, u32[]{:S(2)}) copy-start(s32[8]{0:T(128)} %iota_xor_fusion.order) | copy-start | bytes 100
  29.5 35.6 %all-to-all-start.1 = ((bf16[8,16,2,16,128]{4,3,2,1,0:T(8,128)(2,1)}), bf16[8,16,2,16,128]{4,3,2,1,0:T(8,128)(2,1)S(1)}, u32[]{:S(2)}, u32[]{:S(2)}) async-start(bf16[8,16,2,16,128]{4,3,2,1,0:T(8,128)(2,1)} %all-to-all-done), calls=%async_computation.1 | async-start | bytes 2097152 | tf_op jit(solution)/shard_map/all_to_all | solution.py:207
  38.0 5.0 %collective-permute-start = (bf16[16,2,16,128]{3,2,1,0:T(8,128)(2,1)}, bf16[16,2,16,128]{3,2,1,0:T(8,128)(2,1)S(1)}, u32[]{:S(2)}, u32[]{:S(2)}) collective-permute-start(bf16[16,2,16,128]{3,2,1,0:T(8,128)(2,1)} %get-tuple-element.80), channel_id=1, source_target_pairs={{0,1},{1,0},{2,3},{3,2},{4,5},{5,4},{6,7},{7,6},{8,9},{9,8},{10,11... | collective-permute-start | bytes 393224 | tf_op jit(solution)/shard_map/ppermute | solution.py:225
  38.0 6.5 %collective-permute-start.1 = (bf16[16,2,16,128]{3,2,1,0:T(8,128)(2,1)}, bf16[16,2,16,128]{3,2,1,0:T(8,128)(2,1)S(1)}, u32[]{:S(2)}, u32[]{:S(2)}) collective-permute-start(bf16[16,2,16,128]{3,2,1,0:T(8,128)(2,1)} %get-tuple-element.81), channel_id=1, source_target_pairs={{0,2},{1,3},{2,0},{3,1},{4,6},{5,7},{6,4},{7,5},{8,10},{9,11},{10,... | collective-permute-start | bytes 393224 | tf_op jit(solution)/shard_map/ppermute | solution.py:225
  38.6 8.0 %collective-permute-start.2 = (bf16[16,2,16,128]{3,2,1,0:T(8,128)(2,1)}, bf16[16,2,16,128]{3,2,1,0:T(8,128)(2,1)S(1)}, u32[]{:S(2)}, u32[]{:S(2)}) collective-permute-start(bf16[16,2,16,128]{3,2,1,0:T(8,128)(2,1)} %get-tuple-element.82), channel_id=1, source_target_pairs={{0,3},{1,2},{2,1},{3,0},{4,7},{5,6},{6,5},{7,4},{8,11},{9,10},{10,... | collective-permute-start | bytes 393224 | tf_op jit(solution)/shard_map/ppermute | solution.py:225
  39.9 11.0 %collective-permute-start.3 = (bf16[16,2,16,128]{3,2,1,0:T(8,128)(2,1)}, bf16[16,2,16,128]{3,2,1,0:T(8,128)(2,1)S(1)}, u32[]{:S(2)}, u32[]{:S(2)}) collective-permute-start(bf16[16,2,16,128]{3,2,1,0:T(8,128)(2,1)} %get-tuple-element.83), channel_id=1, source_target_pairs={{0,4},{1,5},{2,6},{3,7},{4,0},{5,1},{6,2},{7,3},{8,12},{9,13},{10,... | collective-permute-start | bytes 393224 | tf_op jit(solution)/shard_map/ppermute | solution.py:225
  40.8 12.1 %collective-permute-start.4 = (bf16[16,2,16,128]{3,2,1,0:T(8,128)(2,1)}, bf16[16,2,16,128]{3,2,1,0:T(8,128)(2,1)S(1)}, u32[]{:S(2)}, u32[]{:S(2)}) collective-permute-start(bf16[16,2,16,128]{3,2,1,0:T(8,128)(2,1)} %get-tuple-element.84), channel_id=1, source_target_pairs={{0,5},{1,4},{2,7},{3,6},{4,1},{5,0},{6,3},{7,2},{8,13},{9,12},{10,... | collective-permute-start | bytes 393224 | tf_op jit(solution)/shard_map/ppermute | solution.py:225
  43.0 13.0 %collective-permute-start.5 = (bf16[16,2,16,128]{3,2,1,0:T(8,128)(2,1)}, bf16[16,2,16,128]{3,2,1,0:T(8,128)(2,1)S(1)}, u32[]{:S(2)}, u32[]{:S(2)}) collective-permute-start(bf16[16,2,16,128]{3,2,1,0:T(8,128)(2,1)} %get-tuple-element.85), channel_id=1, source_target_pairs={{0,6},{1,7},{2,4},{3,5},{4,2},{5,3},{6,0},{7,1},{8,14},{9,15},{10,... | collective-permute-start | bytes 393224 | tf_op jit(solution)/shard_map/ppermute | solution.py:225
  44.5 13.8 %collective-permute-start.6 = (bf16[16,2,16,128]{3,2,1,0:T(8,128)(2,1)}, bf16[16,2,16,128]{3,2,1,0:T(8,128)(2,1)S(1)}, u32[]{:S(2)}, u32[]{:S(2)}) collective-permute-start(bf16[16,2,16,128]{3,2,1,0:T(8,128)(2,1)} %get-tuple-element.86), channel_id=1, source_target_pairs={{0,7},{1,6},{2,5},{3,4},{4,3},{5,2},{6,1},{7,0},{8,15},{9,14},{10,... | collective-permute-start | bytes 393224 | tf_op jit(solution)/shard_map/ppermute | solution.py:225
  66.0 15.0 %collective-permute-start.10 = (bf16[8,2,4,2,16,128]{5,4,3,2,1,0:T(8,128)(2,1)}, bf16[8,2,4,2,16,128]{5,4,3,2,1,0:T(8,128)(2,1)S(1)}, u32[]{:S(2)}, u32[]{:S(2)}) collective-permute-start(bf16[8,2,4,2,16,128]{5,4,3,2,1,0:T(8,128)(2,1)} %slice.6), channel_id=1, source_target_pairs={{32,0},{40,8},{48,16},{56,24},{64,32},{72,40},{80,48},{88,56},{96,... | collective-permute-start | bytes 1572872 | tf_op jit(solution)/shard_map/ppermute | solution.py:213
  69.4 11.8 %collective-permute-start.7 = (bf16[8,1,4,2,16,128]{5,4,3,2,1,0:T(8,128)(2,1)S(1)}, bf16[8,1,4,2,16,128]{5,4,3,2,1,0:T(8,128)(2,1)S(1)}, u32[]{:S(2)}, u32[]{:S(2)}) collective-permute-start(bf16[8,1,4,2,16,128]{5,4,3,2,1,0:T(8,128)(2,1)S(1)} %get-tuple-element.97), channel_id=1, source_target_pairs={{0,8},{8,16},{16,24},{24,0},{32,40},{40,48},{48,56},{56,32},{64,72... | collective-permute-start | bytes 786440 | tf_op jit(solution)/shard_map/ppermute | solution.py:204
  71.1 14.4 %collective-permute-start.8 = (bf16[8,1,4,2,16,128]{5,4,3,2,1,0:T(8,128)(2,1)S(1)}, bf16[8,1,4,2,16,128]{5,4,3,2,1,0:T(8,128)(2,1)S(1)}, u32[]{:S(2)}, u32[]{:S(2)}) collective-permute-start(bf16[8,1,4,2,16,128]{5,4,3,2,1,0:T(8,128)(2,1)S(1)} %get-tuple-element.98), channel_id=1, source_target_pairs={{0,16},{8,24},{16,0},{24,8},{32,48},{40,56},{48,32},{56,40},{64,80... | collective-permute-start | bytes 786440 | tf_op jit(solution)/shard_map/ppermute | solution.py:204
  74.0 11.5 %collective-permute-start.9 = (bf16[8,1,4,2,16,128]{5,4,3,2,1,0:T(8,128)(2,1)S(1)}, bf16[8,1,4,2,16,128]{5,4,3,2,1,0:T(8,128)(2,1)S(1)}, u32[]{:S(2)}, u32[]{:S(2)}) collective-permute-start(bf16[8,1,4,2,16,128]{5,4,3,2,1,0:T(8,128)(2,1)S(1)} %get-tuple-element.99), channel_id=1, source_target_pairs={{0,24},{8,0},{16,8},{24,16},{32,56},{40,32},{48,40},{56,48},{64,88... | collective-permute-start | bytes 786440 | tf_op jit(solution)/shard_map/ppermute | solution.py:204
  75.3 0.9 copy-start.16
  76.2 65.9 %copy-start.21 = (s32[4,9]{1,0:T(4,128)S(1)}, s32[4,9]{1,0:T(4,128)}, u32[]{:S(2)}) copy-start(s32[4,9]{1,0:T(4,128)} %param.6) | copy-start | bytes 436
  81.2 4.3 %copy-start.18 = (bf16[8,2,4,2,16,128]{5,4,3,2,1,0:T(8,128)(2,1)}, bf16[8,2,4,2,16,128]{5,4,3,2,1,0:T(8,128)(2,1)S(1)}, u32[]{:S(2)}) copy-start(bf16[8,2,4,2,16,128]{5,4,3,2,1,0:T(8,128)(2,1)S(1)} %get-tuple-element.112) | copy-start | bytes 1572868
  81.2 4.3 %copy-start.19 = (bf16[8,2,4,2,16,128]{5,4,3,2,1,0:T(8,128)(2,1)}, bf16[8,2,4,2,16,128]{5,4,3,2,1,0:T(8,128)(2,1)S(1)}, u32[]{:S(2)}) copy-start(bf16[8,2,4,2,16,128]{5,4,3,2,1,0:T(8,128)(2,1)S(1)} %get-tuple-element.111) | copy-start | bytes 1572868
  81.2 4.3 %copy-start.20 = (bf16[8,2,4,2,16,128]{5,4,3,2,1,0:T(8,128)(2,1)}, bf16[8,2,4,2,16,128]{5,4,3,2,1,0:T(8,128)(2,1)S(1)}, u32[]{:S(2)}) copy-start(bf16[8,2,4,2,16,128]{5,4,3,2,1,0:T(8,128)(2,1)S(1)} %get-tuple-element.110) | copy-start | bytes 1572868
  81.2 7.8 %copy-start.2 = (bf16[8,1,4,2,16,128]{5,4,3,2,1,0:T(8,128)(2,1)}, bf16[8,1,4,2,16,128]{5,4,3,2,1,0:T(8,128)(2,1)S(1)}, u32[]{:S(2)}) copy-start(bf16[8,1,4,2,16,128]{5,4,3,2,1,0:T(8,128)(2,1)S(1)} %collective-permute-done.7.refs_1_) | copy-start | bytes 786436
  85.5 3.6 %copy-start.4 = (bf16[8,1,4,2,16,128]{5,4,3,2,1,0:T(8,128)(2,1)}, bf16[8,1,4,2,16,128]{5,4,3,2,1,0:T(8,128)(2,1)S(1)}, u32[]{:S(2)}) copy-start(bf16[8,1,4,2,16,128]{5,4,3,2,1,0:T(8,128)(2,1)S(1)} %collective-permute-done.8.refs_2_) | copy-start | bytes 786436
  85.5 4.9 %copy-start.6 = (bf16[8,1,4,2,16,128]{5,4,3,2,1,0:T(8,128)(2,1)}, bf16[8,1,4,2,16,128]{5,4,3,2,1,0:T(8,128)(2,1)S(1)}, u32[]{:S(2)}) copy-start(bf16[8,1,4,2,16,128]{5,4,3,2,1,0:T(8,128)(2,1)S(1)} %collective-permute-done.9.refs_3_) | copy-start | bytes 786436
  85.5 30.5 %all-to-all-start.2 = ((bf16[8,16,2,16,128]{4,3,2,1,0:T(8,128)(2,1)}), bf16[8,16,2,16,128]{4,3,2,1,0:T(8,128)(2,1)S(1)}, u32[]{:S(2)}, u32[]{:S(2)}) async-start(bf16[8,16,2,16,128]{4,3,2,1,0:T(8,128)(2,1)} %arrange.1), calls=%async_computation.2 | async-start | bytes 2097152 | tf_op jit(solution)/shard_map/all_to_all | solution.py:207
  89.1 14.5 %collective-permute-start.11 = (bf16[8,2,4,2,16,128]{5,4,3,2,1,0:T(8,128)(2,1)}, bf16[8,2,4,2,16,128]{5,4,3,2,1,0:T(8,128)(2,1)S(1)}, u32[]{:S(2)}, u32[]{:S(2)}) collective-permute-start(bf16[8,2,4,2,16,128]{5,4,3,2,1,0:T(8,128)(2,1)} %copy-done.20), channel_id=1, source_target_pairs={{0,8},{8,16},{16,24},{24,0},{32,40},{40,48},{48,56},{56,32},{64,72... | collective-permute-start | bytes 1572872 | tf_op jit(solution)/shard_map/ppermute | solution.py:204
  90.4 25.7 %collective-permute-start.12 = (bf16[8,2,4,2,16,128]{5,4,3,2,1,0:T(8,128)(2,1)}, bf16[8,2,4,2,16,128]{5,4,3,2,1,0:T(8,128)(2,1)S(1)}, u32[]{:S(2)}, u32[]{:S(2)}) collective-permute-start(bf16[8,2,4,2,16,128]{5,4,3,2,1,0:T(8,128)(2,1)} %copy-done.19), channel_id=1, source_target_pairs={{0,16},{8,24},{16,0},{24,8},{32,48},{40,56},{48,32},{56,40},{64,80... | collective-permute-start | bytes 1572872 | tf_op jit(solution)/shard_map/ppermute | solution.py:204
  92.8 23.3 %collective-permute-start.13 = (bf16[8,2,4,2,16,128]{5,4,3,2,1,0:T(8,128)(2,1)}, bf16[8,2,4,2,16,128]{5,4,3,2,1,0:T(8,128)(2,1)S(1)}, u32[]{:S(2)}, u32[]{:S(2)}) collective-permute-start(bf16[8,2,4,2,16,128]{5,4,3,2,1,0:T(8,128)(2,1)} %copy-done.18), channel_id=1, source_target_pairs={{0,24},{8,0},{16,8},{24,16},{32,56},{40,32},{48,40},{56,48},{64,88... | collective-permute-start | bytes 1572872 | tf_op jit(solution)/shard_map/ppermute | solution.py:204
  116.1 20.6 %collective-permute-start.14 = (bf16[8,2,4,2,16,128]{5,4,3,2,1,0:T(8,128)(2,1)S(1)}, bf16[8,2,4,2,16,128]{5,4,3,2,1,0:T(8,128)(2,1)S(1)}, u32[]{:S(2)}, u32[]{:S(2)}) collective-permute-start(bf16[8,2,4,2,16,128]{5,4,3,2,1,0:T(8,128)(2,1)S(1)} %slice.7), channel_id=1, source_target_pairs={{32,0},{40,8},{48,16},{56,24},{64,32},{72,40},{80,48},{88,56},{96,... | collective-permute-start | bytes 1572872 | tf_op jit(solution)/shard_map/ppermute | solution.py:213
  119.1 0.7 copy-start.8
  119.8 14.8 %collective-permute-start.15 = (bf16[8,1,4,2,16,128]{5,4,3,2,1,0:T(8,128)(2,1)S(1)}, bf16[8,1,4,2,16,128]{5,4,3,2,1,0:T(8,128)(2,1)S(1)}, u32[]{:S(2)}, u32[]{:S(2)}) collective-permute-start(bf16[8,1,4,2,16,128]{5,4,3,2,1,0:T(8,128)(2,1)S(1)} %get-tuple-element.115), channel_id=1, source_target_pairs={{0,8},{8,16},{16,24},{24,0},{32,40},{40,48},{48,56},{56,32},{64,72... | collective-permute-start | bytes 786440 | tf_op jit(solution)/shard_map/ppermute | solution.py:204
  121.1 14.2 %collective-permute-start.16 = (bf16[8,1,4,2,16,128]{5,4,3,2,1,0:T(8,128)(2,1)S(1)}, bf16[8,1,4,2,16,128]{5,4,3,2,1,0:T(8,128)(2,1)S(1)}, u32[]{:S(2)}, u32[]{:S(2)}) collective-permute-start(bf16[8,1,4,2,16,128]{5,4,3,2,1,0:T(8,128)(2,1)S(1)} %get-tuple-element.116), channel_id=1, source_target_pairs={{0,16},{8,24},{16,0},{24,8},{32,48},{40,56},{48,32},{56,40},{64,80... | collective-permute-start | bytes 786440 | tf_op jit(solution)/shard_map/ppermute | solution.py:204
  124.2 11.8 %collective-permute-start.17 = (bf16[8,1,4,2,16,128]{5,4,3,2,1,0:T(8,128)(2,1)S(1)}, bf16[8,1,4,2,16,128]{5,4,3,2,1,0:T(8,128)(2,1)S(1)}, u32[]{:S(2)}, u32[]{:S(2)}) collective-permute-start(bf16[8,1,4,2,16,128]{5,4,3,2,1,0:T(8,128)(2,1)S(1)} %get-tuple-element.117), channel_id=1, source_target_pairs={{0,24},{8,0},{16,8},{24,16},{32,56},{40,32},{48,40},{56,48},{64,88... | collective-permute-start | bytes 786440 | tf_op jit(solution)/shard_map/ppermute | solution.py:204
  134.6 0.7 copy-start.10
  135.3 0.7 copy-start.12
  136.0 0.7 copy-start.14
  138.1 0.8 copy-start
  138.9 26.0 %copy-start.1 = (bf16[8,2,4,2,16,128]{5,4,3,2,1,0:T(8,128)(2,1)S(1)}, bf16[8,2,4,2,16,128]{5,4,3,2,1,0:T(8,128)(2,1)}, u32[]{:S(2)}) copy-start(bf16[8,2,4,2,16,128]{5,4,3,2,1,0:T(8,128)(2,1)} %copy-done) | copy-start | bytes 1572868
  138.9 13.6 %collective-permute-start.18 = (bf16[8,2,4,2,16,128]{5,4,3,2,1,0:T(8,128)(2,1)}, bf16[8,2,4,2,16,128]{5,4,3,2,1,0:T(8,128)(2,1)S(1)}, u32[]{:S(2)}, u32[]{:S(2)}) collective-permute-start(bf16[8,2,4,2,16,128]{5,4,3,2,1,0:T(8,128)(2,1)} %get-tuple-element.124), channel_id=1, source_target_pairs={{0,8},{8,16},{16,24},{24,0},{32,40},{40,48},{48,56},{56,32},{64,72... | collective-permute-start | bytes 1572872 | tf_op jit(solution)/shard_map/ppermute | solution.py:204
  138.9 26.0 %collective-permute-start.19 = (bf16[8,2,4,2,16,128]{5,4,3,2,1,0:T(8,128)(2,1)}, bf16[8,2,4,2,16,128]{5,4,3,2,1,0:T(8,128)(2,1)}, u32[]{:S(2)}, u32[]{:S(2)}) collective-permute-start(bf16[8,2,4,2,16,128]{5,4,3,2,1,0:T(8,128)(2,1)} %get-tuple-element.125), channel_id=1, source_target_pairs={{0,16},{8,24},{16,0},{24,8},{32,48},{40,56},{48,32},{56,40},{64,80... | collective-permute-start | bytes 1572872 | tf_op jit(solution)/shard_map/ppermute | solution.py:204
  141.9 23.0 %collective-permute-start.20 = (bf16[8,2,4,2,16,128]{5,4,3,2,1,0:T(8,128)(2,1)}, bf16[8,2,4,2,16,128]{5,4,3,2,1,0:T(8,128)(2,1)}, u32[]{:S(2)}, u32[]{:S(2)}) collective-permute-start(bf16[8,2,4,2,16,128]{5,4,3,2,1,0:T(8,128)(2,1)} %get-tuple-element.126), channel_id=1, source_target_pairs={{0,24},{8,0},{16,8},{24,16},{32,56},{40,32},{48,40},{56,48},{64,88... | collective-permute-start | bytes 1572872 | tf_op jit(solution)/shard_map/ppermute | solution.py:204
  142.1 1.0 copy-start.3
  143.1 0.9 copy-start.5
  144.0 0.9 copy-start.7
  145.0 19.9 %copy-start.9 = (bf16[8,1,4,2,16,128]{5,4,3,2,1,0:T(8,128)(2,1)S(1)}, bf16[8,1,4,2,16,128]{5,4,3,2,1,0:T(8,128)(2,1)}, u32[]{:S(2)}) copy-start(bf16[8,1,4,2,16,128]{5,4,3,2,1,0:T(8,128)(2,1)} %copy-done.8) | copy-start | bytes 786436
  145.0 19.9 %copy-start.11 = (bf16[8,1,4,2,16,128]{5,4,3,2,1,0:T(8,128)(2,1)S(1)}, bf16[8,1,4,2,16,128]{5,4,3,2,1,0:T(8,128)(2,1)}, u32[]{:S(2)}) copy-start(bf16[8,1,4,2,16,128]{5,4,3,2,1,0:T(8,128)(2,1)} %copy-done.10) | copy-start | bytes 786436
  145.0 19.9 %copy-start.13 = (bf16[8,1,4,2,16,128]{5,4,3,2,1,0:T(8,128)(2,1)S(1)}, bf16[8,1,4,2,16,128]{5,4,3,2,1,0:T(8,128)(2,1)}, u32[]{:S(2)}) copy-start(bf16[8,1,4,2,16,128]{5,4,3,2,1,0:T(8,128)(2,1)} %copy-done.12) | copy-start | bytes 786436
  145.0 19.9 %copy-start.15 = (bf16[8,1,4,2,16,128]{5,4,3,2,1,0:T(8,128)(2,1)S(1)}, bf16[8,1,4,2,16,128]{5,4,3,2,1,0:T(8,128)(2,1)}, u32[]{:S(2)}) copy-start(bf16[8,1,4,2,16,128]{5,4,3,2,1,0:T(8,128)(2,1)} %copy-done.14) | copy-start | bytes 786436

commit v3 on v2

v3 whole, which is shorter than its diff:
```python
import functools
import math

import jax
import jax.numpy as jnp
import numpy as np
from jax import lax
from jax.experimental import pallas as pl
from jax.experimental.pallas import tpu as pltpu
from jax.sharding import PartitionSpec as P

WINLEN = 100
NBIN = 16
BLOCK = 128
WIN_DEV = 16
WINDOWS = 512
PAIRS = 9
NZ, NY, NC = 8, 4, 8
NF = 2
GROUP = 4
REACH = 12
COLS = 512


def dft_rows():
    t = np.arange(WINLEN)
    bins = np.arange(NBIN) + 4
    angle = 2.0 * np.pi * bins[:, None] * t[None, :] / WINLEN
    table = np.stack([np.cos(angle), -np.sin(angle)], axis=1) * math.sqrt(2.0 / WINLEN)
    high = table.astype(jnp.bfloat16)
    low = (table - high.astype(np.float64)).astype(jnp.bfloat16)
    parts = np.stack([high, low]).astype(np.float32).reshape(2, NC, NF, 2, WINLEN)
    parts = parts.transpose(2, 1, 0, 3, 4)
    rows = parts[:, :, :, :, None, :, None] * np.eye(WIN_DEV, dtype=np.float32)[:, None, :]
    return rows.reshape(NF, NC, 4 * WIN_DEV, WINLEN * WIN_DEV).astype(jnp.bfloat16)


def spectra_body(records, alive, lhs, store):
    x = records[...]
    signal = x.astype(jnp.float32)
    power = jnp.sum(signal * signal, axis=0) * (1.0 / WINLEN)
    scale = alive[...].astype(jnp.float32) / jnp.sqrt(power + 1e-05)
    x = x.reshape(WINLEN * WIN_DEV, COLS)
    y = jnp.dot(lhs, x, preferred_element_type=jnp.float32)
    for k in range(NC):
        at = 4 * WIN_DEV * k
        value = y[at : at + 2 * WIN_DEV] + y[at + 2 * WIN_DEV : at + 4 * WIN_DEV]
        for p in range(2):
            scaled = (value[p * WIN_DEV : (p + 1) * WIN_DEV] * scale).astype(jnp.bfloat16)
            for b in range(COLS // BLOCK):
                store(k, b, p, scaled[:, b * BLOCK : (b + 1) * BLOCK])


def spectra_kernel(records, alive, rows, out):
    def store(k, b, p, part):
        out[k, b, p] = part

    spectra_body(records, alive, rows[0].reshape(NC * 4 * WIN_DEV, WINLEN * WIN_DEV), store)


def spectra_of(f, records, alive, rows):
    channels = records.shape[2]
    blocks, per = channels // BLOCK, COLS // BLOCK
    return pl.pallas_call(
        spectra_kernel,
        grid=(channels // COLS,),
        in_specs=[
            pl.BlockSpec((WINLEN, WIN_DEV, COLS), lambda n: (0, 0, n)),
            pl.BlockSpec((1, COLS), lambda n: (0, n)),
            pl.BlockSpec((1,) + rows.shape[1:], lambda n: (f, 0, 0, 0)),
        ],
        out_specs=pl.BlockSpec((NC, per, 2, WIN_DEV, BLOCK), lambda n: (0, n, 0, 0, 0)),
        out_shape=jax.ShapeDtypeStruct((NC, blocks, 2, WIN_DEV, BLOCK), jnp.bfloat16),
        compiler_params=pltpu.CompilerParams(vmem_limit_bytes=60 << 20),
        name="spectra",
    )(records, alive, rows)


def spectra_apart_kernel(order, records, alive, *refs):
    rows, outs = refs[:NC], refs[NC:]

    def store(k, b, p, part):
        outs[k][b, p] = part

    spectra_body(records, alive, jnp.concatenate([r[0, 0] for r in rows], axis=0), store)


def spectra_apart(f, records, alive, rows, order):
    channels = records.shape[2]
    blocks, per = channels // BLOCK, COLS // BLOCK
    grid_spec = pltpu.PrefetchScalarGridSpec(
        num_scalar_prefetch=1,
        grid=(channels // COLS,),
        in_specs=[
            pl.BlockSpec((WINLEN, WIN_DEV, COLS), lambda n, o: (0, 0, n)),
            pl.BlockSpec((1, COLS), lambda n, o: (0, n)),
        ]
        + [pl.BlockSpec((1, 1) + rows.shape[2:], lambda n, o, k=k: (f, o[k], 0, 0)) for k in range(NC)],
        out_specs=[pl.BlockSpec((per, 2, WIN_DEV, BLOCK), lambda n, o: (n, 0, 0, 0))] * NC,
    )
    return pl.pallas_call(
        spectra_apart_kernel,
        grid_spec=grid_spec,
        out_shape=[jax.ShapeDtypeStruct((blocks, 2, WIN_DEV, BLOCK), jnp.bfloat16)] * NC,
        compiler_params=pltpu.CompilerParams(vmem_limit_bytes=60 << 20),
        name="spectra",
    )(order, records, alive, *([rows] * NC))


def place_plane(out, plane, value):
    out[plane, :NY] = value
    out[lax.rem(plane + NZ - 1, NZ), NY:] = value[:2]


def widen_kernel(planes, out):
    for k in range(NZ):
        place_plane(out, k, planes[k])


def widen(planes):
    vmem = pl.BlockSpec(memory_space=pltpu.VMEM)
    return pl.pallas_call(
        widen_kernel,
        in_specs=[vmem],
        out_specs=vmem,
        out_shape=jax.ShapeDtypeStruct((NZ, NY + 2, GROUP, 2, WIN_DEV, BLOCK), jnp.bfloat16),
        compiler_params=pltpu.CompilerParams(vmem_limit_bytes=16 << 20),
        name="widen",
    )(planes.reshape(NZ, NY, GROUP, 2, WIN_DEV, BLOCK))


def arrange_kernel(order, *refs):
    for k in range(NC):
        refs[NC][order[k]] = refs[k][...]


def arrange(order, slots):
    vmem = pl.BlockSpec(memory_space=pltpu.VMEM)
    return pl.pallas_call(
        arrange_kernel,
        in_specs=[pl.BlockSpec(memory_space=pltpu.SMEM)] + [vmem] * NC,
        out_specs=vmem,
        out_shape=jax.ShapeDtypeStruct((NC,) + slots[0].shape, jnp.bfloat16),
        compiler_params=pltpu.CompilerParams(vmem_limit_bytes=16 << 20),
        name="arrange",
    )(order, *slots)


def pack_kernel(place, planes, *outs):
    for k in range(NY):
        outs[k][...] = planes[:, pl.ds(lax.rem(place[0] + k, NY), 3)]


def pack(place, planes):
    vmem = pl.BlockSpec(memory_space=pltpu.VMEM)
    shape = jax.ShapeDtypeStruct((NZ, 3, GROUP, 2, WIN_DEV, BLOCK), jnp.bfloat16)
    return pl.pallas_call(
        pack_kernel,
        in_specs=[pl.BlockSpec(memory_space=pltpu.SMEM), vmem],
        out_specs=[vmem] * NY,
        out_shape=[shape] * NY,
        compiler_params=pltpu.CompilerParams(vmem_limit_bytes=16 << 20),
        name="pack",
    )(place, planes)


def pack_group_kernel(first, place, planes, *refs):
    halo, outs = (None, refs) if first == 0 else (refs[0], refs[1:])
    for n, out in enumerate(outs):
        group = lax.rem(place[0] + n % NY, NY) + max(first, 0) + n // NY
        if first == 0:
            out[...] = planes[:, group]
        else:

            @pl.when(group < NY)
            def _():
                out[...] = planes[:, group]

            @pl.when(group >= NY)
            def _():
                out[...] = halo[:, group - NY]


def pack_groups(place, first, count, *sources):
    vmem = pl.BlockSpec(memory_space=pltpu.VMEM)
    shape = jax.ShapeDtypeStruct((NZ, GROUP, 2, WIN_DEV, BLOCK), jnp.bfloat16)
    return pl.pallas_call(
        functools.partial(pack_group_kernel, first),
        in_specs=[pl.BlockSpec(memory_space=pltpu.SMEM)] + [vmem] * len(sources),
        out_specs=[vmem] * (NY * count),
        out_shape=[shape] * (NY * count),
        compiler_params=pltpu.CompilerParams(vmem_limit_bytes=16 << 20),
        name="pack",
    )(place, *sources)


def real_and_imag(product):
    real = product[:BLOCK, :BLOCK] + product[BLOCK:, BLOCK:]
    imag = product[:BLOCK, BLOCK:] - product[BLOCK:, :BLOCK]
    inverse = 1.0 / math.sqrt(WINDOWS)
    return (real * inverse).astype(jnp.bfloat16), (imag * inverse).astype(jnp.bfloat16)


def fill(window, at, tiles, y, p):
    rows = NZ * WIN_DEV
    window[at, y * rows : (y + 1) * rows, p * BLOCK : (p + 1) * BLOCK] = tiles.reshape(rows, BLOCK)


def stack_kernel(held, relative, *refs):
    sources, out, window, own_t = refs[:-3], refs[-3], refs[-2], refs[-1]
    a = pl.program_id(0)

    @pl.when(a == 0)
    def _():
        for y in range(NY):
            for b in range(held):
                for p in range(2):
                    if sources[0].ndim == 6:
                        tiles = sources[y][:, b // GROUP, b % GROUP, p]
                    else:
                        tiles = sources[b // GROUP * NY + y][:, b % GROUP, p]
                    fill(window, b, tiles, y, p)

    own_t[...] = window[a].T
    for k in range(PAIRS):
        other = window[jnp.minimum(relative[a, k], held - 1)]
        product = jnp.dot(own_t[...], other, preferred_element_type=jnp.float32)
        out[0, k, 0, 0], out[0, k, 0, 1] = real_and_imag(product)


def stacks(relative, sources, f, held, earlier=None):
    shape = (GROUP, PAIRS, NF, 2, BLOCK, BLOCK)
    args = list(sources)
    specs = [pl.BlockSpec(memory_space=pltpu.VMEM)] * len(args)
    aliases = {}
    kernel = functools.partial(stack_kernel, held)
    if earlier is not None:
        aliases = {1 + len(args): 0}
        args.append(earlier)
        specs.append(pl.BlockSpec(memory_space=pl.ANY))

        def kernel(relative, *refs):
            stack_kernel(held, relative, *refs[:-4], *refs[-3:])

    grid_spec = pltpu.PrefetchScalarGridSpec(
        num_scalar_prefetch=1,
        grid=(GROUP,),
        in_specs=specs,
        out_specs=pl.BlockSpec((1, PAIRS, 1, 2, BLOCK, BLOCK), lambda a, r: (a, 0, f, 0, 0, 0)),
        scratch_shapes=[
            pltpu.VMEM((held, WINDOWS, 2 * BLOCK), jnp.bfloat16),
            pltpu.VMEM((2 * BLOCK, WINDOWS), jnp.bfloat16),
        ],
    )
    return pl.pallas_call(
        kernel,
        grid_spec=grid_spec,
        out_shape=jax.ShapeDtypeStruct(shape, jnp.bfloat16),
        input_output_aliases=aliases,
        compiler_params=pltpu.CompilerParams(vmem_limit_bytes=20 << 20),
        name="stacks",
    )(relative, *args)


def last_kernel(f, relative, *refs):
    near, last, out = refs[:NY], refs[NY : 2 * NY], refs[2 * NY + 1]
    window, own, staged, sems = refs[2 * NY + 2 :]
    for y in range(NY):
        for b in range(GROUP):
            for p in range(2):
                fill(own, b, near[y][:, b, p], y, p)
                fill(window, b, last[y][:, b, p], y, p)

    def each(step):
        for a in range(GROUP):
            for k in range(PAIRS):
                far = relative[a, k] - 2 * GROUP

                @pl.when(far >= 0)
                def _():
                    step(pltpu.make_async_copy(staged.at[a, far], out.at[a, k, f], sems.at[a, k]))

    for a in range(GROUP):
        own_t = own[a].T
        for b in range(a + 1):
            product = jnp.dot(own_t, window[b], preferred_element_type=jnp.float32)
            staged[a, b, 0], staged[a, b, 1] = real_and_imag(product)
    each(lambda copy: copy.start())
    each(lambda copy: copy.wait())


def last_stacks(relative, near, last, f, earlier):
    vmem = pl.BlockSpec(memory_space=pltpu.VMEM)
    blocks = pltpu.VMEM((GROUP, WINDOWS, 2 * BLOCK), jnp.bfloat16)
    return pl.pallas_call(
        functools.partial(last_kernel, f),
        in_specs=[pl.BlockSpec(memory_space=pltpu.SMEM)]
        + [vmem] * (2 * NY)
        + [pl.BlockSpec(memory_space=pl.ANY)],
        out_specs=pl.BlockSpec(memory_space=pl.ANY),
        out_shape=jax.ShapeDtypeStruct(earlier.shape, earlier.dtype),
        input_output_aliases={1 + 2 * NY: 0},
        scratch_shapes=[
            blocks,
            blocks,
            pltpu.VMEM((GROUP, GROUP, 2, BLOCK, BLOCK), jnp.bfloat16),
            pltpu.SemaphoreType.DMA((GROUP, PAIRS)),
        ],
        compiler_params=pltpu.CompilerParams(vmem_limit_bytes=20 << 20),
        name="last_stacks",
    )(relative, *near, *last, earlier)


def per_device(records, alive, partner):
    tm = lax.axis_index("tm")
    place = (tm % NY).reshape(1).astype(jnp.int32)
    relative = partner - tm * GROUP
    rows = jnp.asarray(dft_rows())
    records, alive = jnp.transpose(records, (1, 0, 2)), alive.reshape(1, -1)
    columns = [[z * NY + y for z in range(NZ)] for y in range(NY)]
    rounds = [[(i, i // NY * NY + (i + k) % NY) for i in range(NZ * NY)] for k in range(NY)]

    def along_y(packed):
        return [packed[0]] + [lax.ppermute(packed[k], "tm", rounds[k]) for k in range(1, NY)]

    def across_z(sent):
        return lax.all_to_all(
            sent, "tm", split_axis=0, concat_axis=0, tiled=True, axis_index_groups=columns
        )

    barrier = lax.optimization_barrier
    plain = jnp.arange(NC, dtype=jnp.int32)
    mixed = jnp.bitwise_xor(plain, lax.axis_index("chan").astype(jnp.int32))
    own0 = spectra_of(0, records, alive, rows)
    own1 = spectra_apart(1, records, alive, rows, mixed)
    sent0 = lax.all_to_all(own0, "chan", split_axis=0, concat_axis=0, tiled=True)
    sent0, own1 = barrier((sent0, own1))
    planes0 = across_z(widen(sent0))
    slots1 = [own1[0]]
    for k in range(1, NC):
        slots1.append(lax.ppermute(own1[k], "chan", [(c, c ^ k) for c in range(NC)]))
    planes0, sent1 = barrier((planes0, arrange(mixed, slots1)))
    found0 = along_y(pack(place, planes0))
    planes1 = across_z(sent1).reshape(NZ, NY, GROUP, 2, WIN_DEV, BLOCK)
    down = [(i, i - NY) for i in range(NY, NZ * NY)]
    halo1 = lax.ppermute(planes1[:, :2], "tm", down)
    near1 = along_y(pack_groups(place, 0, 1, planes1))
    halo1, found0 = barrier((halo1, found0))
    next1 = along_y(pack_groups(place, 1, 1, planes1, halo1))
    result = stacks(relative, found0, 0, REACH)
    last1 = along_y(pack_groups(place, 2, 1, planes1, halo1))
    result = stacks(relative, near1 + next1, 1, 2 * GROUP, result)
    return last_stacks(relative, near1, last1, 1, result)


def solution(mesh):
    return jax.shard_map(
        per_device,
        mesh=mesh,
        in_specs=(P("tm", None, "chan"), P("chan"), P("tm", None)),
        out_specs=P("tm", None, "chan", None, None, None),
        check_vma=False,
    )
```

time: 172 us -> 161 us (0.936)
  waiting for transfers between devices: 79.5 us -> 66.3 us
  local copies, waits for them, and re-layouts: 8.78 us -> 4.93 us
  Pallas kernels: 32.3 us -> 35.8 us
  starting transfers between devices: 50.1 us -> 52.1 us
    ppermute x12, waiting for transfers between devices: 50 us -> 9.28 us  [along_y(): lax.ppermute(packed[k], 'tm', rounds[k])]
    all_to_all x2, waiting for transfers between devices: 6.75 us -> 37 us  [across_z(): lax.all_to_all(sent, 'tm', split_axis=0, concat_axis=0, tiled=True, axis_...]
    pallas_call x8 -> x10, Pallas kernels: 30.7 us -> 35.2 us  [the longest x2 11.8 us: stacks(): pl.pallas_call(kernel, grid_spec=grid_spec, out_shape=jax.ShapeDtypeStruc...]
    ppermute x12, starting transfers between devices: 19.7 us -> 22.9 us  [along_y(): lax.ppermute(packed[k], 'tm', rounds[k])]
    ppermute x2 -> x1, starting transfers between devices: 6.26 us -> 3.4 us  [per_device(): halo1 = lax.ppermute(planes1[:, :2], 'tm', down)]
    unnamed x44 -> x30, local copies, waits for them, and re-layouts: 7.41 us -> 4.9 us
    ppermute x2 -> x1, waiting for transfers between devices: 3.18 us -> 1.04 us  [per_device(): halo1 = lax.ppermute(planes1[:, :2], 'tm', down)]
  transfers between devices with their start and end apart: 24 -> 23, of which waited for: 15 -> 13; matrix products, arithmetic and copies ran while one was open for 0% -> 0% of each run, Pallas kernels for 9% -> 15%
where the time goes in v3:
time: 161 us; the launch traced here: 160 us
  waiting for transfers between devices  66.3 us (41%)
  starting transfers between devices  52.1 us (32%)
  Pallas kernels  35.8 us (22%)
  local copies, waits for them, and re-layouts  4.93 us (3%)
    all_to_all x2, waiting for transfers between devices, across_z(): lax.all_to_all(sent, 'tm', split_axis=0, concat_axis=0, tiled=True, axis_...  37 us
    ppermute x12, starting transfers between devices, along_y(): lax.ppermute(packed[k], 'tm', rounds[k])  22.9 us
    all_to_all x2, starting transfers between devices, across_z(): lax.all_to_all(sent, 'tm', split_axis=0, concat_axis=0, tiled=True, axis_...  13.5 us
    ppermute x7, waiting for transfers between devices, per_device(): lax.ppermute(own1[k], 'chan', [(c, c ^ k) for c in range(NC)])  12.1 us
    pallas_call x2, Pallas kernels, stacks(): pl.pallas_call(kernel, grid_spec=grid_spec, out_shape=jax.ShapeDtypeStruc...  11.8 us
    ppermute x12, waiting for transfers between devices, along_y(): lax.ppermute(packed[k], 'tm', rounds[k])  9.28 us
    pallas_call x1, Pallas kernels, spectra_apart(): pl.pallas_call(spectra_apart_kernel, grid_spec=grid_spec, out_shape=[jax....  8.44 us
    ppermute x7, starting transfers between devices, per_device(): lax.ppermute(own1[k], 'chan', [(c, c ^ k) for c in range(NC)])  7.97 us
  transfers between devices with their start and end apart: 23, of which 13 were waited for; matrix products, arithmetic and copies ran while one was open for 0% of the time, Pallas kernels for 15%

profile of v3, /device:TPU:32, one launch (start us, length us, event | category | flops | bytes accessed | tf_op | source)
XLA Modules:
  0.0 160.0 jit_solution(13885639371159583248)
XLA Ops:
  0.0 7.9 %spectra.2 = bf16[8,16,2,16,128]{4,3,2,1,0:T(8,128)(2,1)} custom-call(bf16[100,16,2048]{2,1,0:T(8,128)(2,1)} %bitcast.10, s32[1,2048]{1,0:T(1,128)} %bitcast.12, bf16[2,8,64,1600]{3,2,1,0:T(8,128)(2,1)} %constant.24.clone.rows.refs_0_.refs_1_.refs_2_.refs_3_.refs_4_.refs_5_.refs_6_.refs_7_), custom_call_target="tpu_custom_call" | custom-call | tf_op jit(solution)/shard_map/spectra/pallas_call | solution.py:64
  7.9 4.3 %all-to-all-start = ((bf16[8,16,2,16,128]{4,3,2,1,0:T(8,128)(2,1)}), bf16[8,16,2,16,128]{4,3,2,1,0:T(8,128)(2,1)S(1)}, u32[]{:S(2)}, u32[]{:S(2)}) async-start(bf16[8,16,2,16,128]{4,3,2,1,0:T(8,128)(2,1)} %spectra.2), calls=%async_computation | async-start | bytes 2097152 | tf_op jit(solution)/shard_map/all_to_all | solution.py:336
  12.2 0.6 iota_xor_fusion.order
  12.8 8.4 %spectra.3 = (bf16[16,2,16,128]{3,2,1,0:T(8,128)(2,1)}, bf16[16,2,16,128]{3,2,1,0:T(8,128)(2,1)}, bf16[16,2,16,128]{3,2,1,0:T(8,128)(2,1)}, bf16[16,2,16,128]{3,...) custom-call(s32[8]{0:T(128)} %iota_xor_fusion.order, ...), custom_call_target="tpu_custom_call" | custom-call | tf_op jit(solution)/shard_map/spectra/pallas_call | solution.py:101
  21.4 6.8 %all-to-all-done = bf16[8,16,2,16,128]{4,3,2,1,0:T(8,128)(2,1)S(1)} async-done(((bf16[8,16,2,16,128]{4,3,2,1,0:T(8,128)(2,1)}), bf16[8,16,2,16,128]{4,3,2,1,0:T(8,128)(2,1)S(1)}, u32[]{:S(2)}, u32[]{:S(2)}) %all-to-all-start) | async-done | bytes 1048608 | tf_op jit(solution)/shard_map/all_to_all | solution.py:336
  28.2 0.2 widen.1
  28.4 1.1 copy-done
  29.5 8.6 %all-to-all-start.1 = ((bf16[8,6,4,2,16,128]{5,4,3,2,1,0:T(8,128)(2,1)}), bf16[8,6,4,2,16,128]{5,4,3,2,1,0:T(8,128)(2,1)S(1)}, u32[]{:S(2)}, u32[]{:S(2)}) async-start(bf16[8,6,4,2,16,128]{5,4,3,2,1,0:T(8,128)(2,1)} %copy-done), calls=%async_computation.1 | async-start | bytes 3145728 | tf_op jit(solution)/shard_map/all_to_all | solution.py:327
  38.1 0.7 collective-permute-start.1
  38.7 1.2 collective-permute-start.2
  40.0 1.0 collective-permute-start.3
  41.0 2.2 %collective-permute-start.4 = (bf16[16,2,16,128]{3,2,1,0:T(8,128)(2,1)S(1)}, bf16[16,2,16,128]{3,2,1,0:T(8,128)(2,1)S(1)}, u32[]{:S(2)}, u32[]{:S(2)}) collective-permute-start(bf16[16,2,16,128]{3,2,1,0:T(8,128)(2,1)S(1)} %copy-done.11), channel_id=1, source_target_pairs={{0,5},{1,4},{2,7},{3,6},{4,1},{5,0},{6,3},{7,2},{8,13},{9,12},{10,... | collective-permute-start | bytes 393224 | tf_op jit(solution)/shard_map/ppermute | solution.py:341
  43.2 1.2 collective-permute-start.5
  44.4 0.1 collective-permute-done.1.refs_2_
  44.5 1.7 %collective-permute-start.6 = (bf16[16,2,16,128]{3,2,1,0:T(8,128)(2,1)S(1)}, bf16[16,2,16,128]{3,2,1,0:T(8,128)(2,1)S(1)}, u32[]{:S(2)}, u32[]{:S(2)}) collective-permute-start(bf16[16,2,16,128]{3,2,1,0:T(8,128)(2,1)S(1)} %copy-done.9), channel_id=1, source_target_pairs={{0,7},{1,6},{2,5},{3,4},{4,3},{5,2},{6,1},{7,0},{8,15},{9,14},{10,... | collective-permute-start | bytes 393224 | tf_op jit(solution)/shard_map/ppermute | solution.py:341
  46.2 0.1 collective-permute-done.2.refs_3_
  46.3 4.5 %collective-permute-done.3.refs_4_ = bf16[16,2,16,128]{3,2,1,0:T(8,128)(2,1)S(1)} collective-permute-done((bf16[16,2,16,128]{3,2,1,0:T(8,128)(2,1)S(1)}, bf16[16,2,16,128]{3,2,1,0:T(8,128)(2,1)S(1)}, u32[]{:S(2)}, u32[]{:S(2)}) %collective-permute-start.3) | collective-permute-done | bytes 131104 | tf_op jit(solution)/shard_map/ppermute | solution.py:341
  50.8 1.9 %collective-permute-done.4.refs_5_ = bf16[16,2,16,128]{3,2,1,0:T(8,128)(2,1)S(1)} collective-permute-done((bf16[16,2,16,128]{3,2,1,0:T(8,128)(2,1)S(1)}, bf16[16,2,16,128]{3,2,1,0:T(8,128)(2,1)S(1)}, u32[]{:S(2)}, u32[]{:S(2)}) %collective-permute-start.4) | collective-permute-done | bytes 131104 | tf_op jit(solution)/shard_map/ppermute | solution.py:341
  52.7 3.2 %collective-permute-done.5.refs_6_ = bf16[16,2,16,128]{3,2,1,0:T(8,128)(2,1)S(1)} collective-permute-done((bf16[16,2,16,128]{3,2,1,0:T(8,128)(2,1)S(1)}, bf16[16,2,16,128]{3,2,1,0:T(8,128)(2,1)S(1)}, u32[]{:S(2)}, u32[]{:S(2)}) %collective-permute-start.5) | collective-permute-done | bytes 131104 | tf_op jit(solution)/shard_map/ppermute | solution.py:341
  55.9 2.2 %collective-permute-done.6.refs_7_ = bf16[16,2,16,128]{3,2,1,0:T(8,128)(2,1)S(1)} collective-permute-done((bf16[16,2,16,128]{3,2,1,0:T(8,128)(2,1)S(1)}, bf16[16,2,16,128]{3,2,1,0:T(8,128)(2,1)S(1)}, u32[]{:S(2)}, u32[]{:S(2)}) %collective-permute-start.6) | collective-permute-done | bytes 131104 | tf_op jit(solution)/shard_map/ppermute | solution.py:341
  58.1 0.6 arrange.1
  58.8 1.0 copy-done.1
  59.8 16.6 %all-to-all-done.1.planes = bf16[8,6,4,2,16,128]{5,4,3,2,1,0:T(8,128)(2,1)S(1)} async-done(((bf16[8,6,4,2,16,128]{5,4,3,2,1,0:T(8,128)(2,1)}), bf16[8,6,4,2,16,128]{5,4,3,2,1,0:T(8,128)(2,1)S(1)}, u32[]{:S(2)}, u32[]{:S(2)}) %all-to-all-start.1) | async-done | bytes 1572896 | tf_op jit(solution)/shard_map/all_to_all | solution.py:327
  76.4 4.9 %all-to-all-start.2 = ((bf16[8,16,2,16,128]{4,3,2,1,0:T(8,128)(2,1)}), bf16[8,16,2,16,128]{4,3,2,1,0:T(8,128)(2,1)S(1)}, u32[]{:S(2)}, u32[]{:S(2)}) async-start(bf16[8,16,2,16,128]{4,3,2,1,0:T(8,128)(2,1)} %copy-done.1), calls=%async_computation.2 | async-start | bytes 2097152 | tf_op jit(solution)/shard_map/all_to_all | solution.py:327
  81.3 1.5 pack.5
  82.9 1.6 collective-permute-start.11
  84.5 2.9 %collective-permute-start.12 = (bf16[8,3,4,2,16,128]{5,4,3,2,1,0:T(8,128)(2,1)}, bf16[8,3,4,2,16,128]{5,4,3,2,1,0:T(8,128)(2,1)}, u32[]{:S(2)}, u32[]{:S(2)}) collective-permute-start(bf16[8,3,4,2,16,128]{5,4,3,2,1,0:T(8,128)(2,1)} %get-tuple-element.70), channel_id=1, source_target_pairs={{0,16},{8,24},{16,0},{24,8},{32,48},{40,56},{48,32},{56,40},{64,80... | collective-permute-start | bytes 2359304 | tf_op jit(solution)/shard_map/ppermute | solution.py:324
  87.4 1.3 collective-permute-start.13
  88.7 20.4 %all-to-all-done.2 = bf16[8,16,2,16,128]{4,3,2,1,0:T(8,128)(2,1)S(1)} async-done(((bf16[8,16,2,16,128]{4,3,2,1,0:T(8,128)(2,1)}), bf16[8,16,2,16,128]{4,3,2,1,0:T(8,128)(2,1)S(1)}, u32[]{:S(2)}, u32[]{:S(2)}) %all-to-all-start.2) | async-done | bytes 1048608 | tf_op jit(solution)/shard_map/all_to_all | solution.py:327
  109.1 3.4 %collective-permute-start.10 = (bf16[8,2,4,2,16,128]{5,4,3,2,1,0:T(8,128)(2,1)S(1)}, bf16[8,2,4,2,16,128]{5,4,3,2,1,0:T(8,128)(2,1)S(1)}, u32[]{:S(2)}, u32[]{:S(2)}) collective-permute-start(bf16[8,2,4,2,16,128]{5,4,3,2,1,0:T(8,128)(2,1)S(1)} %slice.4), channel_id=1, source_target_pairs={{32,0},{40,8},{48,16},{56,24},{64,32},{72,40},{80,48},{88,56},{96,... | collective-permute-start | bytes 1572872 | tf_op jit(solution)/shard_map/ppermute | solution.py:346
  112.6 1.6 %collective-permute-start.7 = (bf16[8,4,2,16,128]{4,3,2,1,0:T(8,128)(2,1)S(1)}, bf16[8,4,2,16,128]{4,3,2,1,0:T(8,128)(2,1)S(1)}, u32[]{:S(2)}, u32[]{:S(2)}) collective-permute-start(bf16[8,4,2,16,128]{4,3,2,1,0:T(8,128)(2,1)S(1)} %get-tuple-element.64), channel_id=1, source_target_pairs={{0,8},{8,16},{16,24},{24,0},{32,40},{40,48},{48,56},{56,32},{64,72... | collective-permute-start | bytes 786440 | tf_op jit(solution)/shard_map/ppermute | solution.py:324
  114.3 0.9 copy-done.2
  115.2 6.8 %collective-permute-start.8 = (bf16[8,4,2,16,128]{4,3,2,1,0:T(8,128)(2,1)S(1)}, bf16[8,4,2,16,128]{4,3,2,1,0:T(8,128)(2,1)S(1)}, u32[]{:S(2)}, u32[]{:S(2)}) collective-permute-start(bf16[8,4,2,16,128]{4,3,2,1,0:T(8,128)(2,1)S(1)} %get-tuple-element.65), channel_id=1, source_target_pairs={{0,16},{8,24},{16,0},{24,8},{32,48},{40,56},{48,32},{56,40},{64,80... | collective-permute-start | bytes 786440 | tf_op jit(solution)/shard_map/ppermute | solution.py:324
  122.0 1.0 collective-permute-done.12.refs_2_
  123.0 1.0 collective-permute-done.10.refs_0_
  124.0 0.9 pack.7
  125.0 1.6 collective-permute-start.17
  126.5 1.2 pack.6
  127.7 2.9 %collective-permute-start.18 = (bf16[8,4,2,16,128]{4,3,2,1,0:T(8,128)(2,1)}, bf16[8,4,2,16,128]{4,3,2,1,0:T(8,128)(2,1)S(1)}, u32[]{:S(2)}, u32[]{:S(2)}) collective-permute-start(bf16[8,4,2,16,128]{4,3,2,1,0:T(8,128)(2,1)} %get-tuple-element.79), channel_id=1, source_target_pairs={{0,16},{8,24},{16,0},{24,8},{32,48},{40,56},{48,32},{56,40},{64,80... | collective-permute-start | bytes 786440 | tf_op jit(solution)/shard_map/ppermute | solution.py:324
  130.6 1.4 collective-permute-start.19
  132.0 2.2 %collective-permute-done.8.refs_2_ = bf16[8,4,2,16,128]{4,3,2,1,0:T(8,128)(2,1)S(1)} collective-permute-done((bf16[8,4,2,16,128]{4,3,2,1,0:T(8,128)(2,1)S(1)}, bf16[8,4,2,16,128]{4,3,2,1,0:T(8,128)(2,1)S(1)}, u32[]{:S(2)}, u32[]{:S(2)}) %collective-permute-start.8) | collective-permute-done | bytes 262176 | tf_op jit(solution)/shard_map/ppermute | solution.py:324
  134.2 2.8 %collective-permute-start.15 = (bf16[8,4,2,16,128]{4,3,2,1,0:T(8,128)(2,1)}, bf16[8,4,2,16,128]{4,3,2,1,0:T(8,128)(2,1)S(1)}, u32[]{:S(2)}, u32[]{:S(2)}) collective-permute-start(bf16[8,4,2,16,128]{4,3,2,1,0:T(8,128)(2,1)} %get-tuple-element.75), channel_id=1, source_target_pairs={{0,16},{8,24},{16,0},{24,8},{32,48},{40,56},{48,32},{56,40},{64,80... | collective-permute-start | bytes 786440 | tf_op jit(solution)/shard_map/ppermute | solution.py:324
  137.0 6.1 %collective-permute-done.17.refs_5_ = bf16[8,4,2,16,128]{4,3,2,1,0:T(8,128)(2,1)S(1)} collective-permute-done((bf16[8,4,2,16,128]{4,3,2,1,0:T(8,128)(2,1)S(1)}, bf16[8,4,2,16,128]{4,3,2,1,0:T(8,128)(2,1)S(1)}, u32[]{:S(2)}, u32[]{:S(2)}) %collective-permute-start.17) | collective-permute-done | bytes 262176 | tf_op jit(solution)/shard_map/ppermute | solution.py:324
  143.1 0.7 copy-done.4
  143.8 1.1 copy-done.3
  144.9 6.7 %stacks.2.refs_8_ = bf16[4,9,2,2,128,128]{5,4,3,2,1,0:T(8,128)(2,1)} custom-call(s32[4,9]{1,0:T(4,128)S(1)} %broadcast_subtract_fusion.relative, bf16[8,3,4,2,16,128]{5,4,3,2,1,0:T(8,128)(2,1)S(1)} %get-tuple-element.81.refs_0_, bf16[8,3,4,2,16,128]{5,4,3,2,1,0:T(8,128)(2,1)S(1)} %copy-done.3, ...), custom_call_target="tpu_custom_call" | custom-call | tf_op jit(solution)/shard_map/stacks/pallas_call | solution.py:255
  151.6 5.1 %stacks.3.refs_8_ = bf16[4,9,2,2,128,128]{5,4,3,2,1,0:T(8,128)(2,1)} custom-call(s32[4,9]{1,0:T(4,128)S(1)} %broadcast_subtract_fusion.relative, bf16[8,4,2,16,128]{4,3,2,1,0:T(8,128)(2,1)S(1)} %get-tuple-element.63.refs_0_, bf16[8,4,2,16,128]{4,3,2,1,0:T(8,128)(2,1)S(1)} %collective-permute-done.7.refs_1_, ...), custom_call_target="tpu_custom_call", output_to_operand_aliasing={{}: (9, {})} | custom-call | tf_op jit(solution)/shard_map/stacks/pallas_call | solution.py:255
  156.7 3.1 %last_stacks.1 = bf16[4,9,2,2,128,128]{5,4,3,2,1,0:T(8,128)(2,1)} custom-call(s32[4,9]{1,0:T(4,128)S(1)} %broadcast_subtract_fusion.relative, bf16[8,4,2,16,128]{4,3,2,1,0:T(8,128)(2,1)S(1)} %get-tuple-element.63.refs_0_, bf16[8,4,2,16,128]{4,3,2,1,0:T(8,128)(2,1)S(1)} %collective-permute-done.7.refs_1_, ...), custom_call_target="tpu_custom_call", output_to_operand_aliasing={{}: (9, {})} | custom-call | tf_op jit(solution)/shard_map/last_stacks/pallas_call | solution.py:295
  (42 shorter events, 0.2 us)
Async XLA Ops:
  7.9 20.3 %all-to-all-start = ((bf16[8,16,2,16,128]{4,3,2,1,0:T(8,128)(2,1)}), bf16[8,16,2,16,128]{4,3,2,1,0:T(8,128)(2,1)S(1)}, u32[]{:S(2)}, u32[]{:S(2)}) async-start(bf16[8,16,2,16,128]{4,3,2,1,0:T(8,128)(2,1)} %spectra.2), calls=%async_computation | async-start | bytes 2097152 | tf_op jit(solution)/shard_map/all_to_all | solution.py:336
  21.3 16.8 %copy-start.14 = (bf16[16,2,16,128]{3,2,1,0:T(8,128)(2,1)S(1)}, bf16[16,2,16,128]{3,2,1,0:T(8,128)(2,1)}, u32[]{:S(2)}) copy-start(bf16[16,2,16,128]{3,2,1,0:T(8,128)(2,1)} %get-tuple-element.56) | copy-start | bytes 393220
  21.3 17.5 %copy-start.13 = (bf16[16,2,16,128]{3,2,1,0:T(8,128)(2,1)S(1)}, bf16[16,2,16,128]{3,2,1,0:T(8,128)(2,1)}, u32[]{:S(2)}) copy-start(bf16[16,2,16,128]{3,2,1,0:T(8,128)(2,1)} %get-tuple-element.57) | copy-start | bytes 393220
  21.3 18.7 %copy-start.12 = (bf16[16,2,16,128]{3,2,1,0:T(8,128)(2,1)S(1)}, bf16[16,2,16,128]{3,2,1,0:T(8,128)(2,1)}, u32[]{:S(2)}) copy-start(bf16[16,2,16,128]{3,2,1,0:T(8,128)(2,1)} %get-tuple-element.58) | copy-start | bytes 393220
  21.3 19.7 %copy-start.11 = (bf16[16,2,16,128]{3,2,1,0:T(8,128)(2,1)S(1)}, bf16[16,2,16,128]{3,2,1,0:T(8,128)(2,1)}, u32[]{:S(2)}) copy-start(bf16[16,2,16,128]{3,2,1,0:T(8,128)(2,1)} %get-tuple-element.59) | copy-start | bytes 393220
  21.3 21.9 %copy-start.10 = (bf16[16,2,16,128]{3,2,1,0:T(8,128)(2,1)S(1)}, bf16[16,2,16,128]{3,2,1,0:T(8,128)(2,1)}, u32[]{:S(2)}) copy-start(bf16[16,2,16,128]{3,2,1,0:T(8,128)(2,1)} %get-tuple-element.60) | copy-start | bytes 393220
  21.3 23.2 %copy-start.9 = (bf16[16,2,16,128]{3,2,1,0:T(8,128)(2,1)S(1)}, bf16[16,2,16,128]{3,2,1,0:T(8,128)(2,1)}, u32[]{:S(2)}) copy-start(bf16[16,2,16,128]{3,2,1,0:T(8,128)(2,1)} %get-tuple-element.61) | copy-start | bytes 393220
  21.3 36.8 %copy-start.6 = (bf16[16,2,16,128]{3,2,1,0:T(8,128)(2,1)S(1)}, bf16[16,2,16,128]{3,2,1,0:T(8,128)(2,1)}, u32[]{:S(2)}) copy-start(bf16[16,2,16,128]{3,2,1,0:T(8,128)(2,1)} %get-tuple-element.54.refs_0_) | copy-start | bytes 393220
  21.3 36.8 %copy-start.7 = (s32[8]{0:T(128)S(1)}, s32[8]{0:T(128)}, u32[]{:S(2)}) copy-start(s32[8]{0:T(128)} %iota_xor_fusion.order) | copy-start | bytes 100
  28.4 1.1 copy-start
  29.5 46.9 %all-to-all-start.1 = ((bf16[8,6,4,2,16,128]{5,4,3,2,1,0:T(8,128)(2,1)}), bf16[8,6,4,2,16,128]{5,4,3,2,1,0:T(8,128)(2,1)S(1)}, u32[]{:S(2)}, u32[]{:S(2)}) async-start(bf16[8,6,4,2,16,128]{5,4,3,2,1,0:T(8,128)(2,1)} %copy-done), calls=%async_computation.1 | async-start | bytes 3145728 | tf_op jit(solution)/shard_map/all_to_all | solution.py:327
  38.1 5.1 %collective-permute-start = (bf16[16,2,16,128]{3,2,1,0:T(8,128)(2,1)}, bf16[16,2,16,128]{3,2,1,0:T(8,128)(2,1)S(1)}, u32[]{:S(2)}, u32[]{:S(2)}) collective-permute-start(bf16[16,2,16,128]{3,2,1,0:T(8,128)(2,1)} %get-tuple-element.55), channel_id=1, source_target_pairs={{0,1},{1,0},{2,3},{3,2},{4,5},{5,4},{6,7},{7,6},{8,9},{9,8},{10,11... | collective-permute-start | bytes 393224 | tf_op jit(solution)/shard_map/ppermute | solution.py:341
  38.1 6.4 %collective-permute-start.1 = (bf16[16,2,16,128]{3,2,1,0:T(8,128)(2,1)S(1)}, bf16[16,2,16,128]{3,2,1,0:T(8,128)(2,1)S(1)}, u32[]{:S(2)}, u32[]{:S(2)}) collective-permute-start(bf16[16,2,16,128]{3,2,1,0:T(8,128)(2,1)S(1)} %copy-done.14), channel_id=1, source_target_pairs={{0,2},{1,3},{2,0},{3,1},{4,6},{5,7},{6,4},{7,5},{8,10},{9,11},{10,... | collective-permute-start | bytes 393224 | tf_op jit(solution)/shard_map/ppermute | solution.py:341
  38.7 7.6 %collective-permute-start.2 = (bf16[16,2,16,128]{3,2,1,0:T(8,128)(2,1)S(1)}, bf16[16,2,16,128]{3,2,1,0:T(8,128)(2,1)S(1)}, u32[]{:S(2)}, u32[]{:S(2)}) collective-permute-start(bf16[16,2,16,128]{3,2,1,0:T(8,128)(2,1)S(1)} %copy-done.13), channel_id=1, source_target_pairs={{0,3},{1,2},{2,1},{3,0},{4,7},{5,6},{6,5},{7,4},{8,11},{9,10},{10,... | collective-permute-start | bytes 393224 | tf_op jit(solution)/shard_map/ppermute | solution.py:341
  40.0 10.8 %collective-permute-start.3 = (bf16[16,2,16,128]{3,2,1,0:T(8,128)(2,1)S(1)}, bf16[16,2,16,128]{3,2,1,0:T(8,128)(2,1)S(1)}, u32[]{:S(2)}, u32[]{:S(2)}) collective-permute-start(bf16[16,2,16,128]{3,2,1,0:T(8,128)(2,1)S(1)} %copy-done.12), channel_id=1, source_target_pairs={{0,4},{1,5},{2,6},{3,7},{4,0},{5,1},{6,2},{7,3},{8,12},{9,13},{10,... | collective-permute-start | bytes 393224 | tf_op jit(solution)/shard_map/ppermute | solution.py:341
  41.0 11.7 %collective-permute-start.4 = (bf16[16,2,16,128]{3,2,1,0:T(8,128)(2,1)S(1)}, bf16[16,2,16,128]{3,2,1,0:T(8,128)(2,1)S(1)}, u32[]{:S(2)}, u32[]{:S(2)}) collective-permute-start(bf16[16,2,16,128]{3,2,1,0:T(8,128)(2,1)S(1)} %copy-done.11), channel_id=1, source_target_pairs={{0,5},{1,4},{2,7},{3,6},{4,1},{5,0},{6,3},{7,2},{8,13},{9,12},{10,... | collective-permute-start | bytes 393224 | tf_op jit(solution)/shard_map/ppermute | solution.py:341
  43.2 12.7 %collective-permute-start.5 = (bf16[16,2,16,128]{3,2,1,0:T(8,128)(2,1)S(1)}, bf16[16,2,16,128]{3,2,1,0:T(8,128)(2,1)S(1)}, u32[]{:S(2)}, u32[]{:S(2)}) collective-permute-start(bf16[16,2,16,128]{3,2,1,0:T(8,128)(2,1)S(1)} %copy-done.10), channel_id=1, source_target_pairs={{0,6},{1,7},{2,4},{3,5},{4,2},{5,3},{6,0},{7,1},{8,14},{9,15},{10,... | collective-permute-start | bytes 393224 | tf_op jit(solution)/shard_map/ppermute | solution.py:341
  44.5 13.7 %collective-permute-start.6 = (bf16[16,2,16,128]{3,2,1,0:T(8,128)(2,1)S(1)}, bf16[16,2,16,128]{3,2,1,0:T(8,128)(2,1)S(1)}, u32[]{:S(2)}, u32[]{:S(2)}) collective-permute-start(bf16[16,2,16,128]{3,2,1,0:T(8,128)(2,1)S(1)} %copy-done.9), channel_id=1, source_target_pairs={{0,7},{1,6},{2,5},{3,4},{4,3},{5,2},{6,1},{7,0},{8,15},{9,14},{10,... | collective-permute-start | bytes 393224 | tf_op jit(solution)/shard_map/ppermute | solution.py:341
  58.8 1.0 copy-start.1
  59.8 84.0 %copy-start.8 = (s32[4,9]{1,0:T(4,128)S(1)}, s32[4,9]{1,0:T(4,128)}, u32[]{:S(2)}) copy-start(s32[4,9]{1,0:T(4,128)} %param.6) | copy-start | bytes 436
  76.4 32.7 %all-to-all-start.2 = ((bf16[8,16,2,16,128]{4,3,2,1,0:T(8,128)(2,1)}), bf16[8,16,2,16,128]{4,3,2,1,0:T(8,128)(2,1)S(1)}, u32[]{:S(2)}, u32[]{:S(2)}) async-start(bf16[8,16,2,16,128]{4,3,2,1,0:T(8,128)(2,1)} %copy-done.1), calls=%async_computation.2 | async-start | bytes 2097152 | tf_op jit(solution)/shard_map/all_to_all | solution.py:327
  82.9 31.4 %collective-permute-start.11 = (bf16[8,3,4,2,16,128]{5,4,3,2,1,0:T(8,128)(2,1)}, bf16[8,3,4,2,16,128]{5,4,3,2,1,0:T(8,128)(2,1)S(1)}, u32[]{:S(2)}, u32[]{:S(2)}) collective-permute-start(bf16[8,3,4,2,16,128]{5,4,3,2,1,0:T(8,128)(2,1)} %get-tuple-element.69), channel_id=1, source_target_pairs={{0,8},{8,16},{16,24},{24,0},{32,40},{40,48},{48,56},{56,32},{64,72... | collective-permute-start | bytes 2359304 | tf_op jit(solution)/shard_map/ppermute | solution.py:324
  84.5 38.5 %collective-permute-start.12 = (bf16[8,3,4,2,16,128]{5,4,3,2,1,0:T(8,128)(2,1)}, bf16[8,3,4,2,16,128]{5,4,3,2,1,0:T(8,128)(2,1)}, u32[]{:S(2)}, u32[]{:S(2)}) collective-permute-start(bf16[8,3,4,2,16,128]{5,4,3,2,1,0:T(8,128)(2,1)} %get-tuple-element.70), channel_id=1, source_target_pairs={{0,16},{8,24},{16,0},{24,8},{32,48},{40,56},{48,32},{56,40},{64,80... | collective-permute-start | bytes 2359304 | tf_op jit(solution)/shard_map/ppermute | solution.py:324
  87.4 35.6 %collective-permute-start.13 = (bf16[8,3,4,2,16,128]{5,4,3,2,1,0:T(8,128)(2,1)}, bf16[8,3,4,2,16,128]{5,4,3,2,1,0:T(8,128)(2,1)}, u32[]{:S(2)}, u32[]{:S(2)}) collective-permute-start(bf16[8,3,4,2,16,128]{5,4,3,2,1,0:T(8,128)(2,1)} %get-tuple-element.71), channel_id=1, source_target_pairs={{0,24},{8,0},{16,8},{24,16},{32,56},{40,32},{48,40},{56,48},{64,88... | collective-permute-start | bytes 2359304 | tf_op jit(solution)/shard_map/ppermute | solution.py:324
  109.1 14.9 %collective-permute-start.10 = (bf16[8,2,4,2,16,128]{5,4,3,2,1,0:T(8,128)(2,1)S(1)}, bf16[8,2,4,2,16,128]{5,4,3,2,1,0:T(8,128)(2,1)S(1)}, u32[]{:S(2)}, u32[]{:S(2)}) collective-permute-start(bf16[8,2,4,2,16,128]{5,4,3,2,1,0:T(8,128)(2,1)S(1)} %slice.4), channel_id=1, source_target_pairs={{32,0},{40,8},{48,16},{56,24},{64,32},{72,40},{80,48},{88,56},{96,... | collective-permute-start | bytes 1572872 | tf_op jit(solution)/shard_map/ppermute | solution.py:346
  112.6 18.0 %collective-permute-start.7 = (bf16[8,4,2,16,128]{4,3,2,1,0:T(8,128)(2,1)S(1)}, bf16[8,4,2,16,128]{4,3,2,1,0:T(8,128)(2,1)S(1)}, u32[]{:S(2)}, u32[]{:S(2)}) collective-permute-start(bf16[8,4,2,16,128]{4,3,2,1,0:T(8,128)(2,1)S(1)} %get-tuple-element.64), channel_id=1, source_target_pairs={{0,8},{8,16},{16,24},{24,0},{32,40},{40,48},{48,56},{56,32},{64,72... | collective-permute-start | bytes 786440 | tf_op jit(solution)/shard_map/ppermute | solution.py:324
  114.3 0.9 copy-start.2
  115.2 19.0 %collective-permute-start.8 = (bf16[8,4,2,16,128]{4,3,2,1,0:T(8,128)(2,1)S(1)}, bf16[8,4,2,16,128]{4,3,2,1,0:T(8,128)(2,1)S(1)}, u32[]{:S(2)}, u32[]{:S(2)}) collective-permute-start(bf16[8,4,2,16,128]{4,3,2,1,0:T(8,128)(2,1)S(1)} %get-tuple-element.65), channel_id=1, source_target_pairs={{0,16},{8,24},{16,0},{24,8},{32,48},{40,56},{48,32},{56,40},{64,80... | collective-permute-start | bytes 786440 | tf_op jit(solution)/shard_map/ppermute | solution.py:324
  123.0 11.2 %collective-permute-start.9 = (bf16[8,4,2,16,128]{4,3,2,1,0:T(8,128)(2,1)S(1)}, bf16[8,4,2,16,128]{4,3,2,1,0:T(8,128)(2,1)S(1)}, u32[]{:S(2)}, u32[]{:S(2)}) collective-permute-start(bf16[8,4,2,16,128]{4,3,2,1,0:T(8,128)(2,1)S(1)} %get-tuple-element.66), channel_id=1, source_target_pairs={{0,24},{8,0},{16,8},{24,16},{32,56},{40,32},{48,40},{56,48},{64,88... | collective-permute-start | bytes 786440 | tf_op jit(solution)/shard_map/ppermute | solution.py:324
  125.0 18.1 %collective-permute-start.17 = (bf16[8,4,2,16,128]{4,3,2,1,0:T(8,128)(2,1)S(1)}, bf16[8,4,2,16,128]{4,3,2,1,0:T(8,128)(2,1)S(1)}, u32[]{:S(2)}, u32[]{:S(2)}) collective-permute-start(bf16[8,4,2,16,128]{4,3,2,1,0:T(8,128)(2,1)S(1)} %get-tuple-element.78), channel_id=1, source_target_pairs={{0,8},{8,16},{16,24},{24,0},{32,40},{40,48},{48,56},{56,32},{64,72... | collective-permute-start | bytes 786440 | tf_op jit(solution)/shard_map/ppermute | solution.py:324
  127.7 23.9 %collective-permute-start.18 = (bf16[8,4,2,16,128]{4,3,2,1,0:T(8,128)(2,1)}, bf16[8,4,2,16,128]{4,3,2,1,0:T(8,128)(2,1)S(1)}, u32[]{:S(2)}, u32[]{:S(2)}) collective-permute-start(bf16[8,4,2,16,128]{4,3,2,1,0:T(8,128)(2,1)} %get-tuple-element.79), channel_id=1, source_target_pairs={{0,16},{8,24},{16,0},{24,8},{32,48},{40,56},{48,32},{56,40},{64,80... | collective-permute-start | bytes 786440 | tf_op jit(solution)/shard_map/ppermute | solution.py:324
  130.6 21.0 %collective-permute-start.19 = (bf16[8,4,2,16,128]{4,3,2,1,0:T(8,128)(2,1)}, bf16[8,4,2,16,128]{4,3,2,1,0:T(8,128)(2,1)S(1)}, u32[]{:S(2)}, u32[]{:S(2)}) collective-permute-start(bf16[8,4,2,16,128]{4,3,2,1,0:T(8,128)(2,1)} %get-tuple-element.80), channel_id=1, source_target_pairs={{0,24},{8,0},{16,8},{24,16},{32,56},{40,32},{48,40},{56,48},{64,88... | collective-permute-start | bytes 786440 | tf_op jit(solution)/shard_map/ppermute | solution.py:324
  134.2 22.6 %collective-permute-start.14 = (bf16[8,4,2,16,128]{4,3,2,1,0:T(8,128)(2,1)}, bf16[8,4,2,16,128]{4,3,2,1,0:T(8,128)(2,1)S(1)}, u32[]{:S(2)}, u32[]{:S(2)}) collective-permute-start(bf16[8,4,2,16,128]{4,3,2,1,0:T(8,128)(2,1)} %get-tuple-element.74), channel_id=1, source_target_pairs={{0,8},{8,16},{16,24},{24,0},{32,40},{40,48},{48,56},{56,32},{64,72... | collective-permute-start | bytes 786440 | tf_op jit(solution)/shard_map/ppermute | solution.py:324
  134.2 22.6 %collective-permute-start.15 = (bf16[8,4,2,16,128]{4,3,2,1,0:T(8,128)(2,1)}, bf16[8,4,2,16,128]{4,3,2,1,0:T(8,128)(2,1)S(1)}, u32[]{:S(2)}, u32[]{:S(2)}) collective-permute-start(bf16[8,4,2,16,128]{4,3,2,1,0:T(8,128)(2,1)} %get-tuple-element.75), channel_id=1, source_target_pairs={{0,16},{8,24},{16,0},{24,8},{32,48},{40,56},{48,32},{56,40},{64,80... | collective-permute-start | bytes 786440 | tf_op jit(solution)/shard_map/ppermute | solution.py:324
  143.1 0.7 copy-start.4
  143.8 13.0 %collective-permute-start.16 = (bf16[8,4,2,16,128]{4,3,2,1,0:T(8,128)(2,1)}, bf16[8,4,2,16,128]{4,3,2,1,0:T(8,128)(2,1)}, u32[]{:S(2)}, u32[]{:S(2)}) collective-permute-start(bf16[8,4,2,16,128]{4,3,2,1,0:T(8,128)(2,1)} %get-tuple-element.76), channel_id=1, source_target_pairs={{0,24},{8,0},{16,8},{24,16},{32,56},{40,32},{48,40},{56,48},{64,88... | collective-permute-start | bytes 786440 | tf_op jit(solution)/shard_map/ppermute | solution.py:324
  143.8 1.1 copy-start.3
  144.9 6.7 %copy-start.5 = (bf16[8,4,2,16,128]{4,3,2,1,0:T(8,128)(2,1)S(1)}, bf16[8,4,2,16,128]{4,3,2,1,0:T(8,128)(2,1)}, u32[]{:S(2)}) copy-start(bf16[8,4,2,16,128]{4,3,2,1,0:T(8,128)(2,1)} %copy-done.4) | copy-start | bytes 786436

commit v4 on v3

--- a/solution.py
+++ b/solution.py
@@ -204,62 +204,6 @@
 def fill(window, at, tiles, y, p):
     rows = NZ * WIN_DEV
     window[at, y * rows : (y + 1) * rows, p * BLOCK : (p + 1) * BLOCK] = tiles.reshape(rows, BLOCK)
-
-
-def stack_kernel(held, relative, *refs):
-    sources, out, window, own_t = refs[:-3], refs[-3], refs[-2], refs[-1]
-    a = pl.program_id(0)
-
-    @pl.when(a == 0)
-    def _():
-        for y in range(NY):
-            for b in range(held):
-                for p in range(2):
-                    if sources[0].ndim == 6:
-                        tiles = sources[y][:, b // GROUP, b % GROUP, p]
-                    else:
-                        tiles = sources[b // GROUP * NY + y][:, b % GROUP, p]
-                    fill(window, b, tiles, y, p)
-
-    own_t[...] = window[a].T
-    for k in range(PAIRS):
-        other = window[jnp.minimum(relative[a, k], held - 1)]
-        product = jnp.dot(own_t[...], other, preferred_element_type=jnp.float32)
-        out[0, k, 0, 0], out[0, k, 0, 1] = real_and_imag(product)
-
-
-def stacks(relative, sources, f, held, earlier=None):
-    shape = (GROUP, PAIRS, NF, 2, BLOCK, BLOCK)
-    args = list(sources)
-    specs = [pl.BlockSpec(memory_space=pltpu.VMEM)] * len(args)
-    aliases = {}
-    kernel = functools.partial(stack_kernel, held)
-    if earlier is not None:
-        aliases = {1 + len(args): 0}
-        args.append(earlier)
-        specs.append(pl.BlockSpec(memory_space=pl.ANY))
-
-        def kernel(relative, *refs):
-            stack_kernel(held, relative, *refs[:-4], *refs[-3:])
-
-    grid_spec = pltpu.PrefetchScalarGridSpec(
-        num_scalar_prefetch=1,
-        grid=(GROUP,),
-        in_specs=specs,
-        out_specs=pl.BlockSpec((1, PAIRS, 1, 2, BLOCK, BLOCK), lambda a, r: (a, 0, f, 0, 0, 0)),
-        scratch_shapes=[
-            pltpu.VMEM((held, WINDOWS, 2 * BLOCK), jnp.bfloat16),
-            pltpu.VMEM((2 * BLOCK, WINDOWS), jnp.bfloat16),
-        ],
-    )
-    return pl.pallas_call(
-        kernel,
-        grid_spec=grid_spec,
-        out_shape=jax.ShapeDtypeStruct(shape, jnp.bfloat16),
-        input_output_aliases=aliases,
-        compiler_params=pltpu.CompilerParams(vmem_limit_bytes=20 << 20),
-        name="stacks",
-    )(relative, *args)
 
 
 def last_kernel(f, relative, *refs):
@@ -309,6 +253,66 @@
         compiler_params=pltpu.CompilerParams(vmem_limit_bytes=20 << 20),
         name="last_stacks",
     )(relative, *near, *last, earlier)
+
+
+def pairs_kernel(f, low, high, relative, *refs):
+    sources, out = refs[:-5], refs[-5]
+    window, staged, own_t, sems = refs[-4:]
+    for y in range(NY):
+        for b in range(high):
+            for p in range(2):
+                if sources[0].ndim == 6:
+                    tiles = sources[y][:, b // GROUP, b % GROUP, p]
+                else:
+                    tiles = sources[b // GROUP * NY + y][:, b % GROUP, p]
+                fill(window, b, tiles, y, p)
+
+    def each(a, step):
+        for k in range(PAIRS):
+            partner = relative[a, k]
+
+            @pl.when(jnp.logical_and(partner >= low, partner < high))
+            def _():
+                step(pltpu.make_async_copy(staged.at[a, partner - low], out.at[a, k, f], sems.at[a, k]))
+
+    for a in range(GROUP):
+        own_t[...] = window[a].T
+        for b in range(max(low, a), min(high, a + PAIRS)):
+            product = jnp.dot(own_t[...], window[b], preferred_element_type=jnp.float32)
+            staged[a, b - low, 0], staged[a, b - low, 1] = real_and_imag(product)
+        each(a, lambda copy: copy.start())
+    for a in range(GROUP):
+        each(a, lambda copy: copy.wait())
+
+
+def pairs(relative, sources, f, low, high, earlier=None):
+    vmem = pl.BlockSpec(memory_space=pltpu.VMEM)
+    args = list(sources)
+    specs = [vmem] * len(args)
+    aliases = {}
+    if earlier is not None:
+        aliases = {1 + len(args): 0}
+        args.append(earlier)
+        specs.append(pl.BlockSpec(memory_space=pl.ANY))
+
+    def kernel(relative, *refs):
+        pairs_kernel(f, low, high, relative, *refs[: len(sources)], *refs[len(args) :])
+
+    return pl.pallas_call(
+        kernel,
+        in_specs=[pl.BlockSpec(memory_space=pltpu.SMEM)] + specs,
+        out_specs=pl.BlockSpec(memory_space=pl.ANY),
+        out_shape=jax.ShapeDtypeStruct((GROUP, PAIRS, NF, 2, BLOCK, BLOCK), jnp.bfloat16),
+        input_output_aliases=aliases,
+        scratch_shapes=[
+            pltpu.VMEM((high, WINDOWS, 2 * BLOCK), jnp.bfloat16),
+            pltpu.VMEM((GROUP, high - low, 2, BLOCK, BLOCK), jnp.bfloat16),
+            pltpu.VMEM((2 * BLOCK, WINDOWS), jnp.bfloat16),
+            pltpu.SemaphoreType.DMA((GROUP, PAIRS)),
+        ],
+        compiler_params=pltpu.CompilerParams(vmem_limit_bytes=20 << 20),
+        name="pairs",
+    )(relative, *args)
 
 
 def per_device(records, alive, partner):
@@ -347,9 +351,9 @@
     near1 = along_y(pack_groups(place, 0, 1, planes1))
     halo1, found0 = barrier((halo1, found0))
     next1 = along_y(pack_groups(place, 1, 1, planes1, halo1))
-    result = stacks(relative, found0, 0, REACH)
+    result = pairs(relative, found0, 0, 0, REACH)
     last1 = along_y(pack_groups(place, 2, 1, planes1, halo1))
-    result = stacks(relative, near1 + next1, 1, 2 * GROUP, result)
+    result = pairs(relative, near1 + next1, 1, 0, 2 * GROUP, result)
     return last_stacks(relative, near1, last1, 1, result)
 
 

time: 161 us -> 160 us (level)
  Pallas kernels: 35.8 us -> 33 us
    pallas_call x2, Pallas kernels: 11.8 us -> 9.01 us  [pairs(): pl.pallas_call(kernel, in_specs=[pl.BlockSpec(memory_space=pltpu.SMEM)] +...]
  transfers between devices with their start and end apart: 23 -> 23, of which waited for: 13 -> 14; matrix products, arithmetic and copies ran while one was open for 0% -> 0% of each run, Pallas kernels for 15% -> 14%
where the time goes in v4:
time: 160 us; the launch traced here: 159 us
  waiting for transfers between devices  67.7 us (42%)
  starting transfers between devices  52.1 us (33%)
  Pallas kernels  33 us (21%)
  local copies, waits for them, and re-layouts  4.93 us (3%)
    all_to_all x2, waiting for transfers between devices, across_z(): lax.all_to_all(sent, 'tm', split_axis=0, concat_axis=0, tiled=True, axis_...  37 us
    ppermute x12, starting transfers between devices, along_y(): lax.ppermute(packed[k], 'tm', rounds[k])  22.9 us
    all_to_all x2, starting transfers between devices, across_z(): lax.all_to_all(sent, 'tm', split_axis=0, concat_axis=0, tiled=True, axis_...  13.5 us
    ppermute x7, waiting for transfers between devices, per_device(): lax.ppermute(own1[k], 'chan', [(c, c ^ k) for c in range(NC)])  12.1 us
    ppermute x12, waiting for transfers between devices, along_y(): lax.ppermute(packed[k], 'tm', rounds[k])  10.7 us
    pallas_call x2, Pallas kernels, pairs(): pl.pallas_call(kernel, in_specs=[pl.BlockSpec(memory_space=pltpu.SMEM)] +...  9.01 us
    pallas_call x1, Pallas kernels, spectra_apart(): pl.pallas_call(spectra_apart_kernel, grid_spec=grid_spec, out_shape=[jax....  8.44 us
    ppermute x7, starting transfers between devices, per_device(): lax.ppermute(own1[k], 'chan', [(c, c ^ k) for c in range(NC)])  7.97 us
  transfers between devices with their start and end apart: 23, of which 14 were waited for; matrix products, arithmetic and copies ran while one was open for 0% of the time, Pallas kernels for 14%

profile of v4, /device:TPU:32, one launch (start us, length us, event | category | flops | bytes accessed | tf_op | source)
XLA Modules:
  0.0 158.7 jit_solution(7687619598076913047)
XLA Ops:
  0.0 7.9 %spectra.2 = bf16[8,16,2,16,128]{4,3,2,1,0:T(8,128)(2,1)} custom-call(bf16[100,16,2048]{2,1,0:T(8,128)(2,1)} %bitcast.10, s32[1,2048]{1,0:T(1,128)} %bitcast.12, bf16[2,8,64,1600]{3,2,1,0:T(8,128)(2,1)} %constant.24.clone.rows.refs_0_.refs_1_.refs_2_.refs_3_.refs_4_.refs_5_.refs_6_.refs_7_), custom_call_target="tpu_custom_call" | custom-call | tf_op jit(solution)/shard_map/spectra/pallas_call | solution.py:64
  7.9 4.3 %all-to-all-start = ((bf16[8,16,2,16,128]{4,3,2,1,0:T(8,128)(2,1)}), bf16[8,16,2,16,128]{4,3,2,1,0:T(8,128)(2,1)S(1)}, u32[]{:S(2)}, u32[]{:S(2)}) async-start(bf16[8,16,2,16,128]{4,3,2,1,0:T(8,128)(2,1)} %spectra.2), calls=%async_computation | async-start | bytes 2097152 | tf_op jit(solution)/shard_map/all_to_all | solution.py:340
  12.2 0.6 iota_xor_fusion.order
  12.8 8.4 %spectra.3 = (bf16[16,2,16,128]{3,2,1,0:T(8,128)(2,1)}, bf16[16,2,16,128]{3,2,1,0:T(8,128)(2,1)}, bf16[16,2,16,128]{3,2,1,0:T(8,128)(2,1)}, bf16[16,2,16,128]{3,...) custom-call(s32[8]{0:T(128)} %iota_xor_fusion.order, ...), custom_call_target="tpu_custom_call" | custom-call | tf_op jit(solution)/shard_map/spectra/pallas_call | solution.py:101
  21.4 6.8 %all-to-all-done = bf16[8,16,2,16,128]{4,3,2,1,0:T(8,128)(2,1)S(1)} async-done(((bf16[8,16,2,16,128]{4,3,2,1,0:T(8,128)(2,1)}), bf16[8,16,2,16,128]{4,3,2,1,0:T(8,128)(2,1)S(1)}, u32[]{:S(2)}, u32[]{:S(2)}) %all-to-all-start) | async-done | bytes 1048608 | tf_op jit(solution)/shard_map/all_to_all | solution.py:340
  28.2 0.2 widen.1
  28.4 1.1 copy-done
  29.5 8.6 %all-to-all-start.1 = ((bf16[8,6,4,2,16,128]{5,4,3,2,1,0:T(8,128)(2,1)}), bf16[8,6,4,2,16,128]{5,4,3,2,1,0:T(8,128)(2,1)S(1)}, u32[]{:S(2)}, u32[]{:S(2)}) async-start(bf16[8,6,4,2,16,128]{5,4,3,2,1,0:T(8,128)(2,1)} %copy-done), calls=%async_computation.1 | async-start | bytes 3145728 | tf_op jit(solution)/shard_map/all_to_all | solution.py:331
  38.1 0.7 collective-permute-start.1
  38.7 1.2 collective-permute-start.2
  40.0 1.0 collective-permute-start.3
  41.0 2.2 %collective-permute-start.4 = (bf16[16,2,16,128]{3,2,1,0:T(8,128)(2,1)S(1)}, bf16[16,2,16,128]{3,2,1,0:T(8,128)(2,1)S(1)}, u32[]{:S(2)}, u32[]{:S(2)}) collective-permute-start(bf16[16,2,16,128]{3,2,1,0:T(8,128)(2,1)S(1)} %copy-done.11), channel_id=1, source_target_pairs={{0,5},{1,4},{2,7},{3,6},{4,1},{5,0},{6,3},{7,2},{8,13},{9,12},{10,... | collective-permute-start | bytes 393224 | tf_op jit(solution)/shard_map/ppermute | solution.py:345
  43.2 1.2 collective-permute-start.5
  44.5 1.7 %collective-permute-start.6 = (bf16[16,2,16,128]{3,2,1,0:T(8,128)(2,1)S(1)}, bf16[16,2,16,128]{3,2,1,0:T(8,128)(2,1)S(1)}, u32[]{:S(2)}, u32[]{:S(2)}) collective-permute-start(bf16[16,2,16,128]{3,2,1,0:T(8,128)(2,1)S(1)} %copy-done.9), channel_id=1, source_target_pairs={{0,7},{1,6},{2,5},{3,4},{4,3},{5,2},{6,1},{7,0},{8,15},{9,14},{10,... | collective-permute-start | bytes 393224 | tf_op jit(solution)/shard_map/ppermute | solution.py:345
  46.2 0.1 collective-permute-done.2.refs_3_
  46.3 4.5 %collective-permute-done.3.refs_4_ = bf16[16,2,16,128]{3,2,1,0:T(8,128)(2,1)S(1)} collective-permute-done((bf16[16,2,16,128]{3,2,1,0:T(8,128)(2,1)S(1)}, bf16[16,2,16,128]{3,2,1,0:T(8,128)(2,1)S(1)}, u32[]{:S(2)}, u32[]{:S(2)}) %collective-permute-start.3) | collective-permute-done | bytes 131104 | tf_op jit(solution)/shard_map/ppermute | solution.py:345
  50.8 1.9 %collective-permute-done.4.refs_5_ = bf16[16,2,16,128]{3,2,1,0:T(8,128)(2,1)S(1)} collective-permute-done((bf16[16,2,16,128]{3,2,1,0:T(8,128)(2,1)S(1)}, bf16[16,2,16,128]{3,2,1,0:T(8,128)(2,1)S(1)}, u32[]{:S(2)}, u32[]{:S(2)}) %collective-permute-start.4) | collective-permute-done | bytes 131104 | tf_op jit(solution)/shard_map/ppermute | solution.py:345
  52.7 3.2 %collective-permute-done.5.refs_6_ = bf16[16,2,16,128]{3,2,1,0:T(8,128)(2,1)S(1)} collective-permute-done((bf16[16,2,16,128]{3,2,1,0:T(8,128)(2,1)S(1)}, bf16[16,2,16,128]{3,2,1,0:T(8,128)(2,1)S(1)}, u32[]{:S(2)}, u32[]{:S(2)}) %collective-permute-start.5) | collective-permute-done | bytes 131104 | tf_op jit(solution)/shard_map/ppermute | solution.py:345
  55.9 2.2 %collective-permute-done.6.refs_7_ = bf16[16,2,16,128]{3,2,1,0:T(8,128)(2,1)S(1)} collective-permute-done((bf16[16,2,16,128]{3,2,1,0:T(8,128)(2,1)S(1)}, bf16[16,2,16,128]{3,2,1,0:T(8,128)(2,1)S(1)}, u32[]{:S(2)}, u32[]{:S(2)}) %collective-permute-start.6) | collective-permute-done | bytes 131104 | tf_op jit(solution)/shard_map/ppermute | solution.py:345
  58.1 0.6 arrange.1
  58.8 1.0 copy-done.1
  59.8 16.6 %all-to-all-done.1.planes = bf16[8,6,4,2,16,128]{5,4,3,2,1,0:T(8,128)(2,1)S(1)} async-done(((bf16[8,6,4,2,16,128]{5,4,3,2,1,0:T(8,128)(2,1)}), bf16[8,6,4,2,16,128]{5,4,3,2,1,0:T(8,128)(2,1)S(1)}, u32[]{:S(2)}, u32[]{:S(2)}) %all-to-all-start.1) | async-done | bytes 1572896 | tf_op jit(solution)/shard_map/all_to_all | solution.py:331
  76.4 4.9 %all-to-all-start.2 = ((bf16[8,16,2,16,128]{4,3,2,1,0:T(8,128)(2,1)}), bf16[8,16,2,16,128]{4,3,2,1,0:T(8,128)(2,1)S(1)}, u32[]{:S(2)}, u32[]{:S(2)}) async-start(bf16[8,16,2,16,128]{4,3,2,1,0:T(8,128)(2,1)} %copy-done.1), calls=%async_computation.2 | async-start | bytes 2097152 | tf_op jit(solution)/shard_map/all_to_all | solution.py:331
  81.3 1.5 pack.5
  82.9 1.6 collective-permute-start.11
  84.5 2.9 %collective-permute-start.12 = (bf16[8,3,4,2,16,128]{5,4,3,2,1,0:T(8,128)(2,1)}, bf16[8,3,4,2,16,128]{5,4,3,2,1,0:T(8,128)(2,1)}, u32[]{:S(2)}, u32[]{:S(2)}) collective-permute-start(bf16[8,3,4,2,16,128]{5,4,3,2,1,0:T(8,128)(2,1)} %get-tuple-element.70), channel_id=1, source_target_pairs={{0,16},{8,24},{16,0},{24,8},{32,48},{40,56},{48,32},{56,40},{64,80... | collective-permute-start | bytes 2359304 | tf_op jit(solution)/shard_map/ppermute | solution.py:328
  87.4 1.3 collective-permute-start.13
  88.7 20.4 %all-to-all-done.2 = bf16[8,16,2,16,128]{4,3,2,1,0:T(8,128)(2,1)S(1)} async-done(((bf16[8,16,2,16,128]{4,3,2,1,0:T(8,128)(2,1)}), bf16[8,16,2,16,128]{4,3,2,1,0:T(8,128)(2,1)S(1)}, u32[]{:S(2)}, u32[]{:S(2)}) %all-to-all-start.2) | async-done | bytes 1048608 | tf_op jit(solution)/shard_map/all_to_all | solution.py:331
  109.1 3.4 %collective-permute-start.10 = (bf16[8,2,4,2,16,128]{5,4,3,2,1,0:T(8,128)(2,1)S(1)}, bf16[8,2,4,2,16,128]{5,4,3,2,1,0:T(8,128)(2,1)S(1)}, u32[]{:S(2)}, u32[]{:S(2)}) collective-permute-start(bf16[8,2,4,2,16,128]{5,4,3,2,1,0:T(8,128)(2,1)S(1)} %slice.4), channel_id=1, source_target_pairs={{32,0},{40,8},{48,16},{56,24},{64,32},{72,40},{80,48},{88,56},{96,... | collective-permute-start | bytes 1572872 | tf_op jit(solution)/shard_map/ppermute | solution.py:350
  112.6 1.6 %collective-permute-start.7 = (bf16[8,4,2,16,128]{4,3,2,1,0:T(8,128)(2,1)S(1)}, bf16[8,4,2,16,128]{4,3,2,1,0:T(8,128)(2,1)S(1)}, u32[]{:S(2)}, u32[]{:S(2)}) collective-permute-start(bf16[8,4,2,16,128]{4,3,2,1,0:T(8,128)(2,1)S(1)} %get-tuple-element.64), channel_id=1, source_target_pairs={{0,8},{8,16},{16,24},{24,0},{32,40},{40,48},{48,56},{56,32},{64,72... | collective-permute-start | bytes 786440 | tf_op jit(solution)/shard_map/ppermute | solution.py:328
  114.3 0.9 copy-done.2
  115.2 6.8 %collective-permute-start.8 = (bf16[8,4,2,16,128]{4,3,2,1,0:T(8,128)(2,1)S(1)}, bf16[8,4,2,16,128]{4,3,2,1,0:T(8,128)(2,1)S(1)}, u32[]{:S(2)}, u32[]{:S(2)}) collective-permute-start(bf16[8,4,2,16,128]{4,3,2,1,0:T(8,128)(2,1)S(1)} %get-tuple-element.65), channel_id=1, source_target_pairs={{0,16},{8,24},{16,0},{24,8},{32,48},{40,56},{48,32},{56,40},{64,80... | collective-permute-start | bytes 786440 | tf_op jit(solution)/shard_map/ppermute | solution.py:328
  122.0 1.0 collective-permute-done.12.refs_2_
  123.0 1.0 collective-permute-done.10.refs_0_
  124.0 0.9 pack.7
  125.0 1.6 collective-permute-start.17
  126.5 1.2 pack.6
  127.7 2.9 %collective-permute-start.18 = (bf16[8,4,2,16,128]{4,3,2,1,0:T(8,128)(2,1)}, bf16[8,4,2,16,128]{4,3,2,1,0:T(8,128)(2,1)S(1)}, u32[]{:S(2)}, u32[]{:S(2)}) collective-permute-start(bf16[8,4,2,16,128]{4,3,2,1,0:T(8,128)(2,1)} %get-tuple-element.79), channel_id=1, source_target_pairs={{0,16},{8,24},{16,0},{24,8},{32,48},{40,56},{48,32},{56,40},{64,80... | collective-permute-start | bytes 786440 | tf_op jit(solution)/shard_map/ppermute | solution.py:328
  130.6 1.4 collective-permute-start.19
  132.0 2.2 %collective-permute-done.8.refs_2_ = bf16[8,4,2,16,128]{4,3,2,1,0:T(8,128)(2,1)S(1)} collective-permute-done((bf16[8,4,2,16,128]{4,3,2,1,0:T(8,128)(2,1)S(1)}, bf16[8,4,2,16,128]{4,3,2,1,0:T(8,128)(2,1)S(1)}, u32[]{:S(2)}, u32[]{:S(2)}) %collective-permute-start.8) | collective-permute-done | bytes 262176 | tf_op jit(solution)/shard_map/ppermute | solution.py:328
  134.2 2.8 %collective-permute-start.15 = (bf16[8,4,2,16,128]{4,3,2,1,0:T(8,128)(2,1)}, bf16[8,4,2,16,128]{4,3,2,1,0:T(8,128)(2,1)S(1)}, u32[]{:S(2)}, u32[]{:S(2)}) collective-permute-start(bf16[8,4,2,16,128]{4,3,2,1,0:T(8,128)(2,1)} %get-tuple-element.75), channel_id=1, source_target_pairs={{0,16},{8,24},{16,0},{24,8},{32,48},{40,56},{48,32},{56,40},{64,80... | collective-permute-start | bytes 786440 | tf_op jit(solution)/shard_map/ppermute | solution.py:328
  137.0 6.1 %collective-permute-done.17.refs_5_ = bf16[8,4,2,16,128]{4,3,2,1,0:T(8,128)(2,1)S(1)} collective-permute-done((bf16[8,4,2,16,128]{4,3,2,1,0:T(8,128)(2,1)S(1)}, bf16[8,4,2,16,128]{4,3,2,1,0:T(8,128)(2,1)S(1)}, u32[]{:S(2)}, u32[]{:S(2)}) %collective-permute-start.17) | collective-permute-done | bytes 262176 | tf_op jit(solution)/shard_map/ppermute | solution.py:328
  143.1 0.7 copy-done.4
  143.8 1.1 copy-done.3
  144.9 5.3 %pairs.2.refs_8_ = bf16[4,9,2,2,128,128]{5,4,3,2,1,0:T(8,128)(2,1)} custom-call(s32[4,9]{1,0:T(4,128)S(1)} %broadcast_subtract_fusion.relative, bf16[8,3,4,2,16,128]{5,4,3,2,1,0:T(8,128)(2,1)S(1)} %get-tuple-element.81.refs_0_, bf16[8,3,4,2,16,128]{5,4,3,2,1,0:T(8,128)(2,1)S(1)} %copy-done.3, ...), custom_call_target="tpu_custom_call" | custom-call | tf_op jit(solution)/shard_map/pairs/pallas_call | solution.py:301
  150.3 3.7 %pairs.3.refs_8_ = bf16[4,9,2,2,128,128]{5,4,3,2,1,0:T(8,128)(2,1)} custom-call(s32[4,9]{1,0:T(4,128)S(1)} %broadcast_subtract_fusion.relative, bf16[8,4,2,16,128]{4,3,2,1,0:T(8,128)(2,1)S(1)} %get-tuple-element.63.refs_0_, bf16[8,4,2,16,128]{4,3,2,1,0:T(8,128)(2,1)S(1)} %collective-permute-done.7.refs_1_, ...), custom_call_target="tpu_custom_call", output_to_operand_aliasing={{}: (9, {})} | custom-call | tf_op jit(solution)/shard_map/pairs/pallas_call | solution.py:301
  154.0 1.4 collective-permute-done.15.refs_6_
  155.4 3.1 %last_stacks.1 = bf16[4,9,2,2,128,128]{5,4,3,2,1,0:T(8,128)(2,1)} custom-call(s32[4,9]{1,0:T(4,128)S(1)} %broadcast_subtract_fusion.relative, bf16[8,4,2,16,128]{4,3,2,1,0:T(8,128)(2,1)S(1)} %get-tuple-element.63.refs_0_, bf16[8,4,2,16,128]{4,3,2,1,0:T(8,128)(2,1)S(1)} %collective-permute-done.7.refs_1_, ...), custom_call_target="tpu_custom_call", output_to_operand_aliasing={{}: (9, {})} | custom-call | tf_op jit(solution)/shard_map/last_stacks/pallas_call | solution.py:239
  (42 shorter events, 0.3 us)
Async XLA Ops:
  7.9 20.3 %all-to-all-start = ((bf16[8,16,2,16,128]{4,3,2,1,0:T(8,128)(2,1)}), bf16[8,16,2,16,128]{4,3,2,1,0:T(8,128)(2,1)S(1)}, u32[]{:S(2)}, u32[]{:S(2)}) async-start(bf16[8,16,2,16,128]{4,3,2,1,0:T(8,128)(2,1)} %spectra.2), calls=%async_computation | async-start | bytes 2097152 | tf_op jit(solution)/shard_map/all_to_all | solution.py:340
  21.3 16.8 %copy-start.14 = (bf16[16,2,16,128]{3,2,1,0:T(8,128)(2,1)S(1)}, bf16[16,2,16,128]{3,2,1,0:T(8,128)(2,1)}, u32[]{:S(2)}) copy-start(bf16[16,2,16,128]{3,2,1,0:T(8,128)(2,1)} %get-tuple-element.56) | copy-start | bytes 393220
  21.3 17.5 %copy-start.13 = (bf16[16,2,16,128]{3,2,1,0:T(8,128)(2,1)S(1)}, bf16[16,2,16,128]{3,2,1,0:T(8,128)(2,1)}, u32[]{:S(2)}) copy-start(bf16[16,2,16,128]{3,2,1,0:T(8,128)(2,1)} %get-tuple-element.57) | copy-start | bytes 393220
  21.3 18.7 %copy-start.12 = (bf16[16,2,16,128]{3,2,1,0:T(8,128)(2,1)S(1)}, bf16[16,2,16,128]{3,2,1,0:T(8,128)(2,1)}, u32[]{:S(2)}) copy-start(bf16[16,2,16,128]{3,2,1,0:T(8,128)(2,1)} %get-tuple-element.58) | copy-start | bytes 393220
  21.3 19.7 %copy-start.11 = (bf16[16,2,16,128]{3,2,1,0:T(8,128)(2,1)S(1)}, bf16[16,2,16,128]{3,2,1,0:T(8,128)(2,1)}, u32[]{:S(2)}) copy-start(bf16[16,2,16,128]{3,2,1,0:T(8,128)(2,1)} %get-tuple-element.59) | copy-start | bytes 393220
  21.3 21.9 %copy-start.10 = (bf16[16,2,16,128]{3,2,1,0:T(8,128)(2,1)S(1)}, bf16[16,2,16,128]{3,2,1,0:T(8,128)(2,1)}, u32[]{:S(2)}) copy-start(bf16[16,2,16,128]{3,2,1,0:T(8,128)(2,1)} %get-tuple-element.60) | copy-start | bytes 393220
  21.3 23.2 %copy-start.9 = (bf16[16,2,16,128]{3,2,1,0:T(8,128)(2,1)S(1)}, bf16[16,2,16,128]{3,2,1,0:T(8,128)(2,1)}, u32[]{:S(2)}) copy-start(bf16[16,2,16,128]{3,2,1,0:T(8,128)(2,1)} %get-tuple-element.61) | copy-start | bytes 393220
  21.3 36.8 %copy-start.6 = (bf16[16,2,16,128]{3,2,1,0:T(8,128)(2,1)S(1)}, bf16[16,2,16,128]{3,2,1,0:T(8,128)(2,1)}, u32[]{:S(2)}) copy-start(bf16[16,2,16,128]{3,2,1,0:T(8,128)(2,1)} %get-tuple-element.54.refs_0_) | copy-start | bytes 393220
  21.3 36.8 %copy-start.7 = (s32[8]{0:T(128)S(1)}, s32[8]{0:T(128)}, u32[]{:S(2)}) copy-start(s32[8]{0:T(128)} %iota_xor_fusion.order) | copy-start | bytes 100
  28.4 1.1 copy-start
  29.5 46.9 %all-to-all-start.1 = ((bf16[8,6,4,2,16,128]{5,4,3,2,1,0:T(8,128)(2,1)}), bf16[8,6,4,2,16,128]{5,4,3,2,1,0:T(8,128)(2,1)S(1)}, u32[]{:S(2)}, u32[]{:S(2)}) async-start(bf16[8,6,4,2,16,128]{5,4,3,2,1,0:T(8,128)(2,1)} %copy-done), calls=%async_computation.1 | async-start | bytes 3145728 | tf_op jit(solution)/shard_map/all_to_all | solution.py:331
  38.1 5.1 %collective-permute-start = (bf16[16,2,16,128]{3,2,1,0:T(8,128)(2,1)}, bf16[16,2,16,128]{3,2,1,0:T(8,128)(2,1)S(1)}, u32[]{:S(2)}, u32[]{:S(2)}) collective-permute-start(bf16[16,2,16,128]{3,2,1,0:T(8,128)(2,1)} %get-tuple-element.55), channel_id=1, source_target_pairs={{0,1},{1,0},{2,3},{3,2},{4,5},{5,4},{6,7},{7,6},{8,9},{9,8},{10,11... | collective-permute-start | bytes 393224 | tf_op jit(solution)/shard_map/ppermute | solution.py:345
  38.1 6.4 %collective-permute-start.1 = (bf16[16,2,16,128]{3,2,1,0:T(8,128)(2,1)S(1)}, bf16[16,2,16,128]{3,2,1,0:T(8,128)(2,1)S(1)}, u32[]{:S(2)}, u32[]{:S(2)}) collective-permute-start(bf16[16,2,16,128]{3,2,1,0:T(8,128)(2,1)S(1)} %copy-done.14), channel_id=1, source_target_pairs={{0,2},{1,3},{2,0},{3,1},{4,6},{5,7},{6,4},{7,5},{8,10},{9,11},{10,... | collective-permute-start | bytes 393224 | tf_op jit(solution)/shard_map/ppermute | solution.py:345
  38.7 7.6 %collective-permute-start.2 = (bf16[16,2,16,128]{3,2,1,0:T(8,128)(2,1)S(1)}, bf16[16,2,16,128]{3,2,1,0:T(8,128)(2,1)S(1)}, u32[]{:S(2)}, u32[]{:S(2)}) collective-permute-start(bf16[16,2,16,128]{3,2,1,0:T(8,128)(2,1)S(1)} %copy-done.13), channel_id=1, source_target_pairs={{0,3},{1,2},{2,1},{3,0},{4,7},{5,6},{6,5},{7,4},{8,11},{9,10},{10,... | collective-permute-start | bytes 393224 | tf_op jit(solution)/shard_map/ppermute | solution.py:345
  40.0 10.8 %collective-permute-start.3 = (bf16[16,2,16,128]{3,2,1,0:T(8,128)(2,1)S(1)}, bf16[16,2,16,128]{3,2,1,0:T(8,128)(2,1)S(1)}, u32[]{:S(2)}, u32[]{:S(2)}) collective-permute-start(bf16[16,2,16,128]{3,2,1,0:T(8,128)(2,1)S(1)} %copy-done.12), channel_id=1, source_target_pairs={{0,4},{1,5},{2,6},{3,7},{4,0},{5,1},{6,2},{7,3},{8,12},{9,13},{10,... | collective-permute-start | bytes 393224 | tf_op jit(solution)/shard_map/ppermute | solution.py:345
  41.0 11.7 %collective-permute-start.4 = (bf16[16,2,16,128]{3,2,1,0:T(8,128)(2,1)S(1)}, bf16[16,2,16,128]{3,2,1,0:T(8,128)(2,1)S(1)}, u32[]{:S(2)}, u32[]{:S(2)}) collective-permute-start(bf16[16,2,16,128]{3,2,1,0:T(8,128)(2,1)S(1)} %copy-done.11), channel_id=1, source_target_pairs={{0,5},{1,4},{2,7},{3,6},{4,1},{5,0},{6,3},{7,2},{8,13},{9,12},{10,... | collective-permute-start | bytes 393224 | tf_op jit(solution)/shard_map/ppermute | solution.py:345
  43.2 12.7 %collective-permute-start.5 = (bf16[16,2,16,128]{3,2,1,0:T(8,128)(2,1)S(1)}, bf16[16,2,16,128]{3,2,1,0:T(8,128)(2,1)S(1)}, u32[]{:S(2)}, u32[]{:S(2)}) collective-permute-start(bf16[16,2,16,128]{3,2,1,0:T(8,128)(2,1)S(1)} %copy-done.10), channel_id=1, source_target_pairs={{0,6},{1,7},{2,4},{3,5},{4,2},{5,3},{6,0},{7,1},{8,14},{9,15},{10,... | collective-permute-start | bytes 393224 | tf_op jit(solution)/shard_map/ppermute | solution.py:345
  44.5 13.7 %collective-permute-start.6 = (bf16[16,2,16,128]{3,2,1,0:T(8,128)(2,1)S(1)}, bf16[16,2,16,128]{3,2,1,0:T(8,128)(2,1)S(1)}, u32[]{:S(2)}, u32[]{:S(2)}) collective-permute-start(bf16[16,2,16,128]{3,2,1,0:T(8,128)(2,1)S(1)} %copy-done.9), channel_id=1, source_target_pairs={{0,7},{1,6},{2,5},{3,4},{4,3},{5,2},{6,1},{7,0},{8,15},{9,14},{10,... | collective-permute-start | bytes 393224 | tf_op jit(solution)/shard_map/ppermute | solution.py:345
  58.8 1.0 copy-start.1
  59.8 84.0 %copy-start.8 = (s32[4,9]{1,0:T(4,128)S(1)}, s32[4,9]{1,0:T(4,128)}, u32[]{:S(2)}) copy-start(s32[4,9]{1,0:T(4,128)} %param.6) | copy-start | bytes 436
  76.4 32.7 %all-to-all-start.2 = ((bf16[8,16,2,16,128]{4,3,2,1,0:T(8,128)(2,1)}), bf16[8,16,2,16,128]{4,3,2,1,0:T(8,128)(2,1)S(1)}, u32[]{:S(2)}, u32[]{:S(2)}) async-start(bf16[8,16,2,16,128]{4,3,2,1,0:T(8,128)(2,1)} %copy-done.1), calls=%async_computation.2 | async-start | bytes 2097152 | tf_op jit(solution)/shard_map/all_to_all | solution.py:331
  82.9 31.4 %collective-permute-start.11 = (bf16[8,3,4,2,16,128]{5,4,3,2,1,0:T(8,128)(2,1)}, bf16[8,3,4,2,16,128]{5,4,3,2,1,0:T(8,128)(2,1)S(1)}, u32[]{:S(2)}, u32[]{:S(2)}) collective-permute-start(bf16[8,3,4,2,16,128]{5,4,3,2,1,0:T(8,128)(2,1)} %get-tuple-element.69), channel_id=1, source_target_pairs={{0,8},{8,16},{16,24},{24,0},{32,40},{40,48},{48,56},{56,32},{64,72... | collective-permute-start | bytes 2359304 | tf_op jit(solution)/shard_map/ppermute | solution.py:328
  84.5 38.5 %collective-permute-start.12 = (bf16[8,3,4,2,16,128]{5,4,3,2,1,0:T(8,128)(2,1)}, bf16[8,3,4,2,16,128]{5,4,3,2,1,0:T(8,128)(2,1)}, u32[]{:S(2)}, u32[]{:S(2)}) collective-permute-start(bf16[8,3,4,2,16,128]{5,4,3,2,1,0:T(8,128)(2,1)} %get-tuple-element.70), channel_id=1, source_target_pairs={{0,16},{8,24},{16,0},{24,8},{32,48},{40,56},{48,32},{56,40},{64,80... | collective-permute-start | bytes 2359304 | tf_op jit(solution)/shard_map/ppermute | solution.py:328
  87.4 35.6 %collective-permute-start.13 = (bf16[8,3,4,2,16,128]{5,4,3,2,1,0:T(8,128)(2,1)}, bf16[8,3,4,2,16,128]{5,4,3,2,1,0:T(8,128)(2,1)}, u32[]{:S(2)}, u32[]{:S(2)}) collective-permute-start(bf16[8,3,4,2,16,128]{5,4,3,2,1,0:T(8,128)(2,1)} %get-tuple-element.71), channel_id=1, source_target_pairs={{0,24},{8,0},{16,8},{24,16},{32,56},{40,32},{48,40},{56,48},{64,88... | collective-permute-start | bytes 2359304 | tf_op jit(solution)/shard_map/ppermute | solution.py:328
  109.1 14.9 %collective-permute-start.10 = (bf16[8,2,4,2,16,128]{5,4,3,2,1,0:T(8,128)(2,1)S(1)}, bf16[8,2,4,2,16,128]{5,4,3,2,1,0:T(8,128)(2,1)S(1)}, u32[]{:S(2)}, u32[]{:S(2)}) collective-permute-start(bf16[8,2,4,2,16,128]{5,4,3,2,1,0:T(8,128)(2,1)S(1)} %slice.4), channel_id=1, source_target_pairs={{32,0},{40,8},{48,16},{56,24},{64,32},{72,40},{80,48},{88,56},{96,... | collective-permute-start | bytes 1572872 | tf_op jit(solution)/shard_map/ppermute | solution.py:350
  112.6 18.0 %collective-permute-start.7 = (bf16[8,4,2,16,128]{4,3,2,1,0:T(8,128)(2,1)S(1)}, bf16[8,4,2,16,128]{4,3,2,1,0:T(8,128)(2,1)S(1)}, u32[]{:S(2)}, u32[]{:S(2)}) collective-permute-start(bf16[8,4,2,16,128]{4,3,2,1,0:T(8,128)(2,1)S(1)} %get-tuple-element.64), channel_id=1, source_target_pairs={{0,8},{8,16},{16,24},{24,0},{32,40},{40,48},{48,56},{56,32},{64,72... | collective-permute-start | bytes 786440 | tf_op jit(solution)/shard_map/ppermute | solution.py:328
  114.3 0.9 copy-start.2
  115.2 19.0 %collective-permute-start.8 = (bf16[8,4,2,16,128]{4,3,2,1,0:T(8,128)(2,1)S(1)}, bf16[8,4,2,16,128]{4,3,2,1,0:T(8,128)(2,1)S(1)}, u32[]{:S(2)}, u32[]{:S(2)}) collective-permute-start(bf16[8,4,2,16,128]{4,3,2,1,0:T(8,128)(2,1)S(1)} %get-tuple-element.65), channel_id=1, source_target_pairs={{0,16},{8,24},{16,0},{24,8},{32,48},{40,56},{48,32},{56,40},{64,80... | collective-permute-start | bytes 786440 | tf_op jit(solution)/shard_map/ppermute | solution.py:328
  123.0 11.2 %collective-permute-start.9 = (bf16[8,4,2,16,128]{4,3,2,1,0:T(8,128)(2,1)S(1)}, bf16[8,4,2,16,128]{4,3,2,1,0:T(8,128)(2,1)S(1)}, u32[]{:S(2)}, u32[]{:S(2)}) collective-permute-start(bf16[8,4,2,16,128]{4,3,2,1,0:T(8,128)(2,1)S(1)} %get-tuple-element.66), channel_id=1, source_target_pairs={{0,24},{8,0},{16,8},{24,16},{32,56},{40,32},{48,40},{56,48},{64,88... | collective-permute-start | bytes 786440 | tf_op jit(solution)/shard_map/ppermute | solution.py:328
  125.0 18.1 %collective-permute-start.17 = (bf16[8,4,2,16,128]{4,3,2,1,0:T(8,128)(2,1)S(1)}, bf16[8,4,2,16,128]{4,3,2,1,0:T(8,128)(2,1)S(1)}, u32[]{:S(2)}, u32[]{:S(2)}) collective-permute-start(bf16[8,4,2,16,128]{4,3,2,1,0:T(8,128)(2,1)S(1)} %get-tuple-element.78), channel_id=1, source_target_pairs={{0,8},{8,16},{16,24},{24,0},{32,40},{40,48},{48,56},{56,32},{64,72... | collective-permute-start | bytes 786440 | tf_op jit(solution)/shard_map/ppermute | solution.py:328
  127.7 22.5 %collective-permute-start.18 = (bf16[8,4,2,16,128]{4,3,2,1,0:T(8,128)(2,1)}, bf16[8,4,2,16,128]{4,3,2,1,0:T(8,128)(2,1)S(1)}, u32[]{:S(2)}, u32[]{:S(2)}) collective-permute-start(bf16[8,4,2,16,128]{4,3,2,1,0:T(8,128)(2,1)} %get-tuple-element.79), channel_id=1, source_target_pairs={{0,16},{8,24},{16,0},{24,8},{32,48},{40,56},{48,32},{56,40},{64,80... | collective-permute-start | bytes 786440 | tf_op jit(solution)/shard_map/ppermute | solution.py:328
  130.6 19.6 %collective-permute-start.19 = (bf16[8,4,2,16,128]{4,3,2,1,0:T(8,128)(2,1)}, bf16[8,4,2,16,128]{4,3,2,1,0:T(8,128)(2,1)S(1)}, u32[]{:S(2)}, u32[]{:S(2)}) collective-permute-start(bf16[8,4,2,16,128]{4,3,2,1,0:T(8,128)(2,1)} %get-tuple-element.80), channel_id=1, source_target_pairs={{0,24},{8,0},{16,8},{24,16},{32,56},{40,32},{48,40},{56,48},{64,88... | collective-permute-start | bytes 786440 | tf_op jit(solution)/shard_map/ppermute | solution.py:328
  134.2 19.8 %collective-permute-start.14 = (bf16[8,4,2,16,128]{4,3,2,1,0:T(8,128)(2,1)}, bf16[8,4,2,16,128]{4,3,2,1,0:T(8,128)(2,1)S(1)}, u32[]{:S(2)}, u32[]{:S(2)}) collective-permute-start(bf16[8,4,2,16,128]{4,3,2,1,0:T(8,128)(2,1)} %get-tuple-element.74), channel_id=1, source_target_pairs={{0,8},{8,16},{16,24},{24,0},{32,40},{40,48},{48,56},{56,32},{64,72... | collective-permute-start | bytes 786440 | tf_op jit(solution)/shard_map/ppermute | solution.py:328
  134.2 21.2 %collective-permute-start.15 = (bf16[8,4,2,16,128]{4,3,2,1,0:T(8,128)(2,1)}, bf16[8,4,2,16,128]{4,3,2,1,0:T(8,128)(2,1)S(1)}, u32[]{:S(2)}, u32[]{:S(2)}) collective-permute-start(bf16[8,4,2,16,128]{4,3,2,1,0:T(8,128)(2,1)} %get-tuple-element.75), channel_id=1, source_target_pairs={{0,16},{8,24},{16,0},{24,8},{32,48},{40,56},{48,32},{56,40},{64,80... | collective-permute-start | bytes 786440 | tf_op jit(solution)/shard_map/ppermute | solution.py:328
  143.1 0.7 copy-start.4
  143.8 11.6 %collective-permute-start.16 = (bf16[8,4,2,16,128]{4,3,2,1,0:T(8,128)(2,1)}, bf16[8,4,2,16,128]{4,3,2,1,0:T(8,128)(2,1)}, u32[]{:S(2)}, u32[]{:S(2)}) collective-permute-start(bf16[8,4,2,16,128]{4,3,2,1,0:T(8,128)(2,1)} %get-tuple-element.76), channel_id=1, source_target_pairs={{0,24},{8,0},{16,8},{24,16},{32,56},{40,32},{48,40},{56,48},{64,88... | collective-permute-start | bytes 786440 | tf_op jit(solution)/shard_map/ppermute | solution.py:328
  143.8 1.1 copy-start.3
  144.9 5.4 %copy-start.5 = (bf16[8,4,2,16,128]{4,3,2,1,0:T(8,128)(2,1)S(1)}, bf16[8,4,2,16,128]{4,3,2,1,0:T(8,128)(2,1)}, u32[]{:S(2)}) copy-start(bf16[8,4,2,16,128]{4,3,2,1,0:T(8,128)(2,1)} %copy-done.4) | copy-start | bytes 786436

commit v5 on v4

--- a/solution.py
+++ b/solution.py
@@ -207,12 +207,11 @@
 
 
 def last_kernel(f, relative, *refs):
-    near, last, out = refs[:NY], refs[NY : 2 * NY], refs[2 * NY + 1]
-    window, own, staged, sems = refs[2 * NY + 2 :]
+    own_t, last, out = refs[0], refs[1 : NY + 1], refs[NY + 2]
+    window, staged, sems = refs[NY + 3 :]
     for y in range(NY):
         for b in range(GROUP):
             for p in range(2):
-                fill(own, b, near[y][:, b, p], y, p)
                 fill(window, b, last[y][:, b, p], y, p)
 
     def each(step):
@@ -225,39 +224,37 @@
                     step(pltpu.make_async_copy(staged.at[a, far], out.at[a, k, f], sems.at[a, k]))
 
     for a in range(GROUP):
-        own_t = own[a].T
         for b in range(a + 1):
-            product = jnp.dot(own_t, window[b], preferred_element_type=jnp.float32)
+            product = jnp.dot(own_t[a], window[b], preferred_element_type=jnp.float32)
             staged[a, b, 0], staged[a, b, 1] = real_and_imag(product)
     each(lambda copy: copy.start())
     each(lambda copy: copy.wait())
 
 
-def last_stacks(relative, near, last, f, earlier):
+def last_stacks(relative, own_t, last, f, earlier):
     vmem = pl.BlockSpec(memory_space=pltpu.VMEM)
     blocks = pltpu.VMEM((GROUP, WINDOWS, 2 * BLOCK), jnp.bfloat16)
     return pl.pallas_call(
         functools.partial(last_kernel, f),
         in_specs=[pl.BlockSpec(memory_space=pltpu.SMEM)]
-        + [vmem] * (2 * NY)
+        + [vmem] * (NY + 1)
         + [pl.BlockSpec(memory_space=pl.ANY)],
         out_specs=pl.BlockSpec(memory_space=pl.ANY),
         out_shape=jax.ShapeDtypeStruct(earlier.shape, earlier.dtype),
-        input_output_aliases={1 + 2 * NY: 0},
+        input_output_aliases={2 + NY: 0},
         scratch_shapes=[
-            blocks,
             blocks,
             pltpu.VMEM((GROUP, GROUP, 2, BLOCK, BLOCK), jnp.bfloat16),
             pltpu.SemaphoreType.DMA((GROUP, PAIRS)),
         ],
         compiler_params=pltpu.CompilerParams(vmem_limit_bytes=20 << 20),
         name="last_stacks",
-    )(relative, *near, *last, earlier)
+    )(relative, own_t, *last, earlier)
 
 
 def pairs_kernel(f, low, high, relative, *refs):
-    sources, out = refs[:-5], refs[-5]
-    window, staged, own_t, sems = refs[-4:]
+    sources, out, own_t = refs[:-5], refs[-5], refs[-4]
+    window, staged, sems = refs[-3:]
     for y in range(NY):
         for b in range(high):
             for p in range(2):
@@ -276,9 +273,9 @@
                 step(pltpu.make_async_copy(staged.at[a, partner - low], out.at[a, k, f], sems.at[a, k]))
 
     for a in range(GROUP):
-        own_t[...] = window[a].T
+        own_t[a] = window[a].T
         for b in range(max(low, a), min(high, a + PAIRS)):
-            product = jnp.dot(own_t[...], window[b], preferred_element_type=jnp.float32)
+            product = jnp.dot(own_t[a], window[b], preferred_element_type=jnp.float32)
             staged[a, b - low, 0], staged[a, b - low, 1] = real_and_imag(product)
         each(a, lambda copy: copy.start())
     for a in range(GROUP):
@@ -301,13 +298,15 @@
     return pl.pallas_call(
         kernel,
         in_specs=[pl.BlockSpec(memory_space=pltpu.SMEM)] + specs,
-        out_specs=pl.BlockSpec(memory_space=pl.ANY),
-        out_shape=jax.ShapeDtypeStruct((GROUP, PAIRS, NF, 2, BLOCK, BLOCK), jnp.bfloat16),
+        out_specs=[pl.BlockSpec(memory_space=pl.ANY), vmem],
+        out_shape=[
+            jax.ShapeDtypeStruct((GROUP, PAIRS, NF, 2, BLOCK, BLOCK), jnp.bfloat16),
+            jax.ShapeDtypeStruct((GROUP, 2 * BLOCK, WINDOWS), jnp.bfloat16),
+        ],
         input_output_aliases=aliases,
         scratch_shapes=[
             pltpu.VMEM((high, WINDOWS, 2 * BLOCK), jnp.bfloat16),
             pltpu.VMEM((GROUP, high - low, 2, BLOCK, BLOCK), jnp.bfloat16),
-            pltpu.VMEM((2 * BLOCK, WINDOWS), jnp.bfloat16),
             pltpu.SemaphoreType.DMA((GROUP, PAIRS)),
         ],
         compiler_params=pltpu.CompilerParams(vmem_limit_bytes=20 << 20),
@@ -351,10 +350,10 @@
     near1 = along_y(pack_groups(place, 0, 1, planes1))
     halo1, found0 = barrier((halo1, found0))
     next1 = along_y(pack_groups(place, 1, 1, planes1, halo1))
-    result = pairs(relative, found0, 0, 0, REACH)
+    result, _ = pairs(relative, found0, 0, 0, REACH)
     last1 = along_y(pack_groups(place, 2, 1, planes1, halo1))
-    result = pairs(relative, near1 + next1, 1, 0, 2 * GROUP, result)
-    return last_stacks(relative, near1, last1, 1, result)
+    result, own_t = pairs(relative, near1 + next1, 1, 0, 2 * GROUP, result)
+    return last_stacks(relative, own_t, last1, 1, result)
 
 
 def solution(mesh):

time: 160 us -> 163 us (1.019)
  the two profiles are of different devices: /device:TPU:32 before, /device:TPU:72 now
where the time goes in v5:
time: 163 us
  starting transfers between devices  59.8 us (37%)
  waiting for transfers between devices  55.9 us (34%)
  Pallas kernels  33.7 us (21%)
  local copies, waits for them, and re-layouts  12.1 us (7%)
    all_to_all x2, waiting for transfers between devices, across_z(): lax.all_to_all(sent, 'tm', split_axis=0, concat_axis=0, tiled=True, axis_...  35.9 us
    ppermute x12, starting transfers between devices, along_y(): lax.ppermute(packed[k], 'tm', rounds[k])  30.1 us
    all_to_all x2, starting transfers between devices, across_z(): lax.all_to_all(sent, 'tm', split_axis=0, concat_axis=0, tiled=True, axis_...  14 us
    unnamed x50, local copies, waits for them, and re-layouts  12.1 us
    ppermute x7, waiting for transfers between devices, per_device(): lax.ppermute(own1[k], 'chan', [(c, c ^ k) for c in range(NC)])  12.1 us
    pallas_call x2, Pallas kernels, pairs(): pl.pallas_call(kernel, in_specs=[pl.BlockSpec(memory_space=pltpu.SMEM)] +...  9.79 us
    pallas_call x1, Pallas kernels, spectra_apart(): pl.pallas_call(spectra_apart_kernel, grid_spec=grid_spec, out_shape=[jax....  8.44 us
    ppermute x7, starting transfers between devices, per_device(): lax.ppermute(own1[k], 'chan', [(c, c ^ k) for c in range(NC)])  7.97 us
  transfers between devices with their start and end apart: 23, of which 11 were waited for; matrix products, arithmetic and copies ran while one was open for 0% of the time, Pallas kernels for 14%

profile of v5, /device:TPU:72, one launch (start us, length us, event | category | flops | bytes accessed | tf_op | source)
XLA Modules:
  0.0 162.5 jit_solution(4659488887167979276)
XLA Ops:
  0.0 7.9 %spectra.2 = bf16[8,16,2,16,128]{4,3,2,1,0:T(8,128)(2,1)} custom-call(bf16[100,16,2048]{2,1,0:T(8,128)(2,1)} %bitcast.10, s32[1,2048]{1,0:T(1,128)} %bitcast.12, bf16[2,8,64,1600]{3,2,1,0:T(8,128)(2,1)} %constant.24.clone.rows.refs_0_.refs_1_.refs_2_.refs_3_.refs_4_.refs_5_.refs_6_.refs_7_), custom_call_target="tpu_custom_call" | custom-call | tf_op jit(solution)/shard_map/spectra/pallas_call | solution.py:64
  7.9 4.3 %all-to-all-start = ((bf16[8,16,2,16,128]{4,3,2,1,0:T(8,128)(2,1)}), bf16[8,16,2,16,128]{4,3,2,1,0:T(8,128)(2,1)S(1)}, u32[]{:S(2)}, u32[]{:S(2)}) async-start(bf16[8,16,2,16,128]{4,3,2,1,0:T(8,128)(2,1)} %spectra.2), calls=%async_computation | async-start | bytes 2097152 | tf_op jit(solution)/shard_map/all_to_all | solution.py:339
  12.8 8.4 %spectra.3 = (bf16[16,2,16,128]{3,2,1,0:T(8,128)(2,1)}, bf16[16,2,16,128]{3,2,1,0:T(8,128)(2,1)}, bf16[16,2,16,128]{3,2,1,0:T(8,128)(2,1)}, bf16[16,2,16,128]{3,...) custom-call(s32[8]{0:T(128)} %iota_xor_fusion.order, ...), custom_call_target="tpu_custom_call" | custom-call | tf_op jit(solution)/shard_map/spectra/pallas_call | solution.py:101
  21.3 6.9 %all-to-all-done = bf16[8,16,2,16,128]{4,3,2,1,0:T(8,128)(2,1)S(1)} async-done(((bf16[8,16,2,16,128]{4,3,2,1,0:T(8,128)(2,1)}), bf16[8,16,2,16,128]{4,3,2,1,0:T(8,128)(2,1)S(1)}, u32[]{:S(2)}, u32[]{:S(2)}) %all-to-all-start) | async-done | bytes 1048608 | tf_op jit(solution)/shard_map/all_to_all | solution.py:339
  28.4 1.1 copy-done
  29.5 8.1 %all-to-all-start.1 = ((bf16[8,6,4,2,16,128]{5,4,3,2,1,0:T(8,128)(2,1)}), bf16[8,6,4,2,16,128]{5,4,3,2,1,0:T(8,128)(2,1)S(1)}, u32[]{:S(2)}, u32[]{:S(2)}) async-start(bf16[8,6,4,2,16,128]{5,4,3,2,1,0:T(8,128)(2,1)} %copy-done), calls=%async_computation.1 | async-start | bytes 3145728 | tf_op jit(solution)/shard_map/all_to_all | solution.py:330
  38.3 1.2 collective-permute-start.2
  39.5 1.0 collective-permute-start.3
  40.5 2.2 %collective-permute-start.4 = (bf16[16,2,16,128]{3,2,1,0:T(8,128)(2,1)S(1)}, bf16[16,2,16,128]{3,2,1,0:T(8,128)(2,1)S(1)}, u32[]{:S(2)}, u32[]{:S(2)}) collective-permute-start(bf16[16,2,16,128]{3,2,1,0:T(8,128)(2,1)S(1)} %copy-done.21), channel_id=1, source_target_pairs={{0,5},{1,4},{2,7},{3,6},{4,1},{5,0},{6,3},{7,2},{8,13},{9,12},{10,... | collective-permute-start | bytes 393224 | tf_op jit(solution)/shard_map/ppermute | solution.py:344
  42.7 1.2 collective-permute-start.5
  44.0 1.7 %collective-permute-start.6 = (bf16[16,2,16,128]{3,2,1,0:T(8,128)(2,1)S(1)}, bf16[16,2,16,128]{3,2,1,0:T(8,128)(2,1)S(1)}, u32[]{:S(2)}, u32[]{:S(2)}) collective-permute-start(bf16[16,2,16,128]{3,2,1,0:T(8,128)(2,1)S(1)} %copy-done.19), channel_id=1, source_target_pairs={{0,7},{1,6},{2,5},{3,4},{4,3},{5,2},{6,1},{7,0},{8,15},{9,14},{10,... | collective-permute-start | bytes 393224 | tf_op jit(solution)/shard_map/ppermute | solution.py:344
  45.9 4.5 %collective-permute-done.3.refs_4_ = bf16[16,2,16,128]{3,2,1,0:T(8,128)(2,1)S(1)} collective-permute-done((bf16[16,2,16,128]{3,2,1,0:T(8,128)(2,1)S(1)}, bf16[16,2,16,128]{3,2,1,0:T(8,128)(2,1)S(1)}, u32[]{:S(2)}, u32[]{:S(2)}) %collective-permute-start.3) | collective-permute-done | bytes 131104 | tf_op jit(solution)/shard_map/ppermute | solution.py:344
  50.3 1.9 %collective-permute-done.4.refs_5_ = bf16[16,2,16,128]{3,2,1,0:T(8,128)(2,1)S(1)} collective-permute-done((bf16[16,2,16,128]{3,2,1,0:T(8,128)(2,1)S(1)}, bf16[16,2,16,128]{3,2,1,0:T(8,128)(2,1)S(1)}, u32[]{:S(2)}, u32[]{:S(2)}) %collective-permute-start.4) | collective-permute-done | bytes 131104 | tf_op jit(solution)/shard_map/ppermute | solution.py:344
  52.2 3.2 %collective-permute-done.5.refs_6_ = bf16[16,2,16,128]{3,2,1,0:T(8,128)(2,1)S(1)} collective-permute-done((bf16[16,2,16,128]{3,2,1,0:T(8,128)(2,1)S(1)}, bf16[16,2,16,128]{3,2,1,0:T(8,128)(2,1)S(1)}, u32[]{:S(2)}, u32[]{:S(2)}) %collective-permute-start.5) | collective-permute-done | bytes 131104 | tf_op jit(solution)/shard_map/ppermute | solution.py:344
  55.4 2.2 %collective-permute-done.6.refs_7_ = bf16[16,2,16,128]{3,2,1,0:T(8,128)(2,1)S(1)} collective-permute-done((bf16[16,2,16,128]{3,2,1,0:T(8,128)(2,1)S(1)}, bf16[16,2,16,128]{3,2,1,0:T(8,128)(2,1)S(1)}, u32[]{:S(2)}, u32[]{:S(2)}) %collective-permute-start.6) | collective-permute-done | bytes 131104 | tf_op jit(solution)/shard_map/ppermute | solution.py:344
  58.3 1.0 copy-done.1
  59.3 15.7 %all-to-all-done.1.planes = bf16[8,6,4,2,16,128]{5,4,3,2,1,0:T(8,128)(2,1)S(1)} async-done(((bf16[8,6,4,2,16,128]{5,4,3,2,1,0:T(8,128)(2,1)}), bf16[8,6,4,2,16,128]{5,4,3,2,1,0:T(8,128)(2,1)S(1)}, u32[]{:S(2)}, u32[]{:S(2)}) %all-to-all-start.1) | async-done | bytes 1572896 | tf_op jit(solution)/shard_map/all_to_all | solution.py:330
  75.0 5.9 %all-to-all-start.2 = ((bf16[8,16,2,16,128]{4,3,2,1,0:T(8,128)(2,1)}), bf16[8,16,2,16,128]{4,3,2,1,0:T(8,128)(2,1)S(1)}, u32[]{:S(2)}, u32[]{:S(2)}) async-start(bf16[8,16,2,16,128]{4,3,2,1,0:T(8,128)(2,1)} %copy-done.1), calls=%async_computation.2 | async-start | bytes 2097152 | tf_op jit(solution)/shard_map/all_to_all | solution.py:330
  80.9 1.6 pack.5
  82.4 1.6 collective-permute-start.11
  84.0 0.9 collective-permute-start.12
  85.0 2.4 %collective-permute-start.13 = (bf16[8,3,4,2,16,128]{5,4,3,2,1,0:T(8,128)(2,1)}, bf16[8,3,4,2,16,128]{5,4,3,2,1,0:T(8,128)(2,1)}, u32[]{:S(2)}, u32[]{:S(2)}) collective-permute-start(bf16[8,3,4,2,16,128]{5,4,3,2,1,0:T(8,128)(2,1)} %get-tuple-element.74), channel_id=1, source_target_pairs={{0,24},{8,0},{16,8},{24,16},{32,56},{40,32},{48,40},{56,48},{64,88... | collective-permute-start | bytes 2359304 | tf_op jit(solution)/shard_map/ppermute | solution.py:327
  87.4 20.3 %all-to-all-done.2 = bf16[8,16,2,16,128]{4,3,2,1,0:T(8,128)(2,1)S(1)} async-done(((bf16[8,16,2,16,128]{4,3,2,1,0:T(8,128)(2,1)}), bf16[8,16,2,16,128]{4,3,2,1,0:T(8,128)(2,1)S(1)}, u32[]{:S(2)}, u32[]{:S(2)}) %all-to-all-start.2) | async-done | bytes 1048608 | tf_op jit(solution)/shard_map/all_to_all | solution.py:330
  107.7 3.4 %collective-permute-start.10 = (bf16[8,2,4,2,16,128]{5,4,3,2,1,0:T(8,128)(2,1)S(1)}, bf16[8,2,4,2,16,128]{5,4,3,2,1,0:T(8,128)(2,1)S(1)}, u32[]{:S(2)}, u32[]{:S(2)}) collective-permute-start(bf16[8,2,4,2,16,128]{5,4,3,2,1,0:T(8,128)(2,1)S(1)} %slice.4), channel_id=1, source_target_pairs={{32,0},{40,8},{48,16},{56,24},{64,32},{72,40},{80,48},{88,56},{96,... | collective-permute-start | bytes 1572872 | tf_op jit(solution)/shard_map/ppermute | solution.py:349
  111.3 1.7 %collective-permute-start.7 = (bf16[8,4,2,16,128]{4,3,2,1,0:T(8,128)(2,1)S(1)}, bf16[8,4,2,16,128]{4,3,2,1,0:T(8,128)(2,1)S(1)}, u32[]{:S(2)}, u32[]{:S(2)}) collective-permute-start(bf16[8,4,2,16,128]{4,3,2,1,0:T(8,128)(2,1)S(1)} %get-tuple-element.67), channel_id=1, source_target_pairs={{0,8},{8,16},{16,24},{24,0},{32,40},{40,48},{48,56},{56,32},{64,72... | collective-permute-start | bytes 786440 | tf_op jit(solution)/shard_map/ppermute | solution.py:327
  112.9 0.9 collective-permute-start.8
  113.9 9.0 %collective-permute-start.9 = (bf16[8,4,2,16,128]{4,3,2,1,0:T(8,128)(2,1)S(1)}, bf16[8,4,2,16,128]{4,3,2,1,0:T(8,128)(2,1)S(1)}, u32[]{:S(2)}, u32[]{:S(2)}) collective-permute-start(bf16[8,4,2,16,128]{4,3,2,1,0:T(8,128)(2,1)S(1)} %get-tuple-element.69), channel_id=1, source_target_pairs={{0,24},{8,0},{16,8},{24,16},{32,56},{40,32},{48,40},{56,48},{64,88... | collective-permute-start | bytes 786440 | tf_op jit(solution)/shard_map/ppermute | solution.py:327
  123.0 0.9 pack.6
  124.6 0.7 collective-permute-start.14
  125.4 1.2 pack.7
  127.3 1.2 collective-permute-start.15
  128.5 0.7 copy-done.4
  129.2 1.9 %collective-permute-start.16 = (bf16[8,4,2,16,128]{4,3,2,1,0:T(8,128)(2,1)}, bf16[8,4,2,16,128]{4,3,2,1,0:T(8,128)(2,1)S(1)}, u32[]{:S(2)}, u32[]{:S(2)}) collective-permute-start(bf16[8,4,2,16,128]{4,3,2,1,0:T(8,128)(2,1)} %get-tuple-element.79), channel_id=1, source_target_pairs={{0,24},{8,0},{16,8},{24,16},{32,56},{40,32},{48,40},{56,48},{64,88... | collective-permute-start | bytes 786440 | tf_op jit(solution)/shard_map/ppermute | solution.py:327
  131.1 0.7 copy-done.6
  131.8 1.7 %collective-permute-start.17 = (bf16[8,4,2,16,128]{4,3,2,1,0:T(8,128)(2,1)}, bf16[8,4,2,16,128]{4,3,2,1,0:T(8,128)(2,1)S(1)}, u32[]{:S(2)}, u32[]{:S(2)}) collective-permute-start(bf16[8,4,2,16,128]{4,3,2,1,0:T(8,128)(2,1)} %get-tuple-element.87), channel_id=1, source_target_pairs={{0,8},{8,16},{16,24},{24,0},{32,40},{40,48},{48,56},{56,32},{64,72... | collective-permute-start | bytes 786440 | tf_op jit(solution)/shard_map/ppermute | solution.py:327
  133.4 0.9 collective-permute-done.9.refs_3_
  134.3 0.7 copy-done.8
  135.0 3.8 %collective-permute-start.18 = (bf16[8,4,2,16,128]{4,3,2,1,0:T(8,128)(2,1)}, bf16[8,4,2,16,128]{4,3,2,1,0:T(8,128)(2,1)S(1)}, u32[]{:S(2)}, u32[]{:S(2)}) collective-permute-start(bf16[8,4,2,16,128]{4,3,2,1,0:T(8,128)(2,1)} %get-tuple-element.88), channel_id=1, source_target_pairs={{0,16},{8,24},{16,0},{24,8},{32,48},{40,56},{48,32},{56,40},{64,80... | collective-permute-start | bytes 786440 | tf_op jit(solution)/shard_map/ppermute | solution.py:327
  139.5 4.3 %collective-permute-start.19 = (bf16[8,4,2,16,128]{4,3,2,1,0:T(8,128)(2,1)}, bf16[8,4,2,16,128]{4,3,2,1,0:T(8,128)(2,1)}, u32[]{:S(2)}, u32[]{:S(2)}) collective-permute-start(bf16[8,4,2,16,128]{4,3,2,1,0:T(8,128)(2,1)} %get-tuple-element.89), channel_id=1, source_target_pairs={{0,24},{8,0},{16,8},{24,16},{32,56},{40,32},{48,40},{56,48},{64,88... | collective-permute-start | bytes 786440 | tf_op jit(solution)/shard_map/ppermute | solution.py:327
  143.8 6.1 %pairs.2 = (bf16[4,9,2,2,128,128]{5,4,3,2,1,0:T(8,128)(2,1)}, bf16[4,256,512]{2,1,0:T(8,128)(2,1)}) custom-call(s32[4,9]{1,0:T(4,128)S(1)} %broadcast_subtract_fusion.relative, bf16[8,3,4,2,16,128]{5,4,3,2,1,0:T(8,128)(2,1)S(1)} %get-tuple-element.80.refs_0_, bf16[8,3,4,2,16,128]{5,4,3,2,1,0:T(8,128)(2,1)S(1)} %collective-permute-done.11.refs_1_, ...), custom_call_target="tpu_custom_call" | custom-call | tf_op jit(solution)/shard_map/pairs/pallas_call | solution.py:298
  149.9 0.9 copy-done.3
  150.9 0.9 copy-done.5
  151.8 0.9 copy-done.7
  152.8 0.9 copy-done.9
  153.7 0.9 copy-done.13
  154.7 0.9 copy-done.15
  155.6 3.7 %pairs.3 = (bf16[4,9,2,2,128,128]{5,4,3,2,1,0:T(8,128)(2,1)}, bf16[4,256,512]{2,1,0:T(8,128)(2,1)S(1)}) custom-call(s32[4,9]{1,0:T(4,128)S(1)} %broadcast_subtract_fusion.relative, bf16[8,4,2,16,128]{4,3,2,1,0:T(8,128)(2,1)S(1)} %copy-done.3, bf16[8,4,2,16,128]{4,3,2,1,0:T(8,128)(2,1)S(1)} %copy-done.5, ...), custom_call_target="tpu_custom_call", output_to_operand_aliasing={{0}: (9, {})} | custom-call | tf_op jit(solution)/shard_map/pairs/pallas_call | solution.py:298
  159.3 3.0 %last_stacks.1 = bf16[4,9,2,2,128,128]{5,4,3,2,1,0:T(8,128)(2,1)} custom-call(s32[4,9]{1,0:T(4,128)S(1)} %broadcast_subtract_fusion.relative, bf16[4,256,512]{2,1,0:T(8,128)(2,1)S(1)} %get-tuple-element.85.refs_0_, bf16[8,4,2,16,128]{4,3,2,1,0:T(8,128)(2,1)S(1)} %copy-done.11, ...), custom_call_target="tpu_custom_call", output_to_operand_aliasing={{}: (6, {})} | custom-call | tf_op jit(solution)/shard_map/last_stacks/pallas_call | solution.py:237
  (62 shorter events, 4.6 us)
Async XLA Ops:
  7.9 20.3 %all-to-all-start = ((bf16[8,16,2,16,128]{4,3,2,1,0:T(8,128)(2,1)}), bf16[8,16,2,16,128]{4,3,2,1,0:T(8,128)(2,1)S(1)}, u32[]{:S(2)}, u32[]{:S(2)}) async-start(bf16[8,16,2,16,128]{4,3,2,1,0:T(8,128)(2,1)} %spectra.2), calls=%async_computation | async-start | bytes 2097152 | tf_op jit(solution)/shard_map/all_to_all | solution.py:339
  21.2 16.4 %copy-start.24 = (bf16[16,2,16,128]{3,2,1,0:T(8,128)(2,1)S(1)}, bf16[16,2,16,128]{3,2,1,0:T(8,128)(2,1)}, u32[]{:S(2)}) copy-start(bf16[16,2,16,128]{3,2,1,0:T(8,128)(2,1)} %get-tuple-element.59) | copy-start | bytes 393220
  21.2 17.1 %copy-start.23 = (bf16[16,2,16,128]{3,2,1,0:T(8,128)(2,1)S(1)}, bf16[16,2,16,128]{3,2,1,0:T(8,128)(2,1)}, u32[]{:S(2)}) copy-start(bf16[16,2,16,128]{3,2,1,0:T(8,128)(2,1)} %get-tuple-element.60) | copy-start | bytes 393220
  21.2 18.3 %copy-start.22 = (bf16[16,2,16,128]{3,2,1,0:T(8,128)(2,1)S(1)}, bf16[16,2,16,128]{3,2,1,0:T(8,128)(2,1)}, u32[]{:S(2)}) copy-start(bf16[16,2,16,128]{3,2,1,0:T(8,128)(2,1)} %get-tuple-element.61) | copy-start | bytes 393220
  21.2 19.2 %copy-start.21 = (bf16[16,2,16,128]{3,2,1,0:T(8,128)(2,1)S(1)}, bf16[16,2,16,128]{3,2,1,0:T(8,128)(2,1)}, u32[]{:S(2)}) copy-start(bf16[16,2,16,128]{3,2,1,0:T(8,128)(2,1)} %get-tuple-element.62) | copy-start | bytes 393220
  21.3 21.5 %copy-start.20 = (bf16[16,2,16,128]{3,2,1,0:T(8,128)(2,1)S(1)}, bf16[16,2,16,128]{3,2,1,0:T(8,128)(2,1)}, u32[]{:S(2)}) copy-start(bf16[16,2,16,128]{3,2,1,0:T(8,128)(2,1)} %get-tuple-element.63) | copy-start | bytes 393220
  21.3 22.8 %copy-start.19 = (bf16[16,2,16,128]{3,2,1,0:T(8,128)(2,1)S(1)}, bf16[16,2,16,128]{3,2,1,0:T(8,128)(2,1)}, u32[]{:S(2)}) copy-start(bf16[16,2,16,128]{3,2,1,0:T(8,128)(2,1)} %get-tuple-element.64) | copy-start | bytes 393220
  21.3 36.4 %copy-start.16 = (bf16[16,2,16,128]{3,2,1,0:T(8,128)(2,1)S(1)}, bf16[16,2,16,128]{3,2,1,0:T(8,128)(2,1)}, u32[]{:S(2)}) copy-start(bf16[16,2,16,128]{3,2,1,0:T(8,128)(2,1)} %get-tuple-element.57.refs_0_) | copy-start | bytes 393220
  21.3 36.4 %copy-start.17 = (s32[8]{0:T(128)S(1)}, s32[8]{0:T(128)}, u32[]{:S(2)}) copy-start(s32[8]{0:T(128)} %iota_xor_fusion.order) | copy-start | bytes 100
  28.4 1.1 copy-start
  29.5 45.5 %all-to-all-start.1 = ((bf16[8,6,4,2,16,128]{5,4,3,2,1,0:T(8,128)(2,1)}), bf16[8,6,4,2,16,128]{5,4,3,2,1,0:T(8,128)(2,1)S(1)}, u32[]{:S(2)}, u32[]{:S(2)}) async-start(bf16[8,6,4,2,16,128]{5,4,3,2,1,0:T(8,128)(2,1)} %copy-done), calls=%async_computation.1 | async-start | bytes 3145728 | tf_op jit(solution)/shard_map/all_to_all | solution.py:330
  37.6 5.1 %collective-permute-start = (bf16[16,2,16,128]{3,2,1,0:T(8,128)(2,1)}, bf16[16,2,16,128]{3,2,1,0:T(8,128)(2,1)S(1)}, u32[]{:S(2)}, u32[]{:S(2)}) collective-permute-start(bf16[16,2,16,128]{3,2,1,0:T(8,128)(2,1)} %get-tuple-element.58), channel_id=1, source_target_pairs={{0,1},{1,0},{2,3},{3,2},{4,5},{5,4},{6,7},{7,6},{8,9},{9,8},{10,11... | collective-permute-start | bytes 393224 | tf_op jit(solution)/shard_map/ppermute | solution.py:344
  37.6 6.4 %collective-permute-start.1 = (bf16[16,2,16,128]{3,2,1,0:T(8,128)(2,1)S(1)}, bf16[16,2,16,128]{3,2,1,0:T(8,128)(2,1)S(1)}, u32[]{:S(2)}, u32[]{:S(2)}) collective-permute-start(bf16[16,2,16,128]{3,2,1,0:T(8,128)(2,1)S(1)} %copy-done.24), channel_id=1, source_target_pairs={{0,2},{1,3},{2,0},{3,1},{4,6},{5,7},{6,4},{7,5},{8,10},{9,11},{10,... | collective-permute-start | bytes 393224 | tf_op jit(solution)/shard_map/ppermute | solution.py:344
  38.3 7.6 %collective-permute-start.2 = (bf16[16,2,16,128]{3,2,1,0:T(8,128)(2,1)S(1)}, bf16[16,2,16,128]{3,2,1,0:T(8,128)(2,1)S(1)}, u32[]{:S(2)}, u32[]{:S(2)}) collective-permute-start(bf16[16,2,16,128]{3,2,1,0:T(8,128)(2,1)S(1)} %copy-done.23), channel_id=1, source_target_pairs={{0,3},{1,2},{2,1},{3,0},{4,7},{5,6},{6,5},{7,4},{8,11},{9,10},{10,... | collective-permute-start | bytes 393224 | tf_op jit(solution)/shard_map/ppermute | solution.py:344
  39.5 10.8 %collective-permute-start.3 = (bf16[16,2,16,128]{3,2,1,0:T(8,128)(2,1)S(1)}, bf16[16,2,16,128]{3,2,1,0:T(8,128)(2,1)S(1)}, u32[]{:S(2)}, u32[]{:S(2)}) collective-permute-start(bf16[16,2,16,128]{3,2,1,0:T(8,128)(2,1)S(1)} %copy-done.22), channel_id=1, source_target_pairs={{0,4},{1,5},{2,6},{3,7},{4,0},{5,1},{6,2},{7,3},{8,12},{9,13},{10,... | collective-permute-start | bytes 393224 | tf_op jit(solution)/shard_map/ppermute | solution.py:344
  40.5 11.7 %collective-permute-start.4 = (bf16[16,2,16,128]{3,2,1,0:T(8,128)(2,1)S(1)}, bf16[16,2,16,128]{3,2,1,0:T(8,128)(2,1)S(1)}, u32[]{:S(2)}, u32[]{:S(2)}) collective-permute-start(bf16[16,2,16,128]{3,2,1,0:T(8,128)(2,1)S(1)} %copy-done.21), channel_id=1, source_target_pairs={{0,5},{1,4},{2,7},{3,6},{4,1},{5,0},{6,3},{7,2},{8,13},{9,12},{10,... | collective-permute-start | bytes 393224 | tf_op jit(solution)/shard_map/ppermute | solution.py:344
  42.7 12.7 %collective-permute-start.5 = (bf16[16,2,16,128]{3,2,1,0:T(8,128)(2,1)S(1)}, bf16[16,2,16,128]{3,2,1,0:T(8,128)(2,1)S(1)}, u32[]{:S(2)}, u32[]{:S(2)}) collective-permute-start(bf16[16,2,16,128]{3,2,1,0:T(8,128)(2,1)S(1)} %copy-done.20), channel_id=1, source_target_pairs={{0,6},{1,7},{2,4},{3,5},{4,2},{5,3},{6,0},{7,1},{8,14},{9,15},{10,... | collective-permute-start | bytes 393224 | tf_op jit(solution)/shard_map/ppermute | solution.py:344
  44.0 13.7 %collective-permute-start.6 = (bf16[16,2,16,128]{3,2,1,0:T(8,128)(2,1)S(1)}, bf16[16,2,16,128]{3,2,1,0:T(8,128)(2,1)S(1)}, u32[]{:S(2)}, u32[]{:S(2)}) collective-permute-start(bf16[16,2,16,128]{3,2,1,0:T(8,128)(2,1)S(1)} %copy-done.19), channel_id=1, source_target_pairs={{0,7},{1,6},{2,5},{3,4},{4,3},{5,2},{6,1},{7,0},{8,15},{9,14},{10,... | collective-permute-start | bytes 393224 | tf_op jit(solution)/shard_map/ppermute | solution.py:344
  58.3 1.0 copy-start.1
  59.3 84.4 %copy-start.18 = (s32[4,9]{1,0:T(4,128)S(1)}, s32[4,9]{1,0:T(4,128)}, u32[]{:S(2)}) copy-start(s32[4,9]{1,0:T(4,128)} %param.6) | copy-start | bytes 436
  75.0 32.7 %all-to-all-start.2 = ((bf16[8,16,2,16,128]{4,3,2,1,0:T(8,128)(2,1)}), bf16[8,16,2,16,128]{4,3,2,1,0:T(8,128)(2,1)S(1)}, u32[]{:S(2)}, u32[]{:S(2)}) async-start(bf16[8,16,2,16,128]{4,3,2,1,0:T(8,128)(2,1)} %copy-done.1), calls=%async_computation.2 | async-start | bytes 2097152 | tf_op jit(solution)/shard_map/all_to_all | solution.py:330
  82.4 30.5 %collective-permute-start.11 = (bf16[8,3,4,2,16,128]{5,4,3,2,1,0:T(8,128)(2,1)}, bf16[8,3,4,2,16,128]{5,4,3,2,1,0:T(8,128)(2,1)S(1)}, u32[]{:S(2)}, u32[]{:S(2)}) collective-permute-start(bf16[8,3,4,2,16,128]{5,4,3,2,1,0:T(8,128)(2,1)} %get-tuple-element.72), channel_id=1, source_target_pairs={{0,8},{8,16},{16,24},{24,0},{32,40},{40,48},{48,56},{56,32},{64,72... | collective-permute-start | bytes 2359304 | tf_op jit(solution)/shard_map/ppermute | solution.py:327
  84.0 29.8 %collective-permute-start.12 = (bf16[8,3,4,2,16,128]{5,4,3,2,1,0:T(8,128)(2,1)}, bf16[8,3,4,2,16,128]{5,4,3,2,1,0:T(8,128)(2,1)S(1)}, u32[]{:S(2)}, u32[]{:S(2)}) collective-permute-start(bf16[8,3,4,2,16,128]{5,4,3,2,1,0:T(8,128)(2,1)} %get-tuple-element.73), channel_id=1, source_target_pairs={{0,16},{8,24},{16,0},{24,8},{32,48},{40,56},{48,32},{56,40},{64,80... | collective-permute-start | bytes 2359304 | tf_op jit(solution)/shard_map/ppermute | solution.py:327
  85.0 38.0 %collective-permute-start.13 = (bf16[8,3,4,2,16,128]{5,4,3,2,1,0:T(8,128)(2,1)}, bf16[8,3,4,2,16,128]{5,4,3,2,1,0:T(8,128)(2,1)}, u32[]{:S(2)}, u32[]{:S(2)}) collective-permute-start(bf16[8,3,4,2,16,128]{5,4,3,2,1,0:T(8,128)(2,1)} %get-tuple-element.74), channel_id=1, source_target_pairs={{0,24},{8,0},{16,8},{24,16},{32,56},{40,32},{48,40},{56,48},{64,88... | collective-permute-start | bytes 2359304 | tf_op jit(solution)/shard_map/ppermute | solution.py:327
  107.7 15.3 %collective-permute-start.10 = (bf16[8,2,4,2,16,128]{5,4,3,2,1,0:T(8,128)(2,1)S(1)}, bf16[8,2,4,2,16,128]{5,4,3,2,1,0:T(8,128)(2,1)S(1)}, u32[]{:S(2)}, u32[]{:S(2)}) collective-permute-start(bf16[8,2,4,2,16,128]{5,4,3,2,1,0:T(8,128)(2,1)S(1)} %slice.4), channel_id=1, source_target_pairs={{32,0},{40,8},{48,16},{56,24},{64,32},{72,40},{80,48},{88,56},{96,... | collective-permute-start | bytes 1572872 | tf_op jit(solution)/shard_map/ppermute | solution.py:349
  111.2 15.3 %copy-start.2 = (bf16[8,4,2,16,128]{4,3,2,1,0:T(8,128)(2,1)}, bf16[8,4,2,16,128]{4,3,2,1,0:T(8,128)(2,1)S(1)}, u32[]{:S(2)}) copy-start(bf16[8,4,2,16,128]{4,3,2,1,0:T(8,128)(2,1)S(1)} %get-tuple-element.66.refs_0_) | copy-start | bytes 786436
  111.3 17.3 %collective-permute-start.7 = (bf16[8,4,2,16,128]{4,3,2,1,0:T(8,128)(2,1)S(1)}, bf16[8,4,2,16,128]{4,3,2,1,0:T(8,128)(2,1)S(1)}, u32[]{:S(2)}, u32[]{:S(2)}) collective-permute-start(bf16[8,4,2,16,128]{4,3,2,1,0:T(8,128)(2,1)S(1)} %get-tuple-element.67), channel_id=1, source_target_pairs={{0,8},{8,16},{16,24},{24,0},{32,40},{40,48},{48,56},{56,32},{64,72... | collective-permute-start | bytes 786440 | tf_op jit(solution)/shard_map/ppermute | solution.py:327
  112.9 18.2 %collective-permute-start.8 = (bf16[8,4,2,16,128]{4,3,2,1,0:T(8,128)(2,1)S(1)}, bf16[8,4,2,16,128]{4,3,2,1,0:T(8,128)(2,1)S(1)}, u32[]{:S(2)}, u32[]{:S(2)}) collective-permute-start(bf16[8,4,2,16,128]{4,3,2,1,0:T(8,128)(2,1)S(1)} %get-tuple-element.68), channel_id=1, source_target_pairs={{0,16},{8,24},{16,0},{24,8},{32,48},{40,56},{48,32},{56,40},{64,80... | collective-permute-start | bytes 786440 | tf_op jit(solution)/shard_map/ppermute | solution.py:327
  113.9 20.5 %collective-permute-start.9 = (bf16[8,4,2,16,128]{4,3,2,1,0:T(8,128)(2,1)S(1)}, bf16[8,4,2,16,128]{4,3,2,1,0:T(8,128)(2,1)S(1)}, u32[]{:S(2)}, u32[]{:S(2)}) collective-permute-start(bf16[8,4,2,16,128]{4,3,2,1,0:T(8,128)(2,1)S(1)} %get-tuple-element.69), channel_id=1, source_target_pairs={{0,24},{8,0},{16,8},{24,16},{32,56},{40,32},{48,40},{56,48},{64,88... | collective-permute-start | bytes 786440 | tf_op jit(solution)/shard_map/ppermute | solution.py:327
  123.9 0.7 copy-start.12
  124.6 14.2 %collective-permute-start.14 = (bf16[8,4,2,16,128]{4,3,2,1,0:T(8,128)(2,1)S(1)}, bf16[8,4,2,16,128]{4,3,2,1,0:T(8,128)(2,1)S(1)}, u32[]{:S(2)}, u32[]{:S(2)}) collective-permute-start(bf16[8,4,2,16,128]{4,3,2,1,0:T(8,128)(2,1)S(1)} %get-tuple-element.77), channel_id=1, source_target_pairs={{0,8},{8,16},{16,24},{24,0},{32,40},{40,48},{48,56},{56,32},{64,72... | collective-permute-start | bytes 786440 | tf_op jit(solution)/shard_map/ppermute | solution.py:327
  126.6 0.7 copy-start.10
  127.3 22.6 %collective-permute-start.15 = (bf16[8,4,2,16,128]{4,3,2,1,0:T(8,128)(2,1)}, bf16[8,4,2,16,128]{4,3,2,1,0:T(8,128)(2,1)S(1)}, u32[]{:S(2)}, u32[]{:S(2)}) collective-permute-start(bf16[8,4,2,16,128]{4,3,2,1,0:T(8,128)(2,1)} %get-tuple-element.78), channel_id=1, source_target_pairs={{0,16},{8,24},{16,0},{24,8},{32,48},{40,56},{48,32},{56,40},{64,80... | collective-permute-start | bytes 786440 | tf_op jit(solution)/shard_map/ppermute | solution.py:327
  128.5 0.7 copy-start.4
  129.2 20.7 %collective-permute-start.16 = (bf16[8,4,2,16,128]{4,3,2,1,0:T(8,128)(2,1)}, bf16[8,4,2,16,128]{4,3,2,1,0:T(8,128)(2,1)S(1)}, u32[]{:S(2)}, u32[]{:S(2)}) collective-permute-start(bf16[8,4,2,16,128]{4,3,2,1,0:T(8,128)(2,1)} %get-tuple-element.79), channel_id=1, source_target_pairs={{0,24},{8,0},{16,8},{24,16},{32,56},{40,32},{48,40},{56,48},{64,88... | collective-permute-start | bytes 786440 | tf_op jit(solution)/shard_map/ppermute | solution.py:327
  131.1 0.7 copy-start.6
  131.8 27.5 %collective-permute-start.17 = (bf16[8,4,2,16,128]{4,3,2,1,0:T(8,128)(2,1)}, bf16[8,4,2,16,128]{4,3,2,1,0:T(8,128)(2,1)S(1)}, u32[]{:S(2)}, u32[]{:S(2)}) collective-permute-start(bf16[8,4,2,16,128]{4,3,2,1,0:T(8,128)(2,1)} %get-tuple-element.87), channel_id=1, source_target_pairs={{0,8},{8,16},{16,24},{24,0},{32,40},{40,48},{48,56},{56,32},{64,72... | collective-permute-start | bytes 786440 | tf_op jit(solution)/shard_map/ppermute | solution.py:327
  134.3 0.7 copy-start.8
  135.0 24.3 %collective-permute-start.18 = (bf16[8,4,2,16,128]{4,3,2,1,0:T(8,128)(2,1)}, bf16[8,4,2,16,128]{4,3,2,1,0:T(8,128)(2,1)S(1)}, u32[]{:S(2)}, u32[]{:S(2)}) collective-permute-start(bf16[8,4,2,16,128]{4,3,2,1,0:T(8,128)(2,1)} %get-tuple-element.88), channel_id=1, source_target_pairs={{0,16},{8,24},{16,0},{24,8},{32,48},{40,56},{48,32},{56,40},{64,80... | collective-permute-start | bytes 786440 | tf_op jit(solution)/shard_map/ppermute | solution.py:327
  138.8 0.7 copy-start.14
  139.5 19.8 %collective-permute-start.19 = (bf16[8,4,2,16,128]{4,3,2,1,0:T(8,128)(2,1)}, bf16[8,4,2,16,128]{4,3,2,1,0:T(8,128)(2,1)}, u32[]{:S(2)}, u32[]{:S(2)}) collective-permute-start(bf16[8,4,2,16,128]{4,3,2,1,0:T(8,128)(2,1)} %get-tuple-element.89), channel_id=1, source_target_pairs={{0,24},{8,0},{16,8},{24,16},{32,56},{40,32},{48,40},{56,48},{64,88... | collective-permute-start | bytes 786440 | tf_op jit(solution)/shard_map/ppermute | solution.py:327
  143.8 15.6 %copy-start.11 = (bf16[8,4,2,16,128]{4,3,2,1,0:T(8,128)(2,1)S(1)}, bf16[8,4,2,16,128]{4,3,2,1,0:T(8,128)(2,1)}, u32[]{:S(2)}) copy-start(bf16[8,4,2,16,128]{4,3,2,1,0:T(8,128)(2,1)} %copy-done.10) | copy-start | bytes 786436
  149.9 1.0 copy-start.3
  150.9 0.9 copy-start.5
  151.8 0.9 copy-start.7
  152.8 0.9 copy-start.9
  153.7 0.9 copy-start.13
  154.7 0.9 copy-start.15
